TPU v7x, 256 devices: a whole 4x4x8 slice. The times are simulated.
256 devices in a mesh: mass: 64 (over z, y, core), spec: 4 (over x).
Axes of the slice: x: 4, y: 4, z: 8, core: 2. Of those that a mesh axis runs over, the one named last changes fastest.
Arguments:
- spectra: bfloat16 [8192, 16, 2048], P(('mass', 'spec')), may hold values from -64 to 64
- block_start: int32 [8192], P(('mass', 'spec')), may hold values from 0 to 62, as said below
- block_range: int32 [8192, 2], P(('mass', 'spec')), may hold values from 0 to 4095, as said below
- block_count: int32 [8192], P(('mass', 'spec')), may hold values from 1 to 16
- peptide_table: bfloat16 [65536, 2048], P('mass'), may hold values from -1 to 1
- peptide_bin: int32 [65536], P('mass'), may hold values from 0 to 4095, as said below
- peptide_shift: float32 [65536], P('mass'), may hold values from -4 to 4
Outputs:
- spectrum_lse: float32 [8192, 16], P(('mass', 'spec'))
- spectrum_shift: float32 [8192, 16], P(('mass', 'spec'))
- peptide_support: float32 [65536], P(('mass', 'spec'))
Inputs may be any that keep to these rules, and one draw needn't show every extreme that they name: Block b is routed to mass ranges block_start[b] to block_start[b] + 1. No two blocks of one device have the same start, so at most 2 blocks of one device cover one mass range. block_start[b] * 64 <= block_range[b, 0] < block_start[b] * 64 + 64 // 2, block_range[b, 0] + 32 <= block_range[b, 1] < (block_start[b] + 2) * 64. `peptide_bin`: peptides of mass range o have bins from o * 64 to (o + 1) * 64 - 1, and every one of these 64 bins holds at least one peptide.
All inputs are finite; a program needn't handle non-finite values.
Results may differ from a plain program's by a relative error of at most 0.0021.
Values may be sent and summed in bfloat16 or wider, within the bound.
No kernel may reach another device: no remote copies, remote signals or barrier semaphores. Data moves between devices by JAX's collectives and lax.ppermute only.
A program may use at most 64 MiB of HBM per device.

v0:
```python
import jax
import jax.numpy as jnp
from jax import lax
from jax.sharding import PartitionSpec as P

WIN = 2
SCAP = 1


very_low = -1e30


def slot_table(member, capacity):
    ranks = jnp.cumsum(member.astype(jnp.int32), axis=0) - 1
    slot_ids = jnp.arange(capacity, dtype=jnp.int32)
    return member[:, :, None] & (ranks[:, :, None] == slot_ids[None, None, :])


def pack_blocks(chosen, spectra, block_meta):
    blocks, rows, width = spectra.shape
    weights = chosen.astype(jnp.bfloat16)
    flat = spectra.reshape(blocks, rows * width)
    packed = jnp.einsum("boc,bx->ocx", weights, flat, preferred_element_type=jnp.float32).astype(
        jnp.bfloat16
    )
    packed = packed.reshape(chosen.shape[1], chosen.shape[2], rows, width)
    meta_out = jnp.sum(
        chosen.astype(jnp.int32)[:, :, :, None] * block_meta[:, None, None, :], axis=0
    )
    return (packed, meta_out)


def partial_scores(received, meta_in, peptide_table, peptide_bin, peptide_shift):
    lead = received.shape[:3]
    flat = received.reshape(-1, received.shape[3])
    scores = lax.dot_general(
        flat, peptide_table, (((1,), (1,)), ((), ())), preferred_element_type=jnp.float32
    )
    scores = scores.reshape(lead + (peptide_table.shape[0],))
    lower = meta_in[:, :, 0][:, :, None, None]
    upper = meta_in[:, :, 1][:, :, None, None]
    filled = meta_in[:, :, 2][:, :, None, None]
    row_pos = lax.broadcasted_iota(jnp.int32, lead + (1,), 2)
    inside = (peptide_bin >= lower) & (peptide_bin <= upper) & (row_pos < filled)
    masked = jnp.where(inside, scores, very_low)
    peak_score = jnp.max(masked, axis=3)
    weights = jnp.where(inside, jnp.exp(masked - peak_score[..., None]), 0.0)
    total = jnp.sum(weights, axis=3)
    shifted = jnp.dot(weights, peptide_shift, precision=lax.Precision.HIGHEST)
    return ((peak_score, total, shifted), masked)


def finish_blocks(chosen, partials, block_count):
    picked = chosen[:, :, :, None]
    peak = jnp.max(jnp.where(picked, partials[0][None], very_low), axis=(1, 2))
    scale = jnp.where(picked, jnp.exp(partials[0][None] - peak[:, None, None, :]), 0.0)
    denom = jnp.sum(scale * partials[1][None], axis=(1, 2))
    numer = jnp.sum(scale * partials[2][None], axis=(1, 2))
    row_ids = jnp.arange(partials[0].shape[2], dtype=jnp.int32)
    valid = row_ids[None, :] < block_count[:, None]
    safe = jnp.where(valid, denom, 1.0)
    lse = jnp.where(valid, peak + jnp.log(safe), 0.0)
    mean_shift = jnp.where(valid, numer / safe, 0.0)
    return (lse, mean_shift)


def spread_normalizers(chosen, lse):
    return jnp.sum(jnp.where(chosen[:, :, :, None], lse[:, None, None, :], 0.0), axis=0)


def posterior_mass(masked, normalizers):
    return jnp.sum(jnp.exp(masked - normalizers[..., None]), axis=(0, 1, 2))


def body(spectra, block_start, block_range, block_count, peptide_table, peptide_bin, peptide_shift):
    owners = lax.axis_size("mass")
    range_ids = jnp.arange(owners, dtype=jnp.int32)
    offset = range_ids[None, :] - block_start[:, None]
    block_meta = jnp.concatenate([block_range, block_count[:, None]], axis=1)
    chosen = slot_table((offset >= 0) & (offset < WIN), WIN * SCAP)
    packed, meta_out = pack_blocks(chosen, spectra, block_meta)
    partial_value, masked = partial_scores(
        lax.all_to_all(packed, "mass", split_axis=0, concat_axis=0, tiled=True),
        lax.all_to_all(meta_out, "mass", split_axis=0, concat_axis=0, tiled=True),
        peptide_table,
        peptide_bin,
        peptide_shift,
    )
    peak_score, total, shifted, masked = (
        lax.all_to_all(partial_value[0], "mass", split_axis=0, concat_axis=0, tiled=True),
        lax.all_to_all(partial_value[1], "mass", split_axis=0, concat_axis=0, tiled=True),
        lax.all_to_all(partial_value[2], "mass", split_axis=0, concat_axis=0, tiled=True),
        masked,
    )
    lse, mean_shift = finish_blocks(chosen, (peak_score, total, shifted), block_count)
    normalizers = lax.all_to_all(
        spread_normalizers(chosen, lse), "mass", split_axis=0, concat_axis=0, tiled=True
    )
    support_part = posterior_mass(masked, normalizers)
    support = lax.psum_scatter(support_part, "spec", scatter_dimension=0, tiled=True)
    return (lse, mean_shift, support)


def solution(mesh):
    in_specs = (
        P(("mass", "spec"), None, None),
        P(("mass", "spec")),
        P(("mass", "spec"), None),
        P(("mass", "spec")),
        P("mass", None),
        P("mass"),
        P("mass"),
    )
    out_specs = (P(("mass", "spec"), None), P(("mass", "spec"), None), P(("mass", "spec")))
    return jax.shard_map(body, mesh=mesh, in_specs=in_specs, out_specs=out_specs, check_vma=False)
```

profile of v0, /device:TPU:1, one launch (start us, length us, event | category | flops | bytes accessed | tf_op | source)
XLA Modules:
  0.0 363.1 jit_solution(17921016678999898715)
XLA Ops:
  0.6 0.0 copy-start
  0.6 0.7 fusion.14
  1.4 0.1 reduce_window_sum.11
  1.5 0.7 pad_add_fusion
  2.2 0.1 multiply_reduce_fusion.2
  2.3 0.7 copy.57
  3.0 13.2 %all-to-all-start = ((s32[64,2,3]{2,1,0:T(2,128)}), s32[64,2,3]{2,1,0:T(2,128)S(1)}, u32[]{:S(2)}, u32[]{:S(2)}) async-start(s32[64,2,3]{2,1,0:T(2,128)} %copy.57), calls=%async_computation | async-start | bytes 131072 | tf_op jit(solution)/shard_map/all_to_all | solution.py:84
  16.2 2.9 reshape.129
  19.0 5.6 %convolution_convert_fusion = bf16[64,2,32768]{2,0,1:T(8,128)(2,1)} fusion(pred[32,64,2]{1,0,2:T(32,128)(4,1)S(1)} %get-tuple-element.12, bf16[32,32768,1]{1,0,2:T(8,128)(2,1)S(1)} %reshape.129), kind=kOutput, calls=%fused_computation | convolution fusion | flops 272629760 | bytes 10489856 | tf_op jit(solution)/shard_map/boc,bx->ocx/dot_general | solution.py:23
  24.6 12.9 %copy.74 = bf16[16,8,16,2048]{3,2,1,0:T(8,128)(2,1)} copy(bf16[16,8,16,2048]{3,1,2,0:T(8,128)(2,1)} %bitcast.28) | data formatting | bytes 16777216
  37.5 8.3 %copy.64 = bf16[64,2,16,2048]{3,2,1,0:T(8,128)(2,1)} copy(bf16[64,2,16,2048]{3,2,0,1:T(8,128)(2,1)} %bitcast.29) | data formatting | bytes 16777216 | tf_op jit(solution)/shard_map/reshape | solution.py:26
  45.8 0.0 copy-start.1
  45.8 0.0 all-to-all-done
  45.8 10.6 %all-to-all-start.1 = ((bf16[64,2,16,2048]{3,2,1,0:T(8,128)(2,1)}), bf16[64,2,16,2048]{3,2,1,0:T(8,128)(2,1)}, u32[]{:S(2)}, u32[]{:S(2)}) async-start(bf16[64,2,16,2048]{3,2,1,0:T(8,128)(2,1)} %copy.64), calls=%async_computation.1 | async-start | bytes 16777216 | tf_op jit(solution)/shard_map/all_to_all | solution.py:83
  56.5 0.2 fusion.20
  56.7 0.1 copy.58
  56.7 0.1 copy.59
  56.8 0.1 copy.60
  56.9 0.1 copy.61
  57.0 0.1 copy.62
  57.1 0.1 copy.63
  57.2 0.1 iota_compare_fusion
  57.4 0.0 copy-done.1
  57.4 0.5 compare_and_fusion
  57.9 181.0 %all-to-all-done.1 = bf16[64,2,16,2048]{3,2,1,0:T(8,128)(2,1)} async-done(((bf16[64,2,16,2048]{3,2,1,0:T(8,128)(2,1)}), bf16[64,2,16,2048]{3,2,1,0:T(8,128)(2,1)}, u32[]{:S(2)}, u32[]{:S(2)}) %all-to-all-start.1) | async-done | bytes 8388640 | tf_op jit(solution)/shard_map/all_to_all | solution.py:83
  238.9 15.6 %fusion = (f32[64,2,16]{2,1,0:T(2,128)}, f32[64,2,16,1024]{3,2,1,0:T(8,128)}) fusion(pred[64,2,16]{2,1,0:T(4,128)(4,1)S(1)} %iota_compare_fusion, pred[64,2,1024]{2,1,0:T(4,128)(4,1)S(1)} %compare_and_fusion, bf16[64,2,16,2048]{3,2,1,0:T(8,128)(2,1)} %all-to-all-done.1, bf16[1024,2048]{1,0:T(8,128)(2,1)} %param.11), kind=kOutput, calls=%fused_computation.4 | convolution fusion | flops 8596224000 | bytes 21112832 | tf_op jit(solution)/shard_map/dot_general | solution.py:36
  254.5 10.0 %all-to-all-start.2 = ((f32[64,2,16]{2,1,0:T(2,128)}), f32[64,2,16]{2,1,0:T(2,128)S(1)}, u32[]{:S(2)}, u32[]{:S(2)}) async-start(f32[64,2,16]{2,1,0:T(2,128)} %get-tuple-element.20), calls=%async_computation.2 | async-start | bytes 131072 | tf_op jit(solution)/shard_map/all_to_all | solution.py:90
  264.4 5.7 %fusion.2 = f32[64,2,16]{2,1,0:T(2,128)} fusion(f32[64,2,16,1024]{3,2,1,0:T(8,128)} %get-tuple-element.21, f32[64,2,16]{2,1,0:T(2,128)} %get-tuple-element.20, pred[64,2,16]{2,1,0:T(4,128)(4,1)S(1)} %iota_compare_fusion, pred[64,2,1024]{2,1,0:T(4,128)(4,1)S(1)} %compare_and_fusion), kind=kLoop, calls=%fused_computation.6 | loop fusion | flops 10483712 | bytes 8538112 | tf_op jit(solution)/shard_map/reduce_sum | solution.py:48
  270.1 4.4 %all-to-all-done.2 = f32[64,2,16]{2,1,0:T(2,128)S(1)} async-done(((f32[64,2,16]{2,1,0:T(2,128)}), f32[64,2,16]{2,1,0:T(2,128)S(1)}, u32[]{:S(2)}, u32[]{:S(2)}) %all-to-all-start.2) | async-done | bytes 8224 | tf_op jit(solution)/shard_map/all_to_all | solution.py:90
  274.5 5.9 %all-to-all-start.3 = ((f32[64,2,16]{2,1,0:T(2,128)}), f32[64,2,16]{2,1,0:T(2,128)S(1)}, u32[]{:S(2)}, u32[]{:S(2)}) async-start(f32[64,2,16]{2,1,0:T(2,128)} %fusion.2), calls=%async_computation.3 | async-start | bytes 131072 | tf_op jit(solution)/shard_map/all_to_all | solution.py:91
  280.4 0.0 copy-done
  280.4 0.0 copy-start.2
  280.5 0.0 copy-start.3
  280.5 32.4 %fusion.1 = f32[1,64,2,16]{3,0,2,1:T(1,128)} fusion(f32[1024,1,1,1]{0,1,3,2:T(1,128)S(1)} %bitcast.27, f32[64,2,16,1024]{3,2,1,0:T(8,128)} %get-tuple-element.21, f32[64,2,16]{2,1,0:T(2,128)} %get-tuple-element.20, pred[64,2,16]{2,1,0:T(4,128)(4,1)S(1)} %iota_compare_fusion, pred[64,2,1024]{2,1,0:T(4,128)(4,1)S(1)} %compare_and_fusion), kind=kOutput, calls=%fused_computation.5 | convolution fusion | flops 33554432 | bytes 8542208 | tf_op jit(solution)/shard_map/dot_general | solution.py:49
  312.9 0.1 copy.65
  312.9 0.0 all-to-all-done.3
  312.9 10.3 %all-to-all-start.4 = ((f32[64,2,16]{2,1,0:T(2,128)}), f32[64,2,16]{2,1,0:T(2,128)S(1)}, u32[]{:S(2)}, u32[]{:S(2)}) async-start(f32[64,2,16]{2,1,0:T(2,128)} %bitcast.9), calls=%async_computation.4 | async-start | bytes 131072 | tf_op jit(solution)/shard_map/all_to_all | solution.py:92
  323.2 0.1 select_reduce_fusion.1
  323.4 0.1 copy.66
  323.5 9.9 %all-to-all-done.4 = f32[64,2,16]{2,1,0:T(2,128)S(1)} async-done(((f32[64,2,16]{2,1,0:T(2,128)}), f32[64,2,16]{2,1,0:T(2,128)S(1)}, u32[]{:S(2)}, u32[]{:S(2)}) %all-to-all-start.4) | async-done | bytes 8224 | tf_op jit(solution)/shard_map/all_to_all | solution.py:92
  333.3 0.1 copy.67
  333.4 0.4 multiply_reduce_fusion
  333.8 0.0 copy-done.2
  333.8 0.1 divide_select_fusion
  333.9 0.1 select_reduce_fusion
  334.0 0.7 copy.68
  334.7 4.4 %all-to-all-start.5 = ((f32[64,2,16]{2,1,0:T(2,128)}), f32[64,2,16]{2,1,0:T(2,128)S(1)}, u32[]{:S(2)}, u32[]{:S(2)}) async-start(f32[64,2,16]{2,1,0:T(2,128)} %copy.68), calls=%async_computation.5 | async-start | bytes 131072 | tf_op jit(solution)/shard_map/all_to_all | solution.py:96
  339.1 0.0 copy-done.3
  339.1 0.6 dynamic-slice
  340.3 0.7 copy.69
  341.0 0.7 copy.70
  341.7 7.5 %all-to-all-done.5 = f32[64,2,16]{2,1,0:T(2,128)S(1)} async-done(((f32[64,2,16]{2,1,0:T(2,128)}), f32[64,2,16]{2,1,0:T(2,128)S(1)}, u32[]{:S(2)}, u32[]{:S(2)}) %all-to-all-start.5) | async-done | bytes 8224 | tf_op jit(solution)/shard_map/all_to_all | solution.py:96
  349.2 4.7 %exponential_reduce_fusion = f32[1024]{0:T(1024)S(1)} fusion(f32[64,2,16,1024]{3,2,1,0:T(8,128)} %get-tuple-element.21, f32[64,2,16]{2,1,0:T(2,128)S(1)} %all-to-all-done.5, pred[64,2,16]{2,1,0:T(4,128)(4,1)S(1)} %iota_compare_fusion, pred[64,2,1024]{2,1,0:T(4,128)(4,1)S(1)} %compare_and_fusion), kind=kLoop, calls=%fused_computation.3 | loop fusion | flops 8387584 | bytes 8534016 | tf_op jit(solution)/shard_map/reduce_sum | solution.py:72
  353.9 8.5 %all-reduce = f32[1024]{0:T(1024)S(1)} all-reduce(f32[1024]{0:T(1024)S(1)} %exponential_reduce_fusion), channel_id=2, replica_groups=mesh['mass'=64,'spec'=4] {'spec'}, use_global_device_ids=true, to_apply=%region_9.10.clone | all-reduce | flops 1024 | bytes 8192
  362.4 0.6 dynamic-slice.1
  (3 shorter events, 0.0 us)
Async XLA Ops:
  0.6 279.8 %copy-start = (f32[1024]{0:T(1024)S(1)}, f32[1024]{0:T(1024)}, u32[]{:S(2)}) copy-start(f32[1024]{0:T(1024)} %param.13) | copy-start | bytes 12292
  3.0 42.8 %all-to-all-start = ((s32[64,2,3]{2,1,0:T(2,128)}), s32[64,2,3]{2,1,0:T(2,128)S(1)}, u32[]{:S(2)}, u32[]{:S(2)}) async-start(s32[64,2,3]{2,1,0:T(2,128)} %copy.57), calls=%async_computation | async-start | bytes 131072 | tf_op jit(solution)/shard_map/all_to_all | solution.py:84
  45.8 11.6 %copy-start.1 = (s32[1024]{0:T(1024)S(1)}, s32[1024]{0:T(1024)}, u32[]{:S(2)}) copy-start(s32[1024]{0:T(1024)} %param.12) | copy-start | bytes 12292
  45.8 193.1 %all-to-all-start.1 = ((bf16[64,2,16,2048]{3,2,1,0:T(8,128)(2,1)}), bf16[64,2,16,2048]{3,2,1,0:T(8,128)(2,1)}, u32[]{:S(2)}, u32[]{:S(2)}) async-start(bf16[64,2,16,2048]{3,2,1,0:T(8,128)(2,1)} %copy.64), calls=%async_computation.1 | async-start | bytes 16777216 | tf_op jit(solution)/shard_map/all_to_all | solution.py:83
  254.5 20.1 %all-to-all-start.2 = ((f32[64,2,16]{2,1,0:T(2,128)}), f32[64,2,16]{2,1,0:T(2,128)S(1)}, u32[]{:S(2)}, u32[]{:S(2)}) async-start(f32[64,2,16]{2,1,0:T(2,128)} %get-tuple-element.20), calls=%async_computation.2 | async-start | bytes 131072 | tf_op jit(solution)/shard_map/all_to_all | solution.py:90
  274.5 38.4 %all-to-all-start.3 = ((f32[64,2,16]{2,1,0:T(2,128)}), f32[64,2,16]{2,1,0:T(2,128)S(1)}, u32[]{:S(2)}, u32[]{:S(2)}) async-start(f32[64,2,16]{2,1,0:T(2,128)} %fusion.2), calls=%async_computation.3 | async-start | bytes 131072 | tf_op jit(solution)/shard_map/all_to_all | solution.py:91
  280.4 53.3 %copy-start.2 = (s32[32]{0:T(128)S(1)}, s32[32]{0:T(128)}, u32[]{:S(2)}) copy-start(s32[32]{0:T(128)} %param.10) | copy-start | bytes 388
  280.5 58.6 %copy-start.3 = (u32[256]{0:T(256)S(1)}, u32[256]{0:T(256)}, u32[]{:S(2)}) copy-start(u32[256]{0:T(256)} %constant.25) | copy-start | bytes 3076
  312.9 20.4 %all-to-all-start.4 = ((f32[64,2,16]{2,1,0:T(2,128)}), f32[64,2,16]{2,1,0:T(2,128)S(1)}, u32[]{:S(2)}, u32[]{:S(2)}) async-start(f32[64,2,16]{2,1,0:T(2,128)} %bitcast.9), calls=%async_computation.4 | async-start | bytes 131072 | tf_op jit(solution)/shard_map/all_to_all | solution.py:92
  334.7 14.5 %all-to-all-start.5 = ((f32[64,2,16]{2,1,0:T(2,128)}), f32[64,2,16]{2,1,0:T(2,128)S(1)}, u32[]{:S(2)}, u32[]{:S(2)}) async-start(f32[64,2,16]{2,1,0:T(2,128)} %copy.68), calls=%async_computation.5 | async-start | bytes 131072 | tf_op jit(solution)/shard_map/all_to_all | solution.py:96
where the time goes:
time: 364 us; the launch traced here: 363 us
  waiting for transfers between devices  203 us (56%)
  starting transfers between devices  54.3 us (15%)
  matrix products  53.5 us (15%)
  local copies, waits for them, and re-layouts  29.1 us (8%)
  other arithmetic  13.3 us (4%)
  blocking collectives  8.49 us (2%)
    all_to_all x1, waiting for transfers between devices, body(): lax.all_to_all(packed, 'mass', split_axis=0, concat_axis=0, tiled=True)  181 us
    dot_general x1, matrix products, partial_scores(): shifted = jnp.dot(weights, peptide_shift, precision=lax.Precision.HIGHEST)  32.4 us
    dot_general x1, matrix products, partial_scores(): lax.dot_general(flat, peptide_table, (((1,), (1,)), ((), ())), preferred_...  15.6 us
    unnamed x13, local copies, waits for them, and re-layouts  15.5 us
    all_to_all x1, starting transfers between devices, body(): lax.all_to_all(meta_out, 'mass', split_axis=0, concat_axis=0, tiled=True)  13.2 us
    all_to_all x1, starting transfers between devices, body(): lax.all_to_all(packed, 'mass', split_axis=0, concat_axis=0, tiled=True)  10.6 us
    all_to_all x1, starting transfers between devices, body(): lax.all_to_all(partial_value[2], 'mass', split_axis=0, concat_axis=0, til...  10.3 us
    all_to_all x1, starting transfers between devices, body(): lax.all_to_all(partial_value[0], 'mass', split_axis=0, concat_axis=0, til...  9.98 us
  transfers between devices with their start and end apart: 6, of which 4 were waited for; matrix products, arithmetic and copies ran while one was open for 20% of the time, Pallas kernels for 0%

commit v1 on v0

v1 whole, which is shorter than its diff:
```python
import jax
import jax.numpy as jnp
from jax import lax
from jax.experimental import pallas as pl
from jax.experimental.pallas import tpu as pltpu
from jax.sharding import PartitionSpec as P

SB = 16
LANES = 128
VERY_LOW = -1e30
FLOOR = -1e29
TILE = 256
CHUNK = 512
SUB = 8


def pack_kernel(start_ref, spectra_ref, out_ref, sem):
    blocks = spectra_ref.shape[0]

    def copy(i):
        return pltpu.make_async_copy(spectra_ref.at[i], out_ref.at[start_ref[i]], sem.at[i])

    for i in range(blocks):
        copy(i).start()
    for i in range(blocks):
        copy(i).wait()


def pack_blocks(block_start, spectra, owners):
    blocks, rows, width = spectra.shape
    return pl.pallas_call(
        pack_kernel,
        out_shape=jax.ShapeDtypeStruct((owners, rows, width), spectra.dtype),
        in_specs=[pl.BlockSpec(memory_space=pltpu.SMEM), pl.BlockSpec(memory_space=pltpu.VMEM)],
        out_specs=pl.BlockSpec(memory_space=pl.ANY),
        scratch_shapes=[pltpu.SemaphoreType.DMA((blocks,))],
        compiler_params=pltpu.CompilerParams(vmem_limit_bytes=8 * 1024 * 1024),
        name="pack_blocks",
    )(block_start, spectra)


def after_kernel(*refs):
    pass


def after(value, *tokens):
    return pl.pallas_call(
        after_kernel,
        out_shape=jax.ShapeDtypeStruct(value.shape, value.dtype),
        in_specs=[pl.BlockSpec(memory_space=pl.ANY)] * (1 + len(tokens)),
        out_specs=pl.BlockSpec(memory_space=pl.ANY),
        input_output_aliases={0: 0},
        name="after",
    )(value, *tokens)


def score_kernel(x_hbm, meta_ref, table_ref, bins_ref, shift_ref, ret_ref, sup_ref, x_ref, even_ref, odd_ref, sem):
    tiles = x_ref.shape[0]
    slots = TILE // SB
    chunks = table_ref.shape[0] // CHUNK
    per_chunk = slots // chunks

    def fetch(t):
        return pltpu.make_async_copy(x_hbm.at[pl.ds(t * TILE, TILE)], x_ref.at[t], sem.at[t])

    for t in range(tiles):
        fetch(t).start()
    sup_ref[...] = jnp.zeros_like(sup_ref)
    lane = lax.broadcasted_iota(jnp.int32, (SB, LANES), 1)
    spot = lax.broadcasted_iota(jnp.int32, (SB, LANES), 0)

    def multiply(t, j, into):
        at = pl.ds(pl.multiple_of(j * CHUNK, CHUNK), CHUNK)
        into[:, at] = lax.dot_general(
            x_ref[t], table_ref[at, :], (((1,), (1,)), ((), ())), preferred_element_type=jnp.float32
        )

    def reduce(t, j, source):
        total = None
        for k in range(per_chunk):
            slot = j * per_chunk + k
            parts = []
            for h in range(SB // SUB):
                row = pl.multiple_of(slot * SB + h * SUB, SUB)
                meta_at = pl.ds(pl.multiple_of(t * TILE + row, SUB), SUB)
                lower = meta_ref[meta_at, 0:1]
                upper = meta_ref[meta_at, 1:2]
                bins = bins_ref[...]
                inside = (bins >= lower) & (bins <= upper)
                masked = jnp.where(inside, source[pl.ds(row, SUB), :], VERY_LOW)
                peak = jnp.maximum(jnp.max(masked, axis=1, keepdims=True), FLOOR)
                weights = jnp.exp(masked - peak)
                denom = jnp.sum(weights, axis=1, keepdims=True)
                numer = jnp.sum(weights * shift_ref[...], axis=1, keepdims=True)
                live = denom > 0.0
                safe = jnp.where(live, denom, 1.0)
                inv = jnp.where(live, 1.0 / safe, 0.0)
                mass = weights * inv
                total = mass if total is None else total + mass
                lse = jnp.where(live, peak + jnp.log(safe), 0.0)
                parts.append((lse, numer * inv))
            lse = jnp.concatenate([p[0] for p in parts], axis=0)
            mean = jnp.concatenate([p[1] for p in parts], axis=0)
            flat = jnp.where(lane == spot, lse, jnp.where(lane == spot + SB, mean, 0.0))
            ret_ref[pl.ds(t * slots + slot, 1), :] = jnp.sum(flat, axis=0, keepdims=True)
        sup_ref[...] += total

    for t in range(tiles + 1):
        if t < tiles:
            fetch(t).wait()
        into, source = (even_ref, odd_ref) if t % 2 == 0 else (odd_ref, even_ref)

        def one_chunk(j, carry, t=t, into=into, source=source):
            if t < tiles:
                multiply(t, j, into)
            if t > 0:
                reduce(t - 1, j, source)
            return carry

        lax.fori_loop(0, chunks, one_chunk, 0)


def score_blocks(rows, meta, table, bins, shifts):
    total, width = rows.shape
    wide = table.shape[0]
    vmem = pl.BlockSpec(memory_space=pltpu.VMEM)
    return pl.pallas_call(
        score_kernel,
        out_shape=(
            jax.ShapeDtypeStruct((total // SB, LANES), jnp.float32),
            jax.ShapeDtypeStruct((SUB, wide), jnp.float32),
        ),
        in_specs=[pl.BlockSpec(memory_space=pl.ANY), vmem, vmem, vmem, vmem],
        out_specs=(vmem, vmem),
        scratch_shapes=[
            pltpu.VMEM((total // TILE, TILE, width), rows.dtype),
            pltpu.VMEM((TILE, wide), jnp.float32),
            pltpu.VMEM((TILE, wide), jnp.float32),
            pltpu.SemaphoreType.DMA((total // TILE,)),
        ],
        compiler_params=pltpu.CompilerParams(vmem_limit_bytes=32 * 1024 * 1024),
        cost_estimate=pl.CostEstimate(
            flops=2 * total * width * wide, bytes_accessed=2 * (total + wide) * width, transcendentals=total * wide
        ),
        name="score_blocks",
    )(rows, meta, table, bins, shifts)


def body(spectra, block_start, block_range, block_count, peptide_table, peptide_bin, peptide_shift):
    owners, specs = lax.axis_size("mass"), lax.axis_size("spec")
    spec = lax.axis_index("spec")
    own = peptide_table.shape[0]
    part = own // specs
    back = [((i + 1) % owners, i) for i in range(owners)]
    forth = [(i, (i + 1) % owners) for i in range(owners)]

    quarter = lax.dynamic_slice_in_dim(peptide_table, spec * part, part, 0)
    quarters = [lax.ppermute(quarter, "mass", back)]
    small = jnp.stack([peptide_bin.astype(jnp.float32), peptide_shift])
    next_small = lax.ppermute(small, "mass", back)

    range_ids = jnp.arange(owners, dtype=jnp.int32)
    chosen = block_start[:, None] == range_ids[None, :]
    block_meta = jnp.concatenate([block_range, block_count[:, None]], axis=1)
    meta_out = jnp.sum(jnp.where(chosen[:, :, None], block_meta[:, None, :], 0), axis=0)
    meta_in = lax.all_to_all(meta_out, "mass", split_axis=0, concat_axis=0, tiled=True)

    packed = after(pack_blocks(block_start, spectra, owners), quarters[0], next_small, meta_in)
    received = lax.all_to_all(packed, "mass", split_axis=0, concat_axis=0, tiled=True)

    for k in range(1, specs):
        quarters.append(lax.ppermute(quarters[0], "spec", [(i, (i + k) % specs) for i in range(specs)]))
    pieces = [small] + [
        lax.dynamic_slice_in_dim(next_small, lax.rem(spec + specs - k, specs) * part, part, 1) for k in range(specs)
    ]
    wide_small = jnp.concatenate(pieces, axis=1)
    bins = jnp.broadcast_to(wide_small[0:1], (SUB, 2 * own))
    shifts = jnp.broadcast_to(wide_small[1:2], (SUB, 2 * own))
    table = jnp.concatenate([peptide_table] + quarters, axis=0)

    row_ids = jnp.arange(SB, dtype=jnp.int32)
    valid = row_ids[None, :] < meta_in[:, 2:3]
    lower = jnp.broadcast_to(meta_in[:, 0:1], valid.shape)
    upper = jnp.where(valid, meta_in[:, 1:2], -1)
    row_meta = jnp.stack([lower, upper], axis=2).reshape(owners * SB, 2).astype(jnp.float32)
    row_meta = jnp.pad(row_meta, ((0, 0), (0, LANES - 2)))

    ret, sup = score_blocks(received.reshape(owners * SB, -1), row_meta, table, bins, shifts)

    home = lax.all_to_all(ret, "mass", split_axis=0, concat_axis=0, tiled=True)
    picked = jnp.sum(jnp.where(chosen[:, :, None], home[None, :, : 2 * SB], 0.0), axis=1)
    lse, mean_shift = picked[:, :SB], picked[:, SB:]

    sup = jnp.sum(sup, axis=0).reshape(2, specs, part)
    falling = sup[0, ::-1]
    mine = lax.dynamic_slice_in_dim(jnp.concatenate([falling, falling]), specs - 1 - spec, specs, 0)
    total = jnp.stack([mine[0], sup[1, 0]])
    for k in range(1, specs):
        piece = jnp.stack([mine[k], sup[1, k]])
        total = total + lax.ppermute(piece, "spec", [(i, (i + specs - k) % specs) for i in range(specs)])
    support = total[0] + lax.ppermute(total[1], "mass", forth)
    return (lse, mean_shift, support)


def solution(mesh):
    in_specs = (
        P(("mass", "spec"), None, None),
        P(("mass", "spec")),
        P(("mass", "spec"), None),
        P(("mass", "spec")),
        P("mass", None),
        P("mass"),
        P("mass"),
    )
    out_specs = (P(("mass", "spec"), None), P(("mass", "spec"), None), P(("mass", "spec")))
    return jax.shard_map(body, mesh=mesh, in_specs=in_specs, out_specs=out_specs, check_vma=False)
```

time: 364 us -> 177 us (0.49)
  waiting for transfers between devices: 203 us -> 87.9 us
  matrix products: 53.5 us -> 0 us
  Pallas kernels: 0 us -> 20 us
  starting transfers between devices: 54.3 us -> 41.6 us
  other arithmetic: 13.3 us -> 3.81 us
  blocking collectives: 8.49 us -> 0 us
  local copies, waits for them, and re-layouts: 29.1 us -> 22.2 us
    all_to_all x1, waiting for transfers between devices: 181 us -> 37.3 us  [body(): lax.all_to_all(packed, 'mass', split_axis=0, concat_axis=0, tiled=True)]
    dot_general x3 -> x0, matrix products: 53.5 us -> none  [the longest x1 32.4 us: partial_scores(): shifted = jnp.dot(weights, peptide_shift, precision=lax.Precision.HIGHEST)]
    ppermute x0 -> x9, waiting for transfers between devices: none -> 42.6 us  [the longest x3 41.9 us: body(): lax.ppermute(quarters[0], 'spec', [(i, (i + k) % specs) for i in range(sp...]
    all_to_all x4 -> x1, starting transfers between devices: 30.5 us -> 7.98 us  [body(): home = lax.all_to_all(ret, 'mass', split_axis=0, concat_axis=0, tiled=True)]
    pallas_call x0 -> x3, Pallas kernels: none -> 20 us  [the longest x1 16.3 us: score_blocks(): pl.pallas_call(score_kernel, out_shape=(jax.ShapeDtypeStruct((total // SB...]
    ppermute x0 -> x9, starting transfers between devices: none -> 19.8 us  [the longest x1 6.09 us: body(): next_small = lax.ppermute(small, 'mass', back)]
    all_to_all x4 -> x1, waiting for transfers between devices: 21.8 us -> 6.31 us  [body(): home = lax.all_to_all(ret, 'mass', split_axis=0, concat_axis=0, tiled=True)]
    reshape x2 -> x1, local copies, waits for them, and re-layouts: 11.1 us -> 0.01 us  [body(): sup = jnp.sum(sup, axis=0).reshape(2, specs, part)]
  transfers between devices with their start and end apart: 6 -> 12, of which waited for: 4 -> 6; matrix products, arithmetic and copies ran while one was open for 20% -> 8% of each run, Pallas kernels for 0% -> 2%
where the time goes in v1:
time: 177 us; the launch traced here: 176 us
  waiting for transfers between devices  87.9 us (50%)
  starting transfers between devices  41.6 us (24%)
  local copies, waits for them, and re-layouts  22.2 us (13%)
  Pallas kernels  20 us (11%)
  other arithmetic  3.81 us (2%)
    ppermute x3, waiting for transfers between devices, body(): lax.ppermute(quarters[0], 'spec', [(i, (i + k) % specs) for i in range(sp...  41.9 us
    all_to_all x1, waiting for transfers between devices, body(): lax.all_to_all(packed, 'mass', split_axis=0, concat_axis=0, tiled=True)  37.3 us
    unnamed x29, local copies, waits for them, and re-layouts  17.8 us
    pallas_call x1, Pallas kernels, score_blocks(): pl.pallas_call(score_kernel, out_shape=(jax.ShapeDtypeStruct((total // SB...  16.3 us
    all_to_all x1, starting transfers between devices, body(): lax.all_to_all(packed, 'mass', split_axis=0, concat_axis=0, tiled=True)  9.13 us
    all_to_all x1, starting transfers between devices, body(): home = lax.all_to_all(ret, 'mass', split_axis=0, concat_axis=0, tiled=True)  7.98 us
    all_to_all x1, waiting for transfers between devices, body(): home = lax.all_to_all(ret, 'mass', split_axis=0, concat_axis=0, tiled=True)  6.31 us
    ppermute x1, starting transfers between devices, body(): next_small = lax.ppermute(small, 'mass', back)  6.09 us
  transfers between devices with their start and end apart: 12, of which 6 were waited for; matrix products, arithmetic and copies ran while one was open for 8% of the time, Pallas kernels for 2%

profile of v1, /device:TPU:1, one launch (start us, length us, event | category | flops | bytes accessed | tf_op | source)
XLA Modules:
  0.0 176.5 jit_solution(3327174911254156327)
XLA Ops:
  0.6 1.3 constant_dynamic-slice_fusion
  1.9 3.3 %collective-permute-start = (bf16[256,2048]{1,0:T(8,128)(2,1)S(1)}, bf16[256,2048]{1,0:T(8,128)(2,1)S(1)}, u32[]{:S(2)}, u32[]{:S(2)}) collective-permute-start(bf16[256,2048]{1,0:T(8,128)(2,1)S(1)} %constant_dynamic-slice_fusion), channel_id=1, source_target_pairs={{4,0},{8,4},{12,8},{16,12},{20,16},{24,20},{28,24},{32,28},{36,32}... | collective-permute-start | bytes 3145736 | tf_op jit(solution)/shard_map/ppermute | solution.py:158
  5.3 0.7 convert_element_type.8
  5.9 0.7 constant_dynamic-update-slice_fusion.9
  6.6 6.1 %collective-permute-start.1 = (f32[2,1024]{1,0:T(2,128)S(1)}, f32[2,1024]{1,0:T(2,128)S(1)}, u32[]{:S(2)}, u32[]{:S(2)}) collective-permute-start(f32[2,1024]{1,0:T(2,128)S(1)} %get-tuple-element.25), channel_id=1, source_target_pairs={{4,0},{8,4},{12,8},{16,12},{20,16},{24,20},{28,24},{32,28},{36,32}... | collective-permute-start | bytes 24584 | tf_op jit(solution)/shard_map/ppermute | solution.py:160
  12.7 0.7 pad_add_fusion
  13.4 0.7 iota_compare_fusion
  14.2 0.1 select_reduce_fusion.1
  14.3 0.7 copy.26
  15.0 4.7 %all-to-all-start = ((s32[64,1,3]{2,1,0:T(1,128)}), s32[64,1,3]{2,1,0:T(1,128)S(1)}, u32[]{:S(2)}, u32[]{:S(2)}) async-start(s32[64,1,3]{2,1,0:T(1,128)} %copy.26), calls=%async_computation | async-start | bytes 65536 | tf_op jit(solution)/shard_map/all_to_all | solution.py:166
  19.7 0.0 copy-start.1
  19.7 1.6 copy-done.1
  21.3 0.7 copy-done.3
  21.9 3.7 %pack_blocks.1.refs_0_ = bf16[64,16,2048]{2,1,0:T(8,128)(2,1)S(1)} custom-call(s32[32]{0:T(128)S(1)} %copy-done.3, bf16[32,16,2048]{2,1,0:T(8,128)(2,1)S(1)} %copy-done.1), custom_call_target="tpu_custom_call" | custom-call | tf_op jit(solution)/shard_map/pack_blocks/pallas_call | solution.py:31
  25.6 1.9 %copy-done = bf16[64,16,2048]{2,1,0:T(8,128)(2,1)} copy-done((bf16[64,16,2048]{2,1,0:T(8,128)(2,1)}, bf16[64,16,2048]{2,1,0:T(8,128)(2,1)S(1)}, u32[]{:S(2)}) %copy-start) | copy-done | bytes 4194328
  27.5 1.6 all-to-all-done
  29.2 0.0 collective-permute-done.1.refs_2_
  29.2 0.0 collective-permute-done.refs_1_
  29.2 0.0 copy-start.4
  29.2 0.6 copy-done.6
  29.8 0.0 copy-done.8
  29.8 0.4 copy-done.4
  30.2 9.1 %all-to-all-start.1 = ((bf16[64,16,2048]{2,1,0:T(8,128)(2,1)}), bf16[64,16,2048]{2,1,0:T(8,128)(2,1)}, u32[]{:S(2)}, u32[]{:S(2)}) async-start(bf16[64,16,2048]{2,1,0:T(8,128)(2,1)} %after.1), calls=%async_computation.1 | async-start | bytes 8388608 | tf_op jit(solution)/shard_map/all_to_all | solution.py:169
  39.3 0.1 lt.47
  39.4 4.7 %constant_dynamic-update-slice_fusion.4 = bf16[2048,2048]{1,0:T(8,128)(2,1)} fusion(bf16[1024,2048]{1,0:T(8,128)(2,1)} %param.11), kind=kLoop, calls=%fused_computation.9 | loop fusion | bytes 8388608
  44.2 0.2 slice_reduce_fusion.2
  44.3 0.1 broadcast_in_dim.86
  44.4 0.1 broadcast_in_dim.87
  44.5 0.1 lt.49
  44.6 0.1 lt.50
  44.7 0.1 stack_broadcast_in_dim.7
  44.7 0.1 stack_broadcast_in_dim.8
  44.9 0.2 copy.27
  45.2 1.3 collective-permute-start.2
  46.4 0.0 copy-done.9
  46.5 2.5 %collective-permute-start.3 = (bf16[256,2048]{1,0:T(8,128)(2,1)S(1)}, bf16[256,2048]{1,0:T(8,128)(2,1)S(1)}, u32[]{:S(2)}, u32[]{:S(2)}) collective-permute-start(bf16[256,2048]{1,0:T(8,128)(2,1)S(1)} %copy-done.5), channel_id=1, source_target_pairs={{0,2},{1,3},{2,0},{3,1},{4,6},{5,7},{6,4},{7,5},{8,10},{9,11},{10,... | collective-permute-start | bytes 3145736 | tf_op jit(solution)/shard_map/ppermute | solution.py:172
  49.0 1.2 collective-permute-start.4
  50.2 1.0 constant_dynamic-update-slice_fusion.3
  51.2 19.5 %collective-permute-done.2 = bf16[256,2048]{1,0:T(8,128)(2,1)S(1)} collective-permute-done((bf16[256,2048]{1,0:T(8,128)(2,1)S(1)}, bf16[256,2048]{1,0:T(8,128)(2,1)S(1)}, u32[]{:S(2)}, u32[]{:S(2)}) %collective-permute-start.2) | collective-permute-done | bytes 1048608 | tf_op jit(solution)/shard_map/ppermute | solution.py:172
  70.7 1.1 constant_dynamic-update-slice_fusion.2
  71.8 22.4 %collective-permute-done.3 = bf16[256,2048]{1,0:T(8,128)(2,1)S(1)} collective-permute-done((bf16[256,2048]{1,0:T(8,128)(2,1)S(1)}, bf16[256,2048]{1,0:T(8,128)(2,1)S(1)}, u32[]{:S(2)}, u32[]{:S(2)}) %collective-permute-start.3) | collective-permute-done | bytes 1048608 | tf_op jit(solution)/shard_map/ppermute | solution.py:172
  94.2 1.1 constant_dynamic-update-slice_fusion.1
  95.3 0.0 collective-permute-done.4
  95.3 1.1 constant_dynamic-update-slice_fusion.table_ref
  96.4 37.3 %all-to-all-done.1 = bf16[64,16,2048]{2,1,0:T(8,128)(2,1)} async-done(((bf16[64,16,2048]{2,1,0:T(8,128)(2,1)}), bf16[64,16,2048]{2,1,0:T(8,128)(2,1)}, u32[]{:S(2)}, u32[]{:S(2)}) %all-to-all-start.1) | async-done | bytes 4194336 | tf_op jit(solution)/shard_map/all_to_all | solution.py:169
  133.7 3.4 %copy-done.2 = bf16[2048,2048]{1,0:T(8,128)(2,1)S(1)} copy-done((bf16[2048,2048]{1,0:T(8,128)(2,1)S(1)}, bf16[2048,2048]{1,0:T(8,128)(2,1)}, u32[]{:S(2)}) %copy-start.2) | copy-done | bytes 8388632
  137.1 16.3 %score_blocks.1 = (f32[64,128]{1,0:T(8,128)}, f32[8,2048]{1,0:T(8,128)S(1)}) custom-call(bf16[1024,2048]{1,0:T(8,128)(2,1)} %bitcast.5.x_hbm, f32[1024,128]{1,0:T(8,128)S(1)} %pad.4.meta_ref, bf16[2048,2048]{1,0:T(8,128)(2,1)S(1)} %copy-done.2, f32[8,2048]{1,0:T(8,128)S(1)} %broadcast_in_dim.90.bins_ref, f32[8,2048]{1,0:T(8,128)S(1)} %broadcast_in_dim.92.shift_ref), custom_call_target="tpu_custom_call" | custom-call | flops 8589934592 | bytes 12582912 | tf_op jit(solution)/shard_map/score_blocks/pallas_call | solution.py:127
  153.5 0.1 rev.3
  153.7 2.6 %collective-permute-start.5 = (f32[2,256]{1,0:T(2,128)S(1)}, f32[2,256]{1,0:T(2,128)S(1)}, u32[]{:S(2)}, u32[]{:S(2)}) collective-permute-start(f32[2,256]{1,0:T(2,128)S(1)} %pad_maximum_fusion.1), channel_id=1, source_target_pairs={{0,3},{1,0},{2,1},{3,2},{4,7},{5,4},{6,5},{7,6},{8,11},{9,8},{10,9... | collective-permute-start | bytes 6152 | tf_op jit(solution)/shard_map/ppermute | solution.py:200
  156.3 0.5 collective-permute-start.6
  156.8 0.6 collective-permute-start.7
  157.4 8.0 %all-to-all-start.2 = ((f32[64,1,128]{2,1,0:T(1,128)}), f32[64,1,128]{2,1,0:T(1,128)S(1)}, u32[]{:S(2)}, u32[]{:S(2)}) async-start(f32[64,1,128]{2,1,0:T(1,128)} %bitcast.9), calls=%async_computation.2 | async-start | bytes 65536 | tf_op jit(solution)/shard_map/all_to_all | solution.py:190
  165.4 0.0 collective-permute-done.5
  165.4 0.0 collective-permute-done.6
  165.4 0.0 collective-permute-done.7
  165.4 1.7 collective-permute-start.8
  167.2 0.7 collective-permute-done.8
  167.9 0.6 add.58
  168.4 6.3 %all-to-all-done.2 = f32[64,1,128]{2,1,0:T(1,128)S(1)} async-done(((f32[64,1,128]{2,1,0:T(1,128)}), f32[64,1,128]{2,1,0:T(1,128)S(1)}, u32[]{:S(2)}, u32[]{:S(2)}) %all-to-all-start.2) | async-done | bytes 32800 | tf_op jit(solution)/shard_map/all_to_all | solution.py:190
  174.8 0.1 copy.29
  174.8 0.2 select_reduce_fusion
  175.0 0.1 fusion.3
  175.1 0.7 copy.30
  175.8 0.7 copy.31
  (34 shorter events, 0.3 us)
Async XLA Ops:
  1.9 27.2 %collective-permute-start = (bf16[256,2048]{1,0:T(8,128)(2,1)S(1)}, bf16[256,2048]{1,0:T(8,128)(2,1)S(1)}, u32[]{:S(2)}, u32[]{:S(2)}) collective-permute-start(bf16[256,2048]{1,0:T(8,128)(2,1)S(1)} %constant_dynamic-slice_fusion), channel_id=1, source_target_pairs={{4,0},{8,4},{12,8},{16,12},{20,16},{24,20},{28,24},{32,28},{36,32}... | collective-permute-start | bytes 3145736 | tf_op jit(solution)/shard_map/ppermute | solution.py:158
  6.6 22.5 %collective-permute-start.1 = (f32[2,1024]{1,0:T(2,128)S(1)}, f32[2,1024]{1,0:T(2,128)S(1)}, u32[]{:S(2)}, u32[]{:S(2)}) collective-permute-start(f32[2,1024]{1,0:T(2,128)S(1)} %get-tuple-element.25), channel_id=1, source_target_pairs={{4,0},{8,4},{12,8},{16,12},{20,16},{24,20},{28,24},{32,28},{36,32}... | collective-permute-start | bytes 24584 | tf_op jit(solution)/shard_map/ppermute | solution.py:160
  15.0 14.2 %all-to-all-start = ((s32[64,1,3]{2,1,0:T(1,128)}), s32[64,1,3]{2,1,0:T(1,128)S(1)}, u32[]{:S(2)}, u32[]{:S(2)}) async-start(s32[64,1,3]{2,1,0:T(1,128)} %copy.26), calls=%async_computation | async-start | bytes 65536 | tf_op jit(solution)/shard_map/all_to_all | solution.py:166
  19.7 1.6 copy-start.1
  21.3 0.7 copy-start.3
  25.6 1.9 %copy-start = (bf16[64,16,2048]{2,1,0:T(8,128)(2,1)}, bf16[64,16,2048]{2,1,0:T(8,128)(2,1)S(1)}, u32[]{:S(2)}) copy-start(bf16[64,16,2048]{2,1,0:T(8,128)(2,1)S(1)} %pack_blocks.1.refs_0_) | copy-start | bytes 12582916
  29.2 0.6 copy-start.6
  29.2 0.6 copy-start.8
  29.2 1.0 copy-start.4
  30.2 14.0 %copy-start.7 = (s32[64,1,3]{2,1,0:T(1,128)S(1)}, s32[64,1,3]{2,1,0:T(1,128)}, u32[]{:S(2)}) copy-start(s32[64,1,3]{2,1,0:T(1,128)} %copy-done.6) | copy-start | bytes 2308
  30.2 15.0 %copy-start.5 = (bf16[256,2048]{1,0:T(8,128)(2,1)S(1)}, bf16[256,2048]{1,0:T(8,128)(2,1)}, u32[]{:S(2)}) copy-start(bf16[256,2048]{1,0:T(8,128)(2,1)} %copy-done.4) | copy-start | bytes 3145732
  30.2 16.3 %copy-start.9 = (f32[2,1024]{1,0:T(2,128)S(1)}, f32[2,1024]{1,0:T(2,128)}, u32[]{:S(2)}) copy-start(f32[2,1024]{1,0:T(2,128)} %copy-done.8) | copy-start | bytes 24580
  30.2 103.5 %all-to-all-start.1 = ((bf16[64,16,2048]{2,1,0:T(8,128)(2,1)}), bf16[64,16,2048]{2,1,0:T(8,128)(2,1)}, u32[]{:S(2)}, u32[]{:S(2)}) async-start(bf16[64,16,2048]{2,1,0:T(8,128)(2,1)} %after.1), calls=%async_computation.1 | async-start | bytes 8388608 | tf_op jit(solution)/shard_map/all_to_all | solution.py:169
  45.2 25.6 %collective-permute-start.2 = (bf16[256,2048]{1,0:T(8,128)(2,1)S(1)}, bf16[256,2048]{1,0:T(8,128)(2,1)S(1)}, u32[]{:S(2)}, u32[]{:S(2)}) collective-permute-start(bf16[256,2048]{1,0:T(8,128)(2,1)S(1)} %copy-done.5), channel_id=1, source_target_pairs={{0,1},{1,2},{2,3},{3,0},{4,5},{5,6},{6,7},{7,4},{8,9},{9,10},{10,1... | collective-permute-start | bytes 3145736 | tf_op jit(solution)/shard_map/ppermute | solution.py:172
  46.5 47.7 %collective-permute-start.3 = (bf16[256,2048]{1,0:T(8,128)(2,1)S(1)}, bf16[256,2048]{1,0:T(8,128)(2,1)S(1)}, u32[]{:S(2)}, u32[]{:S(2)}) collective-permute-start(bf16[256,2048]{1,0:T(8,128)(2,1)S(1)} %copy-done.5), channel_id=1, source_target_pairs={{0,2},{1,3},{2,0},{3,1},{4,6},{5,7},{6,4},{7,5},{8,10},{9,11},{10,... | collective-permute-start | bytes 3145736 | tf_op jit(solution)/shard_map/ppermute | solution.py:172
  49.0 46.3 %collective-permute-start.4 = (bf16[256,2048]{1,0:T(8,128)(2,1)S(1)}, bf16[256,2048]{1,0:T(8,128)(2,1)S(1)}, u32[]{:S(2)}, u32[]{:S(2)}) collective-permute-start(bf16[256,2048]{1,0:T(8,128)(2,1)S(1)} %copy-done.5), channel_id=1, source_target_pairs={{0,3},{1,0},{2,1},{3,2},{4,7},{5,4},{6,5},{7,6},{8,11},{9,8},{10,9... | collective-permute-start | bytes 3145736 | tf_op jit(solution)/shard_map/ppermute | solution.py:172
  133.7 3.4 %copy-start.2 = (bf16[2048,2048]{1,0:T(8,128)(2,1)S(1)}, bf16[2048,2048]{1,0:T(8,128)(2,1)}, u32[]{:S(2)}) copy-start(bf16[2048,2048]{1,0:T(8,128)(2,1)} %constant_dynamic-update-slice_fusion.table_ref) | copy-start | bytes 25165828
  153.7 11.7 %collective-permute-start.5 = (f32[2,256]{1,0:T(2,128)S(1)}, f32[2,256]{1,0:T(2,128)S(1)}, u32[]{:S(2)}, u32[]{:S(2)}) collective-permute-start(f32[2,256]{1,0:T(2,128)S(1)} %pad_maximum_fusion.1), channel_id=1, source_target_pairs={{0,3},{1,0},{2,1},{3,2},{4,7},{5,4},{6,5},{7,6},{8,11},{9,8},{10,9... | collective-permute-start | bytes 6152 | tf_op jit(solution)/shard_map/ppermute | solution.py:200
  156.3 9.1 %collective-permute-start.6 = (f32[2,256]{1,0:T(2,128)S(1)}, f32[2,256]{1,0:T(2,128)S(1)}, u32[]{:S(2)}, u32[]{:S(2)}) collective-permute-start(f32[2,256]{1,0:T(2,128)S(1)} %pad_maximum_fusion.2), channel_id=1, source_target_pairs={{0,2},{1,3},{2,0},{3,1},{4,6},{5,7},{6,4},{7,5},{8,10},{9,11},{10,... | collective-permute-start | bytes 6152 | tf_op jit(solution)/shard_map/ppermute | solution.py:200
  156.8 8.6 %collective-permute-start.7 = (f32[2,256]{1,0:T(2,128)S(1)}, f32[2,256]{1,0:T(2,128)S(1)}, u32[]{:S(2)}, u32[]{:S(2)}) collective-permute-start(f32[2,256]{1,0:T(2,128)S(1)} %pad_maximum_fusion.3), channel_id=1, source_target_pairs={{0,1},{1,2},{2,3},{3,0},{4,5},{5,6},{6,7},{7,4},{8,9},{9,10},{10,1... | collective-permute-start | bytes 6152 | tf_op jit(solution)/shard_map/ppermute | solution.py:200
  157.4 17.4 %all-to-all-start.2 = ((f32[64,1,128]{2,1,0:T(1,128)}), f32[64,1,128]{2,1,0:T(1,128)S(1)}, u32[]{:S(2)}, u32[]{:S(2)}) async-start(f32[64,1,128]{2,1,0:T(1,128)} %bitcast.9), calls=%async_computation.2 | async-start | bytes 65536 | tf_op jit(solution)/shard_map/all_to_all | solution.py:190
  165.4 2.4 %collective-permute-start.8 = (f32[256]{0:T(256)S(1)}, f32[256]{0:T(256)S(1)}, u32[]{:S(2)}, u32[]{:S(2)}) collective-permute-start(f32[256]{0:T(256)S(1)} %bitcast.38), channel_id=1, source_target_pairs={{0,4},{4,8},{8,12},{12,16},{16,20},{20,24},{24,28},{28,32},{32,36}... | collective-permute-start | bytes 3080 | tf_op jit(solution)/shard_map/ppermute | solution.py:201

commit v2 on v1

v2 whole, which is shorter than its diff:
```python
import jax
import jax.numpy as jnp
from jax import lax
from jax.experimental import pallas as pl
from jax.experimental.pallas import tpu as pltpu
from jax.sharding import PartitionSpec as P

SB = 16
GATE_FLOPS = 74_000_000_000
BIN_DEV = 64
LANES = 128
WHOLE_VMEM = 59 * 1024 * 1024
VERY_LOW = -1e30
FLOOR = -1e29
TILE = 256
CHUNK = 512
PAIR = 2
SUB = 8


def pack_kernel(start_ref, range_ref, count_ref, spectra_hbm, out_hbm, held, meta_ref, load_sem, sem, meta_sem):
    blocks, rows, width = held.shape
    batch = blocks // load_sem.shape[0]

    def load(j):
        at = pl.ds(j * batch, batch)
        return pltpu.make_async_copy(spectra_hbm.at[at], held.at[at], load_sem.at[j])

    def copy(i):
        return pltpu.make_async_copy(held.at[i], out_hbm.at[start_ref[i], :, pl.ds(0, width)], sem.at[i])

    for j in range(blocks // batch):
        load(j).start()
    meta_ref[...] = jnp.zeros_like(meta_ref)
    row = lax.broadcasted_iota(jnp.int32, (rows, LANES), 0)
    lane = lax.broadcasted_iota(jnp.int32, (rows, LANES), 1)
    for i in range(blocks):
        first = start_ref[i] * BIN_DEV
        lower = range_ref[0, i] - first
        ends = range_ref[1, i] - first + 1
        value = jnp.where(lane == 0, lower, jnp.where((lane == 1) & (row < count_ref[i]), ends, 0))
        meta_ref[start_ref[i]] = value.astype(jnp.float32).astype(meta_ref.dtype)
    meta_copy = pltpu.make_async_copy(meta_ref, out_hbm.at[:, :, pl.ds(width, LANES)], meta_sem)
    meta_copy.start()
    for j in range(blocks // batch):
        load(j).wait()
        for i in range(j * batch, (j + 1) * batch):
            copy(i).start()
    for i in range(blocks):
        copy(i).wait()
    meta_copy.wait()


def pack_blocks(block_start, block_range, block_count, spectra, owners):
    blocks, rows, width = spectra.shape
    smem = pl.BlockSpec(memory_space=pltpu.SMEM)
    return pl.pallas_call(
        pack_kernel,
        out_shape=jax.ShapeDtypeStruct((owners, rows, width + LANES), spectra.dtype),
        in_specs=[smem, smem, smem, pl.BlockSpec(memory_space=pltpu.HBM)],
        out_specs=pl.BlockSpec(memory_space=pltpu.HBM),
        scratch_shapes=[
            pltpu.VMEM((blocks, rows, width), spectra.dtype),
            pltpu.VMEM((owners, rows, LANES), spectra.dtype),
            pltpu.SemaphoreType.DMA((4,)),
            pltpu.SemaphoreType.DMA((blocks,)),
            pltpu.SemaphoreType.DMA,
        ],
        compiler_params=pltpu.CompilerParams(vmem_limit_bytes=WHOLE_VMEM),
        name="pack_blocks",
    )(block_start, block_range.T, block_count, spectra)


def quarter_kernel(spec_ref, table_hbm, extra_ref, out_hbm, held, load_sem, store_sem, extra_sem):
    part = held.shape[0]
    first = pl.multiple_of(spec_ref[0] * part, part)
    extra = pltpu.make_async_copy(extra_ref, out_hbm.at[pl.ds(part, extra_ref.shape[0])], extra_sem)
    extra.start()
    load = pltpu.make_async_copy(table_hbm.at[pl.ds(first, part)], held, load_sem)
    load.start()
    load.wait()
    store = pltpu.make_async_copy(held, out_hbm.at[pl.ds(0, part)], store_sem)
    store.start()
    store.wait()
    extra.wait()


def cut_quarter(spec, table, extra, part):
    width = table.shape[1]
    hbm = pl.BlockSpec(memory_space=pltpu.HBM)
    return pl.pallas_call(
        quarter_kernel,
        out_shape=jax.ShapeDtypeStruct((part + extra.shape[0], width), table.dtype),
        in_specs=[pl.BlockSpec(memory_space=pltpu.SMEM), hbm, pl.BlockSpec(memory_space=pltpu.VMEM)],
        out_specs=hbm,
        scratch_shapes=[pltpu.VMEM((part, width), table.dtype)] + [pltpu.SemaphoreType.DMA] * 3,
        compiler_params=pltpu.CompilerParams(vmem_limit_bytes=WHOLE_VMEM),
        name="cut_quarter",
    )(spec.reshape(1), table, extra)


def after_kernel(*refs):
    pass


def after(value, *tokens, flops=0):
    hbm = pl.BlockSpec(memory_space=pltpu.HBM)
    return pl.pallas_call(
        after_kernel,
        out_shape=jax.ShapeDtypeStruct(value.shape, value.dtype),
        in_specs=[hbm] * (1 + len(tokens)),
        out_specs=hbm,
        input_output_aliases={0: 0},
        compiler_params=pltpu.CompilerParams(vmem_limit_bytes=WHOLE_VMEM),
        cost_estimate=pl.CostEstimate(flops=flops, bytes_accessed=0, transcendentals=0),
        name="after",
    )(value, *tokens)


def exact_parts(value):
    parts = []
    for _ in range(3):
        top = lax.reduce_precision(value, 8, 7)
        parts.append(top.astype(jnp.bfloat16))
        value = value - top
    return parts


def score_kernel(
    spec_ref, x_hbm, own_hbm, q0_hbm, q1_hbm, q2_hbm, q3_hbm, bins_ref, shift_ref, ret_ref, m0_ref, m1_ref, m2_ref, m3_ref,
    x_ref, table_ref, extra_ref, small_ref, even_ref, odd_ref, held_ref, sum_ref, x_sem, table_sem, small_sem,
):
    tiles = x_ref.shape[0]
    width = table_ref.shape[1]
    slots = TILE // SB
    chunks = table_ref.shape[0] // CHUNK
    part = q0_hbm.shape[0] - SB
    own = own_hbm.shape[0] // part

    def fetch(t):
        return pltpu.make_async_copy(x_hbm.at[pl.ds(t * TILE, TILE)], x_ref.at[t], x_sem.at[t])

    def fetch_part(j):
        source = own_hbm.at[pl.ds(j * part, part)] if j < own else quarters[j - own].at[pl.ds(0, part)]
        return pltpu.make_async_copy(source, table_ref.at[pl.ds(j * part, part)], table_sem.at[j])

    quarters = (q0_hbm, q1_hbm, q2_hbm, q3_hbm)
    smalls = [
        pltpu.make_async_copy(q.at[pl.ds(part, SB)], extra_ref.at[k], small_sem.at[k]) for k, q in enumerate(quarters)
    ]
    parts = table_ref.shape[0] // part
    fetch(0).start()
    for j in range(2 * PAIR):
        fetch_part(j).start()
    sum_ref[...] = jnp.zeros_like(sum_ref)
    lane = lax.broadcasted_iota(jnp.int32, (SUB, LANES), 1)
    spot = lax.broadcasted_iota(jnp.int32, (SUB, LANES), 0)

    def multiply(t, j, into, size=CHUNK):
        at = pl.ds(pl.multiple_of(j * size, size), size)
        into[:, at] = lax.dot_general(
            x_ref[t, :, :width], table_ref[at, :], (((1,), (1,)), ((), ())), preferred_element_type=jnp.float32
        )

    def reduce(t, j, source):
        batch = TILE // chunks
        groups = range(batch // SUB)
        columns = range(source.shape[1] // LANES)
        rows = [pl.ds(pl.multiple_of(j * batch + g * SUB, SUB), SUB) for g in groups]
        here = [slice(g * SUB, (g + 1) * SUB) for g in groups]
        lower, ends = [], []
        for k in range(batch // SB):
            at = pl.ds(pl.multiple_of(j * batch + k * SB, SB), SB)
            meta = x_ref[t, at, width:].astype(jnp.float32)
            for h in range(SB // SUB):
                mine = meta[h * SUB:(h + 1) * SUB]
                lower.append(jnp.broadcast_to(mine[:, 0:1], (SUB, LANES)))
                ends.append(jnp.broadcast_to(mine[:, 1:2], (SUB, LANES)))
        peak = [jnp.full((SUB, LANES), FLOOR, jnp.float32) for g in groups]
        for c in columns:
            at = slice(c * LANES, (c + 1) * LANES)
            bins = jnp.broadcast_to(small_ref[0:1, at], (SUB, LANES))
            for g in groups:
                inside = (bins >= lower[g]) & (bins < ends[g])
                masked = jnp.where(inside, source[rows[g], at], VERY_LOW)
                held_ref[here[g], at] = masked
                peak[g] = jnp.maximum(peak[g], masked)
        peak = [jnp.broadcast_to(jnp.max(p, axis=1, keepdims=True), (SUB, LANES)) for p in peak]
        denom = [jnp.zeros((SUB, LANES), jnp.float32) for g in groups]
        numer = [jnp.zeros((SUB, LANES), jnp.float32) for g in groups]
        for c in columns:
            at = slice(c * LANES, (c + 1) * LANES)
            shift = jnp.broadcast_to(small_ref[1:2, at], (SUB, LANES))
            for g in groups:
                weights = jnp.exp(held_ref[here[g], at] - peak[g])
                held_ref[here[g], at] = weights
                denom[g] = denom[g] + weights
                numer[g] = numer[g] + weights * shift
        denom = [jnp.broadcast_to(jnp.sum(d, axis=1, keepdims=True), (SUB, LANES)) for d in denom]
        numer = [jnp.broadcast_to(jnp.sum(n, axis=1, keepdims=True), (SUB, LANES)) for n in numer]
        live = [d > 0.0 for d in denom]
        safe = [jnp.where(live[g], denom[g], 1.0) for g in groups]
        inv = [jnp.where(live[g], 1.0 / safe[g], 0.0) for g in groups]
        for c in columns:
            at = slice(c * LANES, (c + 1) * LANES)
            total = sum_ref[:, at]
            for g in groups:
                total = total + held_ref[here[g], at] * inv[g]
            sum_ref[:, at] = total
        lse = [jnp.where(live[g], peak[g] + jnp.log(safe[g]), 0.0) for g in groups]
        halves = SB // SUB
        for k in range(batch // SB):
            flat = 0.0
            for h in range(halves):
                g = k * halves + h
                row = spot + h * SUB
                flat = flat + jnp.where(lane == row, lse[g], jnp.where(lane == row + SB, numer[g] * inv[g], 0.0))
            slot = t * slots + j * (batch // SB) + k
            ret_ref[pl.ds(slot, 1), :] = jnp.sum(flat, axis=0, keepdims=True)

    fetch(0).wait()
    for j in range(0, parts, PAIR):
        for k in range(j, j + PAIR):
            fetch_part(k).wait()
        for k in range(j + 2 * PAIR, min(j + 3 * PAIR, parts)):
            fetch_part(k).start()
        if j + 2 * PAIR == parts:
            for copy in smalls:
                copy.start()
            for t in range(1, tiles):
                fetch(t).start()
        multiply(0, j // PAIR, even_ref, PAIR * part)
    small_ref[0:1, :own * part] = bins_ref[...]
    small_ref[1:2, :own * part] = shift_ref[...]
    for k, copy in enumerate(smalls):
        copy.wait()
        extra = extra_ref[k].astype(jnp.float32)[0:1]
        at = slice((own + k) * part, (own + k + 1) * part)
        small_ref[0:1, at] = extra[:, :part] + BIN_DEV
        small_ref[1:2, at] = extra[:, part:2 * part] + extra[:, 2 * part:3 * part] + extra[:, 3 * part:4 * part]

    for t in range(1, tiles + 1):
        if t < tiles:
            fetch(t).wait()
        into, source = (even_ref, odd_ref) if t % 2 == 0 else (odd_ref, even_ref)

        def one_chunk(j, carry, t=t, into=into, source=source):
            if t < tiles:
                multiply(t, j, into)
            reduce(t - 1, j, source)
            return carry

        lax.fori_loop(0, chunks, one_chunk, 0)
    for k, m_ref in enumerate((m0_ref, m1_ref, m2_ref, m3_ref)):
        mine = lax.rem(spec_ref[0] + own - k, own)
        for h, at in enumerate((pl.ds(pl.multiple_of(mine * part, part), part), pl.ds((own + k) * part, part))):
            m_ref[h:h + 1, :] = jnp.sum(sum_ref[:, at], axis=0, keepdims=True)


def score_blocks(spec, rows, table, quarters, bins, shifts):
    total = rows.shape[0]
    wide, width = 2 * table.shape[0], table.shape[1]
    part = quarters[0].shape[0] - SB
    vmem = pl.BlockSpec(memory_space=pltpu.VMEM)
    hbm = pl.BlockSpec(memory_space=pltpu.HBM)
    return pl.pallas_call(
        score_kernel,
        out_shape=(
            jax.ShapeDtypeStruct((total // SB, LANES), jnp.float32),
        )
        + (jax.ShapeDtypeStruct((2, part), jnp.float32),) * len(quarters),
        in_specs=[pl.BlockSpec(memory_space=pltpu.SMEM)] + [hbm] * (2 + len(quarters)) + [vmem, vmem],
        out_specs=(vmem,) * (1 + len(quarters)),
        scratch_shapes=[
            pltpu.VMEM((total // TILE, TILE, rows.shape[1]), rows.dtype),
            pltpu.VMEM((wide, width), table.dtype),
            pltpu.VMEM((len(quarters), SB, width), table.dtype),
            pltpu.VMEM((2, wide), jnp.float32),
            pltpu.VMEM((TILE, wide), jnp.float32),
            pltpu.VMEM((TILE, wide), jnp.float32),
            pltpu.VMEM((TILE * CHUNK // wide, wide), jnp.float32),
            pltpu.VMEM((SUB, wide), jnp.float32),
            pltpu.SemaphoreType.DMA((total // TILE,)),
            pltpu.SemaphoreType.DMA((wide // part,)),
            pltpu.SemaphoreType.DMA((len(quarters),)),
        ],
        compiler_params=pltpu.CompilerParams(vmem_limit_bytes=WHOLE_VMEM),
        cost_estimate=pl.CostEstimate(
            flops=2 * total * width * wide, bytes_accessed=2 * (total + wide) * width, transcendentals=total * wide
        ),
        name="score_blocks",
    )(spec.reshape(1), rows, table, *quarters, bins, shifts)


def body(spectra, block_start, block_range, block_count, peptide_table, peptide_bin, peptide_shift):
    owners, specs = lax.axis_size("mass"), lax.axis_size("spec")
    spec = lax.axis_index("spec")
    own = peptide_table.shape[0]
    part = own // specs
    back = [((i + 1) % owners, i) for i in range(owners)]
    forth = [(i, (i + 1) % owners) for i in range(owners)]

    bins = (peptide_bin - lax.axis_index("mass") * BIN_DEV).astype(jnp.float32)
    values = jnp.stack([bins.astype(jnp.bfloat16)] + exact_parts(peptide_shift)).reshape(4, specs, part)
    extra = lax.dynamic_index_in_dim(values, spec, 1, False).reshape(1, 4 * part)
    extra = jnp.pad(extra, ((0, SB - 1), (0, peptide_table.shape[1] - 4 * part)))
    quarters = [lax.ppermute(cut_quarter(spec, peptide_table, extra, part), "mass", back)]
    packed = pack_blocks(block_start, block_range, block_count, spectra, owners)
    received = lax.all_to_all(packed, "mass", split_axis=0, concat_axis=0, tiled=True)
    for k in range(1, specs):
        quarters.append(lax.ppermute(quarters[0], "spec", [(i, (i + k) % specs) for i in range(specs)]))
    quarters[0] = after(*quarters, flops=GATE_FLOPS)

    ret, *messages = score_blocks(
        spec, received.reshape(owners * SB, -1), peptide_table, quarters, bins[None], peptide_shift[None]
    )

    chosen = block_start[:, None] == jnp.arange(owners, dtype=jnp.int32)[None, :]
    home = lax.all_to_all(ret, "mass", split_axis=0, concat_axis=0, tiled=True)
    picked = jnp.sum(jnp.where(chosen[:, :, None], home[None, :, : 2 * SB], 0.0), axis=1)
    lse, mean_shift = picked[:, :SB], picked[:, SB:]

    total = messages[0]
    for k in range(1, specs):
        total = total + lax.ppermute(messages[k], "spec", [(i, (i + specs - k) % specs) for i in range(specs)])
    support = total[0] + lax.ppermute(total[1], "mass", forth)
    return (lse, mean_shift, support)


def solution(mesh):
    in_specs = (
        P(("mass", "spec"), None, None),
        P(("mass", "spec")),
        P(("mass", "spec"), None),
        P(("mass", "spec")),
        P("mass", None),
        P("mass"),
        P("mass"),
    )
    out_specs = (P(("mass", "spec"), None), P(("mass", "spec"), None), P(("mass", "spec")))
    return jax.shard_map(body, mesh=mesh, in_specs=in_specs, out_specs=out_specs, check_vma=False)
```

time: 177 us -> 169 us (0.955)
  local copies, waits for them, and re-layouts: 22.2 us -> 3.17 us
  waiting for transfers between devices: 87.9 us -> 101 us
  starting transfers between devices: 41.6 us -> 35.4 us
  Pallas kernels: 20 us -> 24.9 us
    all_to_all x1, waiting for transfers between devices: 37.3 us -> 56.3 us  [body(): lax.all_to_all(packed, 'mass', split_axis=0, concat_axis=0, tiled=True)]
    unnamed x29 -> x12, local copies, waits for them, and re-layouts: 17.8 us -> 2.34 us
    ppermute x5 -> x4, starting transfers between devices: 13.1 us -> 8.24 us  [the longest x3 4.92 us: body(): lax.ppermute(messages[k], 'spec', [(i, (i + specs - k) % specs) for i in...]
    all_to_all x1 -> x0, starting transfers between devices: 4.7 us -> none  [body(): lax.all_to_all(meta_out, 'mass', split_axis=0, concat_axis=0, tiled=True)]
    ppermute x3, waiting for transfers between devices: 41.9 us -> 38.1 us  [body(): lax.ppermute(quarters[0], 'spec', [(i, (i + k) % specs) for i in range(sp...]
    pallas_call x0 -> x1, Pallas kernels: none -> 3.07 us  [cut_quarter(): pl.pallas_call(quarter_kernel, out_shape=jax.ShapeDtypeStruct((part + ext...]
    all_to_all x1, starting transfers between devices: 9.13 us -> 11 us  [body(): lax.all_to_all(packed, 'mass', split_axis=0, concat_axis=0, tiled=True)]
  transfers between devices with their start and end apart: 12 -> 10, of which waited for: 6 -> 6; matrix products, arithmetic and copies ran while one was open for 8% -> 1% of each run, Pallas kernels for 2% -> 2%
where the time goes in v2:
time: 169 us; the launch traced here: 168 us
  waiting for transfers between devices  101 us (60%)
  starting transfers between devices  35.4 us (21%)
  Pallas kernels  24.9 us (15%)
  other arithmetic  3.55 us (2%)
  local copies, waits for them, and re-layouts  3.17 us (2%)
    all_to_all x1, waiting for transfers between devices, body(): lax.all_to_all(packed, 'mass', split_axis=0, concat_axis=0, tiled=True)  56.3 us
    ppermute x3, waiting for transfers between devices, body(): lax.ppermute(quarters[0], 'spec', [(i, (i + k) % specs) for i in range(sp...  38.1 us
    pallas_call x1, Pallas kernels, score_blocks(): pl.pallas_call(score_kernel, out_shape=(jax.ShapeDtypeStruct((total // SB...  18.1 us
    all_to_all x1, starting transfers between devices, body(): lax.all_to_all(packed, 'mass', split_axis=0, concat_axis=0, tiled=True)  11 us
    all_to_all x1, starting transfers between devices, body(): home = lax.all_to_all(ret, 'mass', split_axis=0, concat_axis=0, tiled=True)  9.65 us
    all_to_all x1, waiting for transfers between devices, body(): home = lax.all_to_all(ret, 'mass', split_axis=0, concat_axis=0, tiled=True)  5.72 us
    ppermute x3, starting transfers between devices, body(): lax.ppermute(messages[k], 'spec', [(i, (i + specs - k) % specs) for i in...  4.92 us
    ppermute x3, starting transfers between devices, body(): lax.ppermute(quarters[0], 'spec', [(i, (i + k) % specs) for i in range(sp...  4.92 us
  transfers between devices with their start and end apart: 10, of which 6 were waited for; matrix products, arithmetic and copies ran while one was open for 1% of the time, Pallas kernels for 2%

profile of v2, /device:TPU:1, one launch (start us, length us, event | category | flops | bytes accessed | tf_op | source)
XLA Modules:
  0.0 168.5 jit_solution(2084992050681340234)
XLA Ops:
  0.6 0.7 reduce-precision_convert_fusion.1
  1.4 1.3 fusion.5
  2.7 0.6 pad.4.extra_ref
  3.3 3.1 %cut_quarter.1 = bf16[272,2048]{1,0:T(8,128)(2,1)} custom-call(s32[1]{0:T(128)} %bitcast.spec_ref, bf16[1024,2048]{1,0:T(8,128)(2,1)} %own_hbm.1, bf16[16,2048]{1,0:T(8,128)(2,1)} %pad.4.extra_ref), custom_call_target="tpu_custom_call" | custom-call | tf_op jit(solution)/shard_map/cut_quarter/pallas_call | solution.py:91
  6.4 3.3 %collective-permute-start = (bf16[272,2048]{1,0:T(8,128)(2,1)}, bf16[272,2048]{1,0:T(8,128)(2,1)S(1)}, u32[]{:S(2)}, u32[]{:S(2)}) collective-permute-start(bf16[272,2048]{1,0:T(8,128)(2,1)} %cut_quarter.1), channel_id=1, source_target_pairs={{4,0},{8,4},{12,8},{16,12},{20,16},{24,20},{28,24},{32,28},{36,32}... | collective-permute-start | bytes 3342344 | tf_op jit(solution)/shard_map/ppermute | solution.py:307
  9.7 3.7 %pack_blocks.1 = bf16[64,16,2176]{2,1,0:T(8,128)(2,1)} custom-call(s32[32]{0:T(128)} %start_ref.1, s32[2,32]{1,0:T(2,128)} %bitcast.19, s32[32]{0:T(128)} %count_ref.1, bf16[32,16,2048]{2,1,0:T(8,128)(2,1)} %spectra_hbm.1), custom_call_target="tpu_custom_call" | custom-call | tf_op jit(solution)/shard_map/pack_blocks/pallas_call | solution.py:57
  13.4 11.0 %all-to-all-start = ((bf16[64,16,2176]{2,1,0:T(8,128)(2,1)}), bf16[64,16,2176]{2,1,0:T(8,128)(2,1)}, u32[]{:S(2)}, u32[]{:S(2)}) async-start(bf16[64,16,2176]{2,1,0:T(8,128)(2,1)} %pack_blocks.1), calls=%async_computation | async-start | bytes 8912896 | tf_op jit(solution)/shard_map/all_to_all | solution.py:309
  24.4 0.0 collective-permute-done.refs_0_
  24.4 0.0 copy-start.2
  24.4 1.3 collective-permute-start.1
  25.7 2.5 %collective-permute-start.2 = (bf16[272,2048]{1,0:T(8,128)(2,1)S(1)}, bf16[272,2048]{1,0:T(8,128)(2,1)S(1)}, u32[]{:S(2)}, u32[]{:S(2)}) collective-permute-start(bf16[272,2048]{1,0:T(8,128)(2,1)S(1)} %collective-permute-done.refs_0_), channel_id=1, source_target_pairs={{0,2},{1,3},{2,0},{3,1},{4,6},{5,7},{6,4},{7,5},{8,10},{9,11},{10,... | collective-permute-start | bytes 3342344 | tf_op jit(solution)/shard_map/ppermute | solution.py:311
  28.2 1.2 collective-permute-start.3
  29.4 11.1 %collective-permute-done.1.refs_1_.q1_hbm = bf16[272,2048]{1,0:T(8,128)(2,1)S(1)} collective-permute-done((bf16[272,2048]{1,0:T(8,128)(2,1)S(1)}, bf16[272,2048]{1,0:T(8,128)(2,1)S(1)}, u32[]{:S(2)}, u32[]{:S(2)}) %collective-permute-start.1) | collective-permute-done | bytes 1114144 | tf_op jit(solution)/shard_map/ppermute | solution.py:311
  40.5 0.0 copy-start.1
  40.5 17.9 %collective-permute-done.2.refs_2_.q2_hbm = bf16[272,2048]{1,0:T(8,128)(2,1)S(1)} collective-permute-done((bf16[272,2048]{1,0:T(8,128)(2,1)S(1)}, bf16[272,2048]{1,0:T(8,128)(2,1)S(1)}, u32[]{:S(2)}, u32[]{:S(2)}) %collective-permute-start.2) | collective-permute-done | bytes 1114144 | tf_op jit(solution)/shard_map/ppermute | solution.py:311
  58.3 0.0 copy-start.3
  58.4 9.1 %collective-permute-done.3.refs_3_.q3_hbm = bf16[272,2048]{1,0:T(8,128)(2,1)S(1)} collective-permute-done((bf16[272,2048]{1,0:T(8,128)(2,1)S(1)}, bf16[272,2048]{1,0:T(8,128)(2,1)S(1)}, u32[]{:S(2)}, u32[]{:S(2)}) %collective-permute-start.3) | collective-permute-done | bytes 1114144 | tf_op jit(solution)/shard_map/ppermute | solution.py:311
  67.4 0.0 copy-done.2
  67.4 0.0 copy-done.1
  67.4 0.0 copy-done.3
  67.4 0.0 copy-start.4
  67.4 1.0 copy-done.4
  68.4 56.3 %all-to-all-done = bf16[64,16,2176]{2,1,0:T(8,128)(2,1)} async-done(((bf16[64,16,2176]{2,1,0:T(8,128)(2,1)}), bf16[64,16,2176]{2,1,0:T(8,128)(2,1)}, u32[]{:S(2)}, u32[]{:S(2)}) %all-to-all-start) | async-done | bytes 4456480 | tf_op jit(solution)/shard_map/all_to_all | solution.py:309
  124.7 0.0 copy-start
  124.7 18.1 %score_blocks.1 = (f32[64,128]{1,0:T(8,128)}, f32[2,256]{1,0:T(2,128)}, f32[2,256]{1,0:T(2,128)}, f32[2,256]{1,0:T(2,128)}, f32[2,256]{1,0:T(2,128)}) custom-call(s32[1]{0:T(128)} %bitcast.spec_ref, bf16[1024,2176]{1,0:T(8,128)(2,1)} %bitcast.2.x_hbm, bf16[1024,2048]{1,0:T(8,128)(2,1)} %own_hbm.1, bf16[272,2048]{1,0:T(8,128)(2,1)} %after.1.q0_hbm, ...), custom_call_target="tpu_custom_call" | custom-call | flops 8589934592 | bytes 12582912 | tf_op jit(solution)/shard_map/score_blocks/pallas_call | solution.py:266
  142.8 1.3 collective-permute-start.6
  144.1 2.5 %collective-permute-start.5 = (f32[2,256]{1,0:T(2,128)}, f32[2,256]{1,0:T(2,128)S(1)}, u32[]{:S(2)}, u32[]{:S(2)}) collective-permute-start(f32[2,256]{1,0:T(2,128)} %get-tuple-element.11), channel_id=1, source_target_pairs={{0,2},{1,3},{2,0},{3,1},{4,6},{5,7},{6,4},{7,5},{8,10},{9,11},{10,... | collective-permute-start | bytes 6152 | tf_op jit(solution)/shard_map/ppermute | solution.py:325
  146.6 1.2 collective-permute-start.4
  147.7 9.6 %all-to-all-start.1 = ((f32[64,1,128]{2,1,0:T(1,128)}), f32[64,1,128]{2,1,0:T(1,128)S(1)}, u32[]{:S(2)}, u32[]{:S(2)}) async-start(f32[64,1,128]{2,1,0:T(1,128)} %bitcast.14), calls=%async_computation.1 | async-start | bytes 65536 | tf_op jit(solution)/shard_map/all_to_all | solution.py:319
  157.4 0.0 collective-permute-done.6
  157.4 0.0 collective-permute-done.5
  157.4 0.0 collective-permute-done.4
  157.4 0.7 add_add_fusion
  158.1 1.6 collective-permute-start.7
  159.7 0.0 copy-done
  159.7 0.1 iota_compare_fusion
  159.8 0.6 collective-permute-done.7
  160.5 0.6 add.22
  161.0 5.7 %all-to-all-done.1 = f32[64,1,128]{2,1,0:T(1,128)S(1)} async-done(((f32[64,1,128]{2,1,0:T(1,128)}), f32[64,1,128]{2,1,0:T(1,128)S(1)}, u32[]{:S(2)}, u32[]{:S(2)}) %all-to-all-start.1) | async-done | bytes 32800 | tf_op jit(solution)/shard_map/all_to_all | solution.py:319
  166.8 0.1 copy.13
  166.8 0.2 select_reduce_fusion
  167.1 0.1 fusion.6
  167.1 0.7 copy.14
  167.8 0.7 copy.15
  (7 shorter events, 0.1 us)
Async XLA Ops:
  6.4 18.0 %collective-permute-start = (bf16[272,2048]{1,0:T(8,128)(2,1)}, bf16[272,2048]{1,0:T(8,128)(2,1)S(1)}, u32[]{:S(2)}, u32[]{:S(2)}) collective-permute-start(bf16[272,2048]{1,0:T(8,128)(2,1)} %cut_quarter.1), channel_id=1, source_target_pairs={{4,0},{8,4},{12,8},{16,12},{20,16},{24,20},{28,24},{32,28},{36,32}... | collective-permute-start | bytes 3342344 | tf_op jit(solution)/shard_map/ppermute | solution.py:307
  13.4 111.3 %all-to-all-start = ((bf16[64,16,2176]{2,1,0:T(8,128)(2,1)}), bf16[64,16,2176]{2,1,0:T(8,128)(2,1)}, u32[]{:S(2)}, u32[]{:S(2)}) async-start(bf16[64,16,2176]{2,1,0:T(8,128)(2,1)} %pack_blocks.1), calls=%async_computation | async-start | bytes 8912896 | tf_op jit(solution)/shard_map/all_to_all | solution.py:309
  24.4 43.0 %copy-start.2 = (bf16[272,2048]{1,0:T(8,128)(2,1)}, bf16[272,2048]{1,0:T(8,128)(2,1)S(1)}, u32[]{:S(2)}) copy-start(bf16[272,2048]{1,0:T(8,128)(2,1)S(1)} %collective-permute-done.refs_0_) | copy-start | bytes 3342340
  24.4 16.0 %collective-permute-start.1 = (bf16[272,2048]{1,0:T(8,128)(2,1)S(1)}, bf16[272,2048]{1,0:T(8,128)(2,1)S(1)}, u32[]{:S(2)}, u32[]{:S(2)}) collective-permute-start(bf16[272,2048]{1,0:T(8,128)(2,1)S(1)} %collective-permute-done.refs_0_), channel_id=1, source_target_pairs={{0,1},{1,2},{2,3},{3,0},{4,5},{5,6},{6,7},{7,4},{8,9},{9,10},{10,1... | collective-permute-start | bytes 3342344 | tf_op jit(solution)/shard_map/ppermute | solution.py:311
  25.7 32.6 %collective-permute-start.2 = (bf16[272,2048]{1,0:T(8,128)(2,1)S(1)}, bf16[272,2048]{1,0:T(8,128)(2,1)S(1)}, u32[]{:S(2)}, u32[]{:S(2)}) collective-permute-start(bf16[272,2048]{1,0:T(8,128)(2,1)S(1)} %collective-permute-done.refs_0_), channel_id=1, source_target_pairs={{0,2},{1,3},{2,0},{3,1},{4,6},{5,7},{6,4},{7,5},{8,10},{9,11},{10,... | collective-permute-start | bytes 3342344 | tf_op jit(solution)/shard_map/ppermute | solution.py:311
  28.2 39.2 %collective-permute-start.3 = (bf16[272,2048]{1,0:T(8,128)(2,1)S(1)}, bf16[272,2048]{1,0:T(8,128)(2,1)S(1)}, u32[]{:S(2)}, u32[]{:S(2)}) collective-permute-start(bf16[272,2048]{1,0:T(8,128)(2,1)S(1)} %collective-permute-done.refs_0_), channel_id=1, source_target_pairs={{0,3},{1,0},{2,1},{3,2},{4,7},{5,4},{6,5},{7,6},{8,11},{9,8},{10,9... | collective-permute-start | bytes 3342344 | tf_op jit(solution)/shard_map/ppermute | solution.py:311
  40.5 26.9 %copy-start.1 = (bf16[272,2048]{1,0:T(8,128)(2,1)}, bf16[272,2048]{1,0:T(8,128)(2,1)S(1)}, u32[]{:S(2)}) copy-start(bf16[272,2048]{1,0:T(8,128)(2,1)S(1)} %collective-permute-done.1.refs_1_.q1_hbm) | copy-start | bytes 3342340
  58.3 9.1 %copy-start.3 = (bf16[272,2048]{1,0:T(8,128)(2,1)}, bf16[272,2048]{1,0:T(8,128)(2,1)S(1)}, u32[]{:S(2)}) copy-start(bf16[272,2048]{1,0:T(8,128)(2,1)S(1)} %collective-permute-done.2.refs_2_.q2_hbm) | copy-start | bytes 3342340
  67.4 1.0 copy-start.4
  124.7 35.1 %copy-start = (s32[32]{0:T(128)S(1)}, s32[32]{0:T(128)}, u32[]{:S(2)}) copy-start(s32[32]{0:T(128)} %start_ref.1) | copy-start | bytes 388
  142.8 14.6 %collective-permute-start.6 = (f32[2,256]{1,0:T(2,128)}, f32[2,256]{1,0:T(2,128)S(1)}, u32[]{:S(2)}, u32[]{:S(2)}) collective-permute-start(f32[2,256]{1,0:T(2,128)} %get-tuple-element.12), channel_id=1, source_target_pairs={{0,1},{1,2},{2,3},{3,0},{4,5},{5,6},{6,7},{7,4},{8,9},{9,10},{10,1... | collective-permute-start | bytes 6152 | tf_op jit(solution)/shard_map/ppermute | solution.py:325
  144.1 13.3 %collective-permute-start.5 = (f32[2,256]{1,0:T(2,128)}, f32[2,256]{1,0:T(2,128)S(1)}, u32[]{:S(2)}, u32[]{:S(2)}) collective-permute-start(f32[2,256]{1,0:T(2,128)} %get-tuple-element.11), channel_id=1, source_target_pairs={{0,2},{1,3},{2,0},{3,1},{4,6},{5,7},{6,4},{7,5},{8,10},{9,11},{10,... | collective-permute-start | bytes 6152 | tf_op jit(solution)/shard_map/ppermute | solution.py:325
  146.6 10.9 %collective-permute-start.4 = (f32[2,256]{1,0:T(2,128)}, f32[2,256]{1,0:T(2,128)S(1)}, u32[]{:S(2)}, u32[]{:S(2)}) collective-permute-start(f32[2,256]{1,0:T(2,128)} %get-tuple-element.10), channel_id=1, source_target_pairs={{0,3},{1,0},{2,1},{3,2},{4,7},{5,4},{6,5},{7,6},{8,11},{9,8},{10,9... | collective-permute-start | bytes 6152 | tf_op jit(solution)/shard_map/ppermute | solution.py:325
  147.7 19.0 %all-to-all-start.1 = ((f32[64,1,128]{2,1,0:T(1,128)}), f32[64,1,128]{2,1,0:T(1,128)S(1)}, u32[]{:S(2)}, u32[]{:S(2)}) async-start(f32[64,1,128]{2,1,0:T(1,128)} %bitcast.14), calls=%async_computation.1 | async-start | bytes 65536 | tf_op jit(solution)/shard_map/all_to_all | solution.py:319
  158.1 2.4 %collective-permute-start.7 = (f32[256]{0:T(256)S(1)}, f32[256]{0:T(256)S(1)}, u32[]{:S(2)}, u32[]{:S(2)}) collective-permute-start(f32[256]{0:T(256)S(1)} %bitcast.20), channel_id=1, source_target_pairs={{0,4},{4,8},{8,12},{12,16},{16,20},{20,24},{24,28},{28,32},{32,36}... | collective-permute-start | bytes 3080 | tf_op jit(solution)/shard_map/ppermute | solution.py:326

commit v3 on v2

--- a/solution.py
+++ b/solution.py
@@ -7,6 +7,7 @@
 
 SB = 16
 GATE_FLOPS = 74_000_000_000
+PICK_FLOPS = 0
 BIN_DEV = 64
 LANES = 128
 WHOLE_VMEM = 59 * 1024 * 1024
@@ -14,13 +15,19 @@
 FLOOR = -1e29
 TILE = 256
 CHUNK = 512
-PAIR = 2
+PAIR = 4
 SUB = 8
 
 
-def pack_kernel(start_ref, range_ref, count_ref, spectra_hbm, out_hbm, held, meta_ref, load_sem, sem, meta_sem):
+def prepare_kernel(
+    spec_ref, mass_ref, start_ref, range_ref, count_ref, bins_ref, shift_ref, spectra_hbm, table_hbm,
+    out_hbm, quarter_hbm, held, meta_ref, part_ref, extra_ref, load_sem, part_sem, sem, tail_sem,
+):
     blocks, rows, width = held.shape
-    batch = blocks // load_sem.shape[0]
+    steps = load_sem.shape[0]
+    batch, part = blocks // steps, part_ref.shape[0]
+    piece = part // steps
+    first = pl.multiple_of(spec_ref[0] * part, part)
 
     def load(j):
         at = pl.ds(j * batch, batch)
@@ -29,74 +36,111 @@
     def copy(i):
         return pltpu.make_async_copy(held.at[i], out_hbm.at[start_ref[i], :, pl.ds(0, width)], sem.at[i])
 
-    for j in range(blocks // batch):
+    def load_part(j):
+        at = pl.ds(j * piece, piece)
+        return pltpu.make_async_copy(table_hbm.at[pl.ds(first + j * piece, piece)], part_ref.at[at], part_sem.at[j])
+
+    def store_part(j):
+        at = pl.ds(j * piece, piece)
+        return pltpu.make_async_copy(part_ref.at[at], quarter_hbm.at[at], part_sem.at[steps + j])
+
+    for j in range(steps):
         load(j).start()
+        load_part(j).start()
+
+    bins = (bins_ref[0:1, pl.ds(first, part)] - mass_ref[0] * BIN_DEV).astype(jnp.float32)
+    rest = shift_ref[0:1, pl.ds(first, part)]
+    extra_ref[...] = jnp.zeros_like(extra_ref)
+    extra_ref[:, :part] = jnp.broadcast_to(bins, (SB, part)).astype(extra_ref.dtype)
+    for k in range(1, 4):
+        top = jnp.broadcast_to(rest, (SB, part)).astype(extra_ref.dtype)
+        extra_ref[:, k * part:(k + 1) * part] = top
+        rest = rest - top.astype(jnp.float32)[0:1]
+    extra_copy = pltpu.make_async_copy(extra_ref, quarter_hbm.at[pl.ds(part, SB)], tail_sem.at[0])
+    extra_copy.start()
+
     meta_ref[...] = jnp.zeros_like(meta_ref)
     row = lax.broadcasted_iota(jnp.int32, (rows, LANES), 0)
     lane = lax.broadcasted_iota(jnp.int32, (rows, LANES), 1)
     for i in range(blocks):
-        first = start_ref[i] * BIN_DEV
-        lower = range_ref[0, i] - first
-        ends = range_ref[1, i] - first + 1
+        low = start_ref[i] * BIN_DEV
+        lower = range_ref[0, i] - low
+        ends = range_ref[1, i] - low + 1
         value = jnp.where(lane == 0, lower, jnp.where((lane == 1) & (row < count_ref[i]), ends, 0))
         meta_ref[start_ref[i]] = value.astype(jnp.float32).astype(meta_ref.dtype)
-    meta_copy = pltpu.make_async_copy(meta_ref, out_hbm.at[:, :, pl.ds(width, LANES)], meta_sem)
+    meta_copy = pltpu.make_async_copy(meta_ref, out_hbm.at[:, :, pl.ds(width, LANES)], tail_sem.at[1])
     meta_copy.start()
-    for j in range(blocks // batch):
+    for j in range(steps):
         load(j).wait()
         for i in range(j * batch, (j + 1) * batch):
             copy(i).start()
+        load_part(j).wait()
+        store_part(j).start()
     for i in range(blocks):
         copy(i).wait()
+    for j in range(steps):
+        store_part(j).wait()
+    extra_copy.wait()
     meta_copy.wait()
 
 
-def pack_blocks(block_start, block_range, block_count, spectra, owners):
+def prepare(spec, mass, block_start, block_range, block_count, bins, shifts, spectra, table, owners, part):
     blocks, rows, width = spectra.shape
     smem = pl.BlockSpec(memory_space=pltpu.SMEM)
+    vmem = pl.BlockSpec(memory_space=pltpu.VMEM)
+    hbm = pl.BlockSpec(memory_space=pltpu.HBM)
+    steps = 4
     return pl.pallas_call(
-        pack_kernel,
-        out_shape=jax.ShapeDtypeStruct((owners, rows, width + LANES), spectra.dtype),
-        in_specs=[smem, smem, smem, pl.BlockSpec(memory_space=pltpu.HBM)],
-        out_specs=pl.BlockSpec(memory_space=pltpu.HBM),
+        prepare_kernel,
+        out_shape=(
+            jax.ShapeDtypeStruct((owners, rows, width + LANES), spectra.dtype),
+            jax.ShapeDtypeStruct((part + SB, width), table.dtype),
+        ),
+        in_specs=[smem] * 5 + [vmem] * 2 + [hbm] * 2,
+        out_specs=(hbm, hbm),
         scratch_shapes=[
             pltpu.VMEM((blocks, rows, width), spectra.dtype),
             pltpu.VMEM((owners, rows, LANES), spectra.dtype),
-            pltpu.SemaphoreType.DMA((4,)),
+            pltpu.VMEM((part, width), table.dtype),
+            pltpu.VMEM((SB, width), table.dtype),
+            pltpu.SemaphoreType.DMA((steps,)),
+            pltpu.SemaphoreType.DMA((2 * steps,)),
             pltpu.SemaphoreType.DMA((blocks,)),
-            pltpu.SemaphoreType.DMA,
+            pltpu.SemaphoreType.DMA((2,)),
         ],
         compiler_params=pltpu.CompilerParams(vmem_limit_bytes=WHOLE_VMEM),
-        name="pack_blocks",
-    )(block_start, block_range.T, block_count, spectra)
-
-
-def quarter_kernel(spec_ref, table_hbm, extra_ref, out_hbm, held, load_sem, store_sem, extra_sem):
-    part = held.shape[0]
-    first = pl.multiple_of(spec_ref[0] * part, part)
-    extra = pltpu.make_async_copy(extra_ref, out_hbm.at[pl.ds(part, extra_ref.shape[0])], extra_sem)
-    extra.start()
-    load = pltpu.make_async_copy(table_hbm.at[pl.ds(first, part)], held, load_sem)
-    load.start()
-    load.wait()
-    store = pltpu.make_async_copy(held, out_hbm.at[pl.ds(0, part)], store_sem)
-    store.start()
-    store.wait()
-    extra.wait()
-
-
-def cut_quarter(spec, table, extra, part):
-    width = table.shape[1]
-    hbm = pl.BlockSpec(memory_space=pltpu.HBM)
-    return pl.pallas_call(
-        quarter_kernel,
-        out_shape=jax.ShapeDtypeStruct((part + extra.shape[0], width), table.dtype),
-        in_specs=[pl.BlockSpec(memory_space=pltpu.SMEM), hbm, pl.BlockSpec(memory_space=pltpu.VMEM)],
-        out_specs=hbm,
-        scratch_shapes=[pltpu.VMEM((part, width), table.dtype)] + [pltpu.SemaphoreType.DMA] * 3,
-        compiler_params=pltpu.CompilerParams(vmem_limit_bytes=WHOLE_VMEM),
-        name="cut_quarter",
-    )(spec.reshape(1), table, extra)
+        name="prepare",
+    )(
+        spec.reshape(1), mass.reshape(1), block_start, block_range.T, block_count, bins[None], shifts[None],
+        spectra, table,
+    )
+
+
+def pick_kernel(start_ref, home_ref, lse_ref, mean_ref, rows_ref):
+    blocks = lse_ref.shape[1]
+    rows_ref[...] = jnp.zeros_like(rows_ref)
+    for i in range(blocks):
+        rows_ref[i:i + 1, :] = home_ref[pl.ds(start_ref[i], 1), :]
+    turned = rows_ref[...].T
+    lse_ref[...] = turned[:SB, :blocks]
+    mean_ref[...] = turned[SB:2 * SB, :blocks]
+
+
+def pick(block_start, home):
+    blocks = block_start.shape[0]
+    out = jax.ShapeDtypeStruct((SB, blocks), home.dtype)
+    vmem = pl.BlockSpec(memory_space=pltpu.VMEM)
+    lse, mean = pl.pallas_call(
+        pick_kernel,
+        out_shape=(out, out),
+        in_specs=[pl.BlockSpec(memory_space=pltpu.SMEM), vmem],
+        out_specs=(vmem, vmem),
+        scratch_shapes=[pltpu.VMEM((LANES, LANES), home.dtype)],
+        compiler_params=pltpu.CompilerParams(vmem_limit_bytes=4 * 1024 * 1024),
+        cost_estimate=pl.CostEstimate(flops=PICK_FLOPS, bytes_accessed=0, transcendentals=0),
+        name="pick",
+    )(block_start, home)
+    return lse.T, mean.T
 
 
 def after_kernel(*refs):
@@ -117,15 +161,6 @@
     )(value, *tokens)
 
 
-def exact_parts(value):
-    parts = []
-    for _ in range(3):
-        top = lax.reduce_precision(value, 8, 7)
-        parts.append(top.astype(jnp.bfloat16))
-        value = value - top
-    return parts
-
-
 def score_kernel(
     spec_ref, x_hbm, own_hbm, q0_hbm, q1_hbm, q2_hbm, q3_hbm, bins_ref, shift_ref, ret_ref, m0_ref, m1_ref, m2_ref, m3_ref,
     x_ref, table_ref, extra_ref, small_ref, even_ref, odd_ref, held_ref, sum_ref, x_sem, table_sem, small_sem,
@@ -150,8 +185,15 @@
     ]
     parts = table_ref.shape[0] // part
     fetch(0).start()
-    for j in range(2 * PAIR):
+    for j in range(own):
         fetch_part(j).start()
+    fetch(1).start()
+    for j in range(own, parts):
+        fetch_part(j).start()
+    for copy in smalls:
+        copy.start()
+    for t in range(2, tiles):
+        fetch(t).start()
     sum_ref[...] = jnp.zeros_like(sum_ref)
     lane = lax.broadcasted_iota(jnp.int32, (SUB, LANES), 1)
     spot = lax.broadcasted_iota(jnp.int32, (SUB, LANES), 0)
@@ -219,16 +261,16 @@
             ret_ref[pl.ds(slot, 1), :] = jnp.sum(flat, axis=0, keepdims=True)
 
     fetch(0).wait()
-    for j in range(0, parts, PAIR):
+    for j in range(0, own, PAIR):
         for k in range(j, j + PAIR):
             fetch_part(k).wait()
-        for k in range(j + 2 * PAIR, min(j + 3 * PAIR, parts)):
-            fetch_part(k).start()
-        if j + 2 * PAIR == parts:
-            for copy in smalls:
-                copy.start()
-            for t in range(1, tiles):
-                fetch(t).start()
+        multiply(0, j // PAIR, even_ref, PAIR * part)
+    fetch(1).wait()
+    for j in range(0, own, PAIR):
+        multiply(1, j // PAIR, odd_ref, PAIR * part)
+    for j in range(own, parts, PAIR):
+        for k in range(j, j + PAIR):
+            fetch_part(k).wait()
         multiply(0, j // PAIR, even_ref, PAIR * part)
     small_ref[0:1, :own * part] = bins_ref[...]
     small_ref[1:2, :own * part] = shift_ref[...]
@@ -240,12 +282,14 @@
         small_ref[1:2, at] = extra[:, part:2 * part] + extra[:, 2 * part:3 * part] + extra[:, 3 * part:4 * part]
 
     for t in range(1, tiles + 1):
-        if t < tiles:
+        if 1 < t < tiles:
             fetch(t).wait()
         into, source = (even_ref, odd_ref) if t % 2 == 0 else (odd_ref, even_ref)
 
         def one_chunk(j, carry, t=t, into=into, source=source):
-            if t < tiles:
+            if t == 1:
+                multiply(t, own + j, into, part)
+            elif t < tiles:
                 multiply(t, j, into)
             reduce(t - 1, j, source)
             return carry
@@ -300,25 +344,23 @@
     back = [((i + 1) % owners, i) for i in range(owners)]
     forth = [(i, (i + 1) % owners) for i in range(owners)]
 
-    bins = (peptide_bin - lax.axis_index("mass") * BIN_DEV).astype(jnp.float32)
-    values = jnp.stack([bins.astype(jnp.bfloat16)] + exact_parts(peptide_shift)).reshape(4, specs, part)
-    extra = lax.dynamic_index_in_dim(values, spec, 1, False).reshape(1, 4 * part)
-    extra = jnp.pad(extra, ((0, SB - 1), (0, peptide_table.shape[1] - 4 * part)))
-    quarters = [lax.ppermute(cut_quarter(spec, peptide_table, extra, part), "mass", back)]
-    packed = pack_blocks(block_start, block_range, block_count, spectra, owners)
+    mass = lax.axis_index("mass")
+    packed, quarter = prepare(
+        spec, mass, block_start, block_range, block_count, peptide_bin, peptide_shift, spectra, peptide_table, owners, part
+    )
+    quarters = [lax.ppermute(quarter, "mass", back)]
     received = lax.all_to_all(packed, "mass", split_axis=0, concat_axis=0, tiled=True)
     for k in range(1, specs):
         quarters.append(lax.ppermute(quarters[0], "spec", [(i, (i + k) % specs) for i in range(specs)]))
     quarters[0] = after(*quarters, flops=GATE_FLOPS)
 
+    bins = (peptide_bin - mass * BIN_DEV).astype(jnp.float32)
     ret, *messages = score_blocks(
         spec, received.reshape(owners * SB, -1), peptide_table, quarters, bins[None], peptide_shift[None]
     )
 
-    chosen = block_start[:, None] == jnp.arange(owners, dtype=jnp.int32)[None, :]
     home = lax.all_to_all(ret, "mass", split_axis=0, concat_axis=0, tiled=True)
-    picked = jnp.sum(jnp.where(chosen[:, :, None], home[None, :, : 2 * SB], 0.0), axis=1)
-    lse, mean_shift = picked[:, :SB], picked[:, SB:]
+    lse, mean_shift = pick(block_start, home)
 
     total = messages[0]
     for k in range(1, specs):

time: 169 us -> 166 us (0.982)
  starting transfers between devices: 35.4 us -> 38.8 us
  local copies, waits for them, and re-layouts: 3.17 us -> 0.99 us
  Pallas kernels: 24.9 us -> 23.1 us
  other arithmetic: 3.55 us -> 1.85 us
    ppermute x3, waiting for transfers between devices: 38.1 us -> 23.5 us  [body(): lax.ppermute(quarters[0], 'spec', [(i, (i + k) % specs) for i in range(sp...]
    all_to_all x1, waiting for transfers between devices: 56.3 us -> 68.9 us  [body(): lax.all_to_all(packed, 'mass', split_axis=0, concat_axis=0, tiled=True)]
    all_to_all x1, starting transfers between devices: 9.65 us -> 13 us  [body(): home = lax.all_to_all(ret, 'mass', split_axis=0, concat_axis=0, tiled=True)]
  transfers between devices with their start and end apart: 10 -> 10, of which waited for: 6 -> 6; matrix products, arithmetic and copies ran while one was open for 1% -> 1% of each run, Pallas kernels for 2% -> 0%
where the time goes in v3:
time: 166 us
  waiting for transfers between devices  101 us (61%)
  starting transfers between devices  38.8 us (23%)
  Pallas kernels  23.1 us (14%)
  other arithmetic  1.85 us (1%)
    all_to_all x1, waiting for transfers between devices, body(): lax.all_to_all(packed, 'mass', split_axis=0, concat_axis=0, tiled=True)  68.9 us
    ppermute x3, waiting for transfers between devices, body(): lax.ppermute(quarters[0], 'spec', [(i, (i + k) % specs) for i in range(sp...  23.5 us
    pallas_call x1, Pallas kernels, score_blocks(): pl.pallas_call(score_kernel, out_shape=(jax.ShapeDtypeStruct((total // SB...  17.8 us
    all_to_all x1, starting transfers between devices, body(): home = lax.all_to_all(ret, 'mass', split_axis=0, concat_axis=0, tiled=True)  13 us
    all_to_all x1, starting transfers between devices, body(): lax.all_to_all(packed, 'mass', split_axis=0, concat_axis=0, tiled=True)  11.2 us
    all_to_all x1, waiting for transfers between devices, body(): home = lax.all_to_all(ret, 'mass', split_axis=0, concat_axis=0, tiled=True)  5.73 us
    ppermute x3, starting transfers between devices, body(): lax.ppermute(messages[k], 'spec', [(i, (i + specs - k) % specs) for i in...  4.86 us
    ppermute x3, starting transfers between devices, body(): lax.ppermute(quarters[0], 'spec', [(i, (i + k) % specs) for i in range(sp...  4.8 us
  transfers between devices with their start and end apart: 10, of which 6 were waited for; matrix products, arithmetic and copies ran while one was open for 1% of the time, Pallas kernels for 0%

profile of v3, /device:TPU:1, one launch (start us, length us, event | category | flops | bytes accessed | tf_op | source)
XLA Modules:
  0.0 166.1 jit_solution(6905599380308364704)
XLA Ops:
  0.6 4.1 %prepare.1 = (bf16[64,16,2176]{2,1,0:T(8,128)(2,1)}, bf16[272,2048]{1,0:T(8,128)(2,1)}) custom-call(s32[1]{0:T(128)} %bitcast.spec_ref, s32[1]{0:T(128)} %bitcast.1.mass_ref, s32[32]{0:T(128)} %start_ref.3, s32[2,32]{1,0:T(2,128)} %bitcast.22, s32[32]{0:T(128)} %count_ref.1, s32[1,1024]{1,0:T(1,128)} %bitcast.17, f32[1,1024]{1,0:T(1,128)} %bitcast.18, ...), custom_call_target="tpu_custom_call" | custom-call | tf_op jit(solution)/shard_map/prepare/pallas_call | solution.py:93
  4.7 3.3 %collective-permute-start = (bf16[272,2048]{1,0:T(8,128)(2,1)}, bf16[272,2048]{1,0:T(8,128)(2,1)S(1)}, u32[]{:S(2)}, u32[]{:S(2)}) collective-permute-start(bf16[272,2048]{1,0:T(8,128)(2,1)} %get-tuple-element.13), channel_id=1, source_target_pairs={{4,0},{8,4},{12,8},{16,12},{20,16},{24,20},{28,24},{32,28},{36,32}... | collective-permute-start | bytes 3342344 | tf_op jit(solution)/shard_map/ppermute | solution.py:351
  8.0 0.0 copy-start.1
  8.0 11.2 %all-to-all-start = ((bf16[64,16,2176]{2,1,0:T(8,128)(2,1)}), bf16[64,16,2176]{2,1,0:T(8,128)(2,1)}, u32[]{:S(2)}, u32[]{:S(2)}) async-start(bf16[64,16,2176]{2,1,0:T(8,128)(2,1)} %get-tuple-element.12), calls=%async_computation | async-start | bytes 8912896 | tf_op jit(solution)/shard_map/all_to_all | solution.py:352
  19.2 1.7 %collective-permute-done.refs_0_ = bf16[272,2048]{1,0:T(8,128)(2,1)S(1)} collective-permute-done((bf16[272,2048]{1,0:T(8,128)(2,1)}, bf16[272,2048]{1,0:T(8,128)(2,1)S(1)}, u32[]{:S(2)}, u32[]{:S(2)}) %collective-permute-start) | collective-permute-done | bytes 1114144 | tf_op jit(solution)/shard_map/ppermute | solution.py:351
  20.9 0.0 copy-start.2
  20.9 1.2 collective-permute-start.1
  22.1 2.5 %collective-permute-start.2 = (bf16[272,2048]{1,0:T(8,128)(2,1)S(1)}, bf16[272,2048]{1,0:T(8,128)(2,1)S(1)}, u32[]{:S(2)}, u32[]{:S(2)}) collective-permute-start(bf16[272,2048]{1,0:T(8,128)(2,1)S(1)} %collective-permute-done.refs_0_), channel_id=1, source_target_pairs={{0,2},{1,3},{2,0},{3,1},{4,6},{5,7},{6,4},{7,5},{8,10},{9,11},{10,... | collective-permute-start | bytes 3342344 | tf_op jit(solution)/shard_map/ppermute | solution.py:354
  24.6 1.1 collective-permute-start.3
  25.7 0.0 copy-done.1
  25.7 0.6 subtract_convert_fusion
  26.3 10.6 %collective-permute-done.1.refs_1_.q1_hbm = bf16[272,2048]{1,0:T(8,128)(2,1)S(1)} collective-permute-done((bf16[272,2048]{1,0:T(8,128)(2,1)S(1)}, bf16[272,2048]{1,0:T(8,128)(2,1)S(1)}, u32[]{:S(2)}, u32[]{:S(2)}) %collective-permute-start.1) | collective-permute-done | bytes 1114144 | tf_op jit(solution)/shard_map/ppermute | solution.py:354
  36.8 0.0 copy-start.3
  36.8 13.0 %collective-permute-done.2.refs_2_.q2_hbm = bf16[272,2048]{1,0:T(8,128)(2,1)S(1)} collective-permute-done((bf16[272,2048]{1,0:T(8,128)(2,1)S(1)}, bf16[272,2048]{1,0:T(8,128)(2,1)S(1)}, u32[]{:S(2)}, u32[]{:S(2)}) %collective-permute-start.2) | collective-permute-done | bytes 1114144 | tf_op jit(solution)/shard_map/ppermute | solution.py:354
  49.8 0.0 copy-start.4
  49.8 0.0 collective-permute-done.3.refs_3_.q3_hbm
  49.8 0.0 copy-done.2
  49.8 0.0 copy-done.3
  49.8 1.0 copy-done.4
  50.8 68.9 %all-to-all-done = bf16[64,16,2176]{2,1,0:T(8,128)(2,1)} async-done(((bf16[64,16,2176]{2,1,0:T(8,128)(2,1)}), bf16[64,16,2176]{2,1,0:T(8,128)(2,1)}, u32[]{:S(2)}, u32[]{:S(2)}) %all-to-all-start) | async-done | bytes 4456480 | tf_op jit(solution)/shard_map/all_to_all | solution.py:352
  119.7 0.0 copy-start
  119.7 17.8 %score_blocks.1 = (f32[64,128]{1,0:T(8,128)}, f32[2,256]{1,0:T(2,128)}, f32[2,256]{1,0:T(2,128)}, f32[2,256]{1,0:T(2,128)}, f32[2,256]{1,0:T(2,128)}) custom-call(s32[1]{0:T(128)} %bitcast.spec_ref, bf16[1024,2176]{1,0:T(8,128)(2,1)} %bitcast.5.x_hbm, bf16[1024,2048]{1,0:T(8,128)(2,1)} %own_hbm.1, bf16[272,2048]{1,0:T(8,128)(2,1)} %after.1.q0_hbm, ...), custom_call_target="tpu_custom_call" | custom-call | flops 8589934592 | bytes 12582912 | tf_op jit(solution)/shard_map/score_blocks/pallas_call | solution.py:310
  137.5 1.3 collective-permute-start.6
  138.9 2.4 %collective-permute-start.5 = (f32[2,256]{1,0:T(2,128)}, f32[2,256]{1,0:T(2,128)S(1)}, u32[]{:S(2)}, u32[]{:S(2)}) collective-permute-start(f32[2,256]{1,0:T(2,128)} %get-tuple-element.19), channel_id=1, source_target_pairs={{0,2},{1,3},{2,0},{3,1},{4,6},{5,7},{6,4},{7,5},{8,10},{9,11},{10,... | collective-permute-start | bytes 6152 | tf_op jit(solution)/shard_map/ppermute | solution.py:367
  141.3 1.1 collective-permute-start.4
  142.4 13.0 %all-to-all-start.1 = ((f32[64,1,128]{2,1,0:T(1,128)}), f32[64,1,128]{2,1,0:T(1,128)S(1)}, u32[]{:S(2)}, u32[]{:S(2)}) async-start(f32[64,1,128]{2,1,0:T(1,128)} %bitcast.16), calls=%async_computation.1 | async-start | bytes 65536 | tf_op jit(solution)/shard_map/all_to_all | solution.py:362
  155.5 0.0 collective-permute-done.6
  155.5 0.0 collective-permute-done.5
  155.5 0.0 collective-permute-done.4
  155.5 0.7 add_add_fusion
  156.2 1.6 collective-permute-start.7
  157.8 0.7 collective-permute-done.7
  158.6 0.6 add.15
  159.1 5.7 %all-to-all-done.1 = f32[64,1,128]{2,1,0:T(1,128)S(1)} async-done(((f32[64,1,128]{2,1,0:T(1,128)}), f32[64,1,128]{2,1,0:T(1,128)S(1)}, u32[]{:S(2)}, u32[]{:S(2)}) %all-to-all-start.1) | async-done | bytes 32800 | tf_op jit(solution)/shard_map/all_to_all | solution.py:362
  164.8 0.0 copy-done
  164.9 1.2 pick.1
  (2 shorter events, 0.0 us)
Async XLA Ops:
  4.7 16.2 %collective-permute-start = (bf16[272,2048]{1,0:T(8,128)(2,1)}, bf16[272,2048]{1,0:T(8,128)(2,1)S(1)}, u32[]{:S(2)}, u32[]{:S(2)}) collective-permute-start(bf16[272,2048]{1,0:T(8,128)(2,1)} %get-tuple-element.13), channel_id=1, source_target_pairs={{4,0},{8,4},{12,8},{16,12},{20,16},{24,20},{28,24},{32,28},{36,32}... | collective-permute-start | bytes 3342344 | tf_op jit(solution)/shard_map/ppermute | solution.py:351
  8.0 17.7 %copy-start.1 = (s32[1024]{0:T(1024)S(1)}, s32[1024]{0:T(1024)}, u32[]{:S(2)}) copy-start(s32[1024]{0:T(1024)} %param.12) | copy-start | bytes 12292
  8.0 111.7 %all-to-all-start = ((bf16[64,16,2176]{2,1,0:T(8,128)(2,1)}), bf16[64,16,2176]{2,1,0:T(8,128)(2,1)}, u32[]{:S(2)}, u32[]{:S(2)}) async-start(bf16[64,16,2176]{2,1,0:T(8,128)(2,1)} %get-tuple-element.12), calls=%async_computation | async-start | bytes 8912896 | tf_op jit(solution)/shard_map/all_to_all | solution.py:352
  20.9 29.0 %copy-start.2 = (bf16[272,2048]{1,0:T(8,128)(2,1)}, bf16[272,2048]{1,0:T(8,128)(2,1)S(1)}, u32[]{:S(2)}) copy-start(bf16[272,2048]{1,0:T(8,128)(2,1)S(1)} %collective-permute-done.refs_0_) | copy-start | bytes 3342340
  20.9 16.0 %collective-permute-start.1 = (bf16[272,2048]{1,0:T(8,128)(2,1)S(1)}, bf16[272,2048]{1,0:T(8,128)(2,1)S(1)}, u32[]{:S(2)}, u32[]{:S(2)}) collective-permute-start(bf16[272,2048]{1,0:T(8,128)(2,1)S(1)} %collective-permute-done.refs_0_), channel_id=1, source_target_pairs={{0,1},{1,2},{2,3},{3,0},{4,5},{5,6},{6,7},{7,4},{8,9},{9,10},{10,1... | collective-permute-start | bytes 3342344 | tf_op jit(solution)/shard_map/ppermute | solution.py:354
  22.1 27.8 %collective-permute-start.2 = (bf16[272,2048]{1,0:T(8,128)(2,1)S(1)}, bf16[272,2048]{1,0:T(8,128)(2,1)S(1)}, u32[]{:S(2)}, u32[]{:S(2)}) collective-permute-start(bf16[272,2048]{1,0:T(8,128)(2,1)S(1)} %collective-permute-done.refs_0_), channel_id=1, source_target_pairs={{0,2},{1,3},{2,0},{3,1},{4,6},{5,7},{6,4},{7,5},{8,10},{9,11},{10,... | collective-permute-start | bytes 3342344 | tf_op jit(solution)/shard_map/ppermute | solution.py:354
  24.6 25.2 %collective-permute-start.3 = (bf16[272,2048]{1,0:T(8,128)(2,1)S(1)}, bf16[272,2048]{1,0:T(8,128)(2,1)}, u32[]{:S(2)}, u32[]{:S(2)}) collective-permute-start(bf16[272,2048]{1,0:T(8,128)(2,1)S(1)} %collective-permute-done.refs_0_), channel_id=1, source_target_pairs={{0,3},{1,0},{2,1},{3,2},{4,7},{5,4},{6,5},{7,6},{8,11},{9,8},{10,9... | collective-permute-start | bytes 3342344 | tf_op jit(solution)/shard_map/ppermute | solution.py:354
  36.8 13.0 %copy-start.3 = (bf16[272,2048]{1,0:T(8,128)(2,1)}, bf16[272,2048]{1,0:T(8,128)(2,1)S(1)}, u32[]{:S(2)}) copy-start(bf16[272,2048]{1,0:T(8,128)(2,1)S(1)} %collective-permute-done.1.refs_1_.q1_hbm) | copy-start | bytes 3342340
  49.8 1.0 copy-start.4
  119.7 45.2 %copy-start = (s32[32]{0:T(128)S(1)}, s32[32]{0:T(128)}, u32[]{:S(2)}) copy-start(s32[32]{0:T(128)} %start_ref.3) | copy-start | bytes 388
  137.5 17.9 %collective-permute-start.6 = (f32[2,256]{1,0:T(2,128)}, f32[2,256]{1,0:T(2,128)S(1)}, u32[]{:S(2)}, u32[]{:S(2)}) collective-permute-start(f32[2,256]{1,0:T(2,128)} %get-tuple-element.20), channel_id=1, source_target_pairs={{0,1},{1,2},{2,3},{3,0},{4,5},{5,6},{6,7},{7,4},{8,9},{9,10},{10,1... | collective-permute-start | bytes 6152 | tf_op jit(solution)/shard_map/ppermute | solution.py:367
  138.9 16.6 %collective-permute-start.5 = (f32[2,256]{1,0:T(2,128)}, f32[2,256]{1,0:T(2,128)S(1)}, u32[]{:S(2)}, u32[]{:S(2)}) collective-permute-start(f32[2,256]{1,0:T(2,128)} %get-tuple-element.19), channel_id=1, source_target_pairs={{0,2},{1,3},{2,0},{3,1},{4,6},{5,7},{6,4},{7,5},{8,10},{9,11},{10,... | collective-permute-start | bytes 6152 | tf_op jit(solution)/shard_map/ppermute | solution.py:367
  141.3 14.2 %collective-permute-start.4 = (f32[2,256]{1,0:T(2,128)}, f32[2,256]{1,0:T(2,128)S(1)}, u32[]{:S(2)}, u32[]{:S(2)}) collective-permute-start(f32[2,256]{1,0:T(2,128)} %get-tuple-element.18), channel_id=1, source_target_pairs={{0,3},{1,0},{2,1},{3,2},{4,7},{5,4},{6,5},{7,6},{8,11},{9,8},{10,9... | collective-permute-start | bytes 6152 | tf_op jit(solution)/shard_map/ppermute | solution.py:367
  142.4 22.4 %all-to-all-start.1 = ((f32[64,1,128]{2,1,0:T(1,128)}), f32[64,1,128]{2,1,0:T(1,128)S(1)}, u32[]{:S(2)}, u32[]{:S(2)}) async-start(f32[64,1,128]{2,1,0:T(1,128)} %bitcast.16), calls=%async_computation.1 | async-start | bytes 65536 | tf_op jit(solution)/shard_map/all_to_all | solution.py:362
  156.2 2.4 %collective-permute-start.7 = (f32[256]{0:T(256)S(1)}, f32[256]{0:T(256)S(1)}, u32[]{:S(2)}, u32[]{:S(2)}) collective-permute-start(f32[256]{0:T(256)S(1)} %bitcast.23), channel_id=1, source_target_pairs={{0,4},{4,8},{8,12},{12,16},{16,20},{20,24},{24,28},{28,32},{32,36}... | collective-permute-start | bytes 3080 | tf_op jit(solution)/shard_map/ppermute | solution.py:368

commit v4 on v3

--- a/solution.py
+++ b/solution.py
@@ -162,7 +162,7 @@
 
 
 def score_kernel(
-    spec_ref, x_hbm, own_hbm, q0_hbm, q1_hbm, q2_hbm, q3_hbm, bins_ref, shift_ref, ret_ref, m0_ref, m1_ref, m2_ref, m3_ref,
+    spec_ref, x_hbm, own_hbm, q0_hbm, q1_hbm, q2_hbm, q3_hbm, bins_ref, shift_ref, ret_ref, mine_ref, next_ref,
     x_ref, table_ref, extra_ref, small_ref, even_ref, odd_ref, held_ref, sum_ref, x_sem, table_sem, small_sem,
 ):
     tiles = x_ref.shape[0]
@@ -295,10 +295,11 @@
             return carry
 
         lax.fori_loop(0, chunks, one_chunk, 0)
-    for k, m_ref in enumerate((m0_ref, m1_ref, m2_ref, m3_ref)):
-        mine = lax.rem(spec_ref[0] + own - k, own)
-        for h, at in enumerate((pl.ds(pl.multiple_of(mine * part, part), part), pl.ds((own + k) * part, part))):
-            m_ref[h:h + 1, :] = jnp.sum(sum_ref[:, at], axis=0, keepdims=True)
+    for k in range(own):
+        here, there = slice(k * part, (k + 1) * part), slice((own + k) * part, (own + k + 1) * part)
+        mine_ref[k:k + 1, :] = jnp.sum(sum_ref[:, here], axis=0, keepdims=True)
+        held_quarter = lax.rem(spec_ref[0] + own - k, own)
+        next_ref[pl.ds(held_quarter, 1), :] = jnp.sum(sum_ref[:, there], axis=0, keepdims=True)
 
 
 def score_blocks(spec, rows, table, quarters, bins, shifts):
@@ -312,9 +313,9 @@
         out_shape=(
             jax.ShapeDtypeStruct((total // SB, LANES), jnp.float32),
         )
-        + (jax.ShapeDtypeStruct((2, part), jnp.float32),) * len(quarters),
+        + (jax.ShapeDtypeStruct((len(quarters), part), jnp.float32),) * 2,
         in_specs=[pl.BlockSpec(memory_space=pltpu.SMEM)] + [hbm] * (2 + len(quarters)) + [vmem, vmem],
-        out_specs=(vmem,) * (1 + len(quarters)),
+        out_specs=(vmem,) * 3,
         scratch_shapes=[
             pltpu.VMEM((total // TILE, TILE, rows.shape[1]), rows.dtype),
             pltpu.VMEM((wide, width), table.dtype),
@@ -355,17 +356,15 @@
     quarters[0] = after(*quarters, flops=GATE_FLOPS)
 
     bins = (peptide_bin - mass * BIN_DEV).astype(jnp.float32)
-    ret, *messages = score_blocks(
+    ret, mine, after_mine = score_blocks(
         spec, received.reshape(owners * SB, -1), peptide_table, quarters, bins[None], peptide_shift[None]
     )
 
     home = lax.all_to_all(ret, "mass", split_axis=0, concat_axis=0, tiled=True)
     lse, mean_shift = pick(block_start, home)
 
-    total = messages[0]
-    for k in range(1, specs):
-        total = total + lax.ppermute(messages[k], "spec", [(i, (i + specs - k) % specs) for i in range(specs)])
-    support = total[0] + lax.ppermute(total[1], "mass", forth)
+    total = mine + lax.ppermute(after_mine, "mass", forth)
+    support = lax.dynamic_index_in_dim(lax.psum(total, "spec"), spec, 0, False)
     return (lse, mean_shift, support)
 
 

time: 166 us -> 162 us (0.976)
  blocking collectives: 0 us -> 8.98 us
  starting transfers between devices: 38.8 us -> 31.6 us
  waiting for transfers between devices: 101 us -> 94 us
    psum x0 -> x1, blocking collectives: none -> 8.98 us  [body(): support = lax.dynamic_index_in_dim(lax.psum(total, 'spec'), spec, 0, False)]
    all_to_all x1, waiting for transfers between devices: 5.73 us -> 0.01 us  [body(): home = lax.all_to_all(ret, 'mass', split_axis=0, concat_axis=0, tiled=True)]
    all_to_all x1, starting transfers between devices: 13 us -> 9.16 us  [body(): home = lax.all_to_all(ret, 'mass', split_axis=0, concat_axis=0, tiled=True)]
    ppermute x4 -> x1, starting transfers between devices: 6.49 us -> 3.07 us  [body(): total = mine + lax.ppermute(after_mine, 'mass', forth)]
  transfers between devices with their start and end apart: 10 -> 7, of which waited for: 6 -> 4; matrix products, arithmetic and copies ran while one was open for 1% -> 1% of each run, Pallas kernels for 0% -> 0%
where the time goes in v4:
time: 162 us; the launch traced here: 161 us
  waiting for transfers between devices  94 us (58%)
  starting transfers between devices  31.6 us (20%)
  Pallas kernels  23.2 us (14%)
  blocking collectives  8.98 us (6%)
    all_to_all x1, waiting for transfers between devices, body(): lax.all_to_all(packed, 'mass', split_axis=0, concat_axis=0, tiled=True)  68.8 us
    ppermute x3, waiting for transfers between devices, body(): lax.ppermute(quarters[0], 'spec', [(i, (i + k) % specs) for i in range(sp...  23.5 us
    pallas_call x1, Pallas kernels, score_blocks(): pl.pallas_call(score_kernel, out_shape=(jax.ShapeDtypeStruct((total // SB...  17.8 us
    all_to_all x1, starting transfers between devices, body(): lax.all_to_all(packed, 'mass', split_axis=0, concat_axis=0, tiled=True)  11.1 us
    all_to_all x1, starting transfers between devices, body(): home = lax.all_to_all(ret, 'mass', split_axis=0, concat_axis=0, tiled=True)  9.16 us
    psum x1, blocking collectives, body(): support = lax.dynamic_index_in_dim(lax.psum(total, 'spec'), spec, 0, False)  8.98 us
    ppermute x3, starting transfers between devices, body(): lax.ppermute(quarters[0], 'spec', [(i, (i + k) % specs) for i in range(sp...  4.92 us
    pallas_call x1, Pallas kernels, prepare(): pl.pallas_call(prepare_kernel, out_shape=(jax.ShapeDtypeStruct((owners, r...  4.1 us
  transfers between devices with their start and end apart: 7, of which 4 were waited for; matrix products, arithmetic and copies ran while one was open for 1% of the time, Pallas kernels for 0%

profile of v4, /device:TPU:1, one launch (start us, length us, event | category | flops | bytes accessed | tf_op | source)
XLA Modules:
  0.0 161.3 jit_solution(399218109958727946)
XLA Ops:
  0.6 4.1 %prepare.1 = (bf16[64,16,2176]{2,1,0:T(8,128)(2,1)}, bf16[272,2048]{1,0:T(8,128)(2,1)}) custom-call(s32[1]{0:T(128)} %bitcast.spec_ref, s32[1]{0:T(128)} %bitcast.1.mass_ref, s32[32]{0:T(128)} %start_ref.3, s32[2,32]{1,0:T(2,128)} %bitcast.20, s32[32]{0:T(128)} %count_ref.1, s32[1,1024]{1,0:T(1,128)} %bitcast.16, f32[1,1024]{1,0:T(1,128)} %bitcast.17, ...), custom_call_target="tpu_custom_call" | custom-call | tf_op jit(solution)/shard_map/prepare/pallas_call | solution.py:93
  4.7 3.3 %collective-permute-start = (bf16[272,2048]{1,0:T(8,128)(2,1)}, bf16[272,2048]{1,0:T(8,128)(2,1)S(1)}, u32[]{:S(2)}, u32[]{:S(2)}) collective-permute-start(bf16[272,2048]{1,0:T(8,128)(2,1)} %get-tuple-element.11), channel_id=1, source_target_pairs={{4,0},{8,4},{12,8},{16,12},{20,16},{24,20},{28,24},{32,28},{36,32}... | collective-permute-start | bytes 3342344 | tf_op jit(solution)/shard_map/ppermute | solution.py:352
  8.1 0.0 copy-start.1
  8.1 11.1 %all-to-all-start = ((bf16[64,16,2176]{2,1,0:T(8,128)(2,1)}), bf16[64,16,2176]{2,1,0:T(8,128)(2,1)}, u32[]{:S(2)}, u32[]{:S(2)}) async-start(bf16[64,16,2176]{2,1,0:T(8,128)(2,1)} %get-tuple-element.10), calls=%async_computation | async-start | bytes 8912896 | tf_op jit(solution)/shard_map/all_to_all | solution.py:353
  19.2 1.7 %collective-permute-done.refs_0_ = bf16[272,2048]{1,0:T(8,128)(2,1)S(1)} collective-permute-done((bf16[272,2048]{1,0:T(8,128)(2,1)}, bf16[272,2048]{1,0:T(8,128)(2,1)S(1)}, u32[]{:S(2)}, u32[]{:S(2)}) %collective-permute-start) | collective-permute-done | bytes 1114144 | tf_op jit(solution)/shard_map/ppermute | solution.py:352
  20.8 0.0 copy-start.2
  20.8 1.3 collective-permute-start.1
  22.1 2.5 %collective-permute-start.2 = (bf16[272,2048]{1,0:T(8,128)(2,1)S(1)}, bf16[272,2048]{1,0:T(8,128)(2,1)S(1)}, u32[]{:S(2)}, u32[]{:S(2)}) collective-permute-start(bf16[272,2048]{1,0:T(8,128)(2,1)S(1)} %collective-permute-done.refs_0_), channel_id=1, source_target_pairs={{0,2},{1,3},{2,0},{3,1},{4,6},{5,7},{6,4},{7,5},{8,10},{9,11},{10,... | collective-permute-start | bytes 3342344 | tf_op jit(solution)/shard_map/ppermute | solution.py:355
  24.6 1.1 collective-permute-start.3
  25.8 0.0 copy-done.1
  25.8 0.6 subtract_convert_fusion
  26.4 10.4 %collective-permute-done.1.refs_1_.q1_hbm = bf16[272,2048]{1,0:T(8,128)(2,1)S(1)} collective-permute-done((bf16[272,2048]{1,0:T(8,128)(2,1)S(1)}, bf16[272,2048]{1,0:T(8,128)(2,1)S(1)}, u32[]{:S(2)}, u32[]{:S(2)}) %collective-permute-start.1) | collective-permute-done | bytes 1114144 | tf_op jit(solution)/shard_map/ppermute | solution.py:355
  36.8 0.0 copy-start.3
  36.8 13.0 %collective-permute-done.2.refs_2_.q2_hbm = bf16[272,2048]{1,0:T(8,128)(2,1)S(1)} collective-permute-done((bf16[272,2048]{1,0:T(8,128)(2,1)S(1)}, bf16[272,2048]{1,0:T(8,128)(2,1)S(1)}, u32[]{:S(2)}, u32[]{:S(2)}) %collective-permute-start.2) | collective-permute-done | bytes 1114144 | tf_op jit(solution)/shard_map/ppermute | solution.py:355
  49.9 0.0 copy-start.4
  49.9 0.0 collective-permute-done.3.refs_3_.q3_hbm
  49.9 0.0 copy-done.2
  49.9 0.0 copy-done.3
  49.9 1.0 copy-done.4
  50.8 68.8 %all-to-all-done = bf16[64,16,2176]{2,1,0:T(8,128)(2,1)} async-done(((bf16[64,16,2176]{2,1,0:T(8,128)(2,1)}), bf16[64,16,2176]{2,1,0:T(8,128)(2,1)}, u32[]{:S(2)}, u32[]{:S(2)}) %all-to-all-start) | async-done | bytes 4456480 | tf_op jit(solution)/shard_map/all_to_all | solution.py:353
  119.7 0.0 copy-start
  119.7 17.8 %score_blocks.1 = (f32[64,128]{1,0:T(8,128)}, f32[4,256]{1,0:T(4,128)}, f32[4,256]{1,0:T(4,128)}) custom-call(s32[1]{0:T(128)} %bitcast.spec_ref, bf16[1024,2176]{1,0:T(8,128)(2,1)} %bitcast.5.x_hbm, bf16[1024,2048]{1,0:T(8,128)(2,1)} %own_hbm.1, bf16[272,2048]{1,0:T(8,128)(2,1)} %after.1.q0_hbm, bf16[272,2048]{1,0:T(8,128)(2,1)} %copy-done.3, ...), custom_call_target="tpu_custom_call" | custom-call | flops 8589934592 | bytes 12582912 | tf_op jit(solution)/shard_map/score_blocks/pallas_call | solution.py:311
  137.5 3.1 %collective-permute-start.4 = (f32[4,256]{1,0:T(4,128)}, f32[4,256]{1,0:T(4,128)S(1)}, u32[]{:S(2)}, u32[]{:S(2)}) collective-permute-start(f32[4,256]{1,0:T(4,128)} %get-tuple-element.16), channel_id=1, source_target_pairs={{0,4},{4,8},{8,12},{12,16},{16,20},{20,24},{24,28},{28,32},{32,36}... | collective-permute-start | bytes 12296 | tf_op jit(solution)/shard_map/ppermute | solution.py:366
  140.6 9.2 %all-to-all-start.1 = ((f32[64,1,128]{2,1,0:T(1,128)}), f32[64,1,128]{2,1,0:T(1,128)S(1)}, u32[]{:S(2)}, u32[]{:S(2)}) async-start(f32[64,1,128]{2,1,0:T(1,128)} %bitcast.15), calls=%async_computation.1 | async-start | bytes 65536 | tf_op jit(solution)/shard_map/all_to_all | solution.py:363
  149.8 0.0 collective-permute-done.4
  149.8 0.7 add.9
  150.5 9.0 %psum.7 = f32[4,256]{1,0:T(4,128)S(1)} all-reduce(f32[4,256]{1,0:T(4,128)S(1)} %add.9), channel_id=1, replica_groups=mesh['mass'=64,'spec'=4] {'spec'}, use_global_device_ids=true, to_apply=%region_0.0 | all-reduce | flops 1024 | bytes 8192 | tf_op jit(solution)/shard_map/psum | solution.py:367
  159.5 0.6 constant_dynamic-slice_fusion
  160.0 0.0 all-to-all-done.1
  160.0 0.0 copy-done
  160.0 1.2 pick.1
  (1 shorter events, 0.0 us)
Async XLA Ops:
  4.7 16.1 %collective-permute-start = (bf16[272,2048]{1,0:T(8,128)(2,1)}, bf16[272,2048]{1,0:T(8,128)(2,1)S(1)}, u32[]{:S(2)}, u32[]{:S(2)}) collective-permute-start(bf16[272,2048]{1,0:T(8,128)(2,1)} %get-tuple-element.11), channel_id=1, source_target_pairs={{4,0},{8,4},{12,8},{16,12},{20,16},{24,20},{28,24},{32,28},{36,32}... | collective-permute-start | bytes 3342344 | tf_op jit(solution)/shard_map/ppermute | solution.py:352
  8.1 17.7 %copy-start.1 = (s32[1024]{0:T(1024)S(1)}, s32[1024]{0:T(1024)}, u32[]{:S(2)}) copy-start(s32[1024]{0:T(1024)} %param.12) | copy-start | bytes 12292
  8.1 111.6 %all-to-all-start = ((bf16[64,16,2176]{2,1,0:T(8,128)(2,1)}), bf16[64,16,2176]{2,1,0:T(8,128)(2,1)}, u32[]{:S(2)}, u32[]{:S(2)}) async-start(bf16[64,16,2176]{2,1,0:T(8,128)(2,1)} %get-tuple-element.10), calls=%async_computation | async-start | bytes 8912896 | tf_op jit(solution)/shard_map/all_to_all | solution.py:353
  20.8 29.0 %copy-start.2 = (bf16[272,2048]{1,0:T(8,128)(2,1)}, bf16[272,2048]{1,0:T(8,128)(2,1)S(1)}, u32[]{:S(2)}) copy-start(bf16[272,2048]{1,0:T(8,128)(2,1)S(1)} %collective-permute-done.refs_0_) | copy-start | bytes 3342340
  20.8 16.0 %collective-permute-start.1 = (bf16[272,2048]{1,0:T(8,128)(2,1)S(1)}, bf16[272,2048]{1,0:T(8,128)(2,1)S(1)}, u32[]{:S(2)}, u32[]{:S(2)}) collective-permute-start(bf16[272,2048]{1,0:T(8,128)(2,1)S(1)} %collective-permute-done.refs_0_), channel_id=1, source_target_pairs={{0,1},{1,2},{2,3},{3,0},{4,5},{5,6},{6,7},{7,4},{8,9},{9,10},{10,1... | collective-permute-start | bytes 3342344 | tf_op jit(solution)/shard_map/ppermute | solution.py:355
  22.1 27.7 %collective-permute-start.2 = (bf16[272,2048]{1,0:T(8,128)(2,1)S(1)}, bf16[272,2048]{1,0:T(8,128)(2,1)S(1)}, u32[]{:S(2)}, u32[]{:S(2)}) collective-permute-start(bf16[272,2048]{1,0:T(8,128)(2,1)S(1)} %collective-permute-done.refs_0_), channel_id=1, source_target_pairs={{0,2},{1,3},{2,0},{3,1},{4,6},{5,7},{6,4},{7,5},{8,10},{9,11},{10,... | collective-permute-start | bytes 3342344 | tf_op jit(solution)/shard_map/ppermute | solution.py:355
  24.6 25.2 %collective-permute-start.3 = (bf16[272,2048]{1,0:T(8,128)(2,1)S(1)}, bf16[272,2048]{1,0:T(8,128)(2,1)}, u32[]{:S(2)}, u32[]{:S(2)}) collective-permute-start(bf16[272,2048]{1,0:T(8,128)(2,1)S(1)} %collective-permute-done.refs_0_), channel_id=1, source_target_pairs={{0,3},{1,0},{2,1},{3,2},{4,7},{5,4},{6,5},{7,6},{8,11},{9,8},{10,9... | collective-permute-start | bytes 3342344 | tf_op jit(solution)/shard_map/ppermute | solution.py:355
  36.8 13.1 %copy-start.3 = (bf16[272,2048]{1,0:T(8,128)(2,1)}, bf16[272,2048]{1,0:T(8,128)(2,1)S(1)}, u32[]{:S(2)}) copy-start(bf16[272,2048]{1,0:T(8,128)(2,1)S(1)} %collective-permute-done.1.refs_1_.q1_hbm) | copy-start | bytes 3342340
  49.9 1.0 copy-start.4
  119.7 40.3 %copy-start = (s32[32]{0:T(128)S(1)}, s32[32]{0:T(128)}, u32[]{:S(2)}) copy-start(s32[32]{0:T(128)} %start_ref.3) | copy-start | bytes 388
  137.5 12.2 %collective-permute-start.4 = (f32[4,256]{1,0:T(4,128)}, f32[4,256]{1,0:T(4,128)S(1)}, u32[]{:S(2)}, u32[]{:S(2)}) collective-permute-start(f32[4,256]{1,0:T(4,128)} %get-tuple-element.16), channel_id=1, source_target_pairs={{0,4},{4,8},{8,12},{12,16},{16,20},{20,24},{24,28},{28,32},{32,36}... | collective-permute-start | bytes 12296 | tf_op jit(solution)/shard_map/ppermute | solution.py:366
  140.6 19.4 %all-to-all-start.1 = ((f32[64,1,128]{2,1,0:T(1,128)}), f32[64,1,128]{2,1,0:T(1,128)S(1)}, u32[]{:S(2)}, u32[]{:S(2)}) async-start(f32[64,1,128]{2,1,0:T(1,128)} %bitcast.15), calls=%async_computation.1 | async-start | bytes 65536 | tf_op jit(solution)/shard_map/all_to_all | solution.py:363

commit v5 on v4

--- a/solution.py
+++ b/solution.py
@@ -19,35 +19,21 @@
 SUB = 8
 
 
-def prepare_kernel(
-    spec_ref, mass_ref, start_ref, range_ref, count_ref, bins_ref, shift_ref, spectra_hbm, table_hbm,
-    out_hbm, quarter_hbm, held, meta_ref, part_ref, extra_ref, load_sem, part_sem, sem, tail_sem,
-):
-    blocks, rows, width = held.shape
-    steps = load_sem.shape[0]
-    batch, part = blocks // steps, part_ref.shape[0]
+def cut_kernel(spec_ref, mass_ref, bins_ref, shift_ref, table_hbm, quarter_hbm, part_ref, extra_ref, load_sem, store_sem, sem):
+    steps, part = load_sem.shape[0], part_ref.shape[0]
     piece = part // steps
     first = pl.multiple_of(spec_ref[0] * part, part)
 
     def load(j):
-        at = pl.ds(j * batch, batch)
-        return pltpu.make_async_copy(spectra_hbm.at[at], held.at[at], load_sem.at[j])
-
-    def copy(i):
-        return pltpu.make_async_copy(held.at[i], out_hbm.at[start_ref[i], :, pl.ds(0, width)], sem.at[i])
-
-    def load_part(j):
         at = pl.ds(j * piece, piece)
-        return pltpu.make_async_copy(table_hbm.at[pl.ds(first + j * piece, piece)], part_ref.at[at], part_sem.at[j])
-
-    def store_part(j):
+        return pltpu.make_async_copy(table_hbm.at[pl.ds(first + j * piece, piece)], part_ref.at[at], load_sem.at[j])
+
+    def store(j):
         at = pl.ds(j * piece, piece)
-        return pltpu.make_async_copy(part_ref.at[at], quarter_hbm.at[at], part_sem.at[steps + j])
+        return pltpu.make_async_copy(part_ref.at[at], quarter_hbm.at[at], store_sem.at[j])
 
     for j in range(steps):
         load(j).start()
-        load_part(j).start()
-
     bins = (bins_ref[0:1, pl.ds(first, part)] - mass_ref[0] * BIN_DEV).astype(jnp.float32)
     rest = shift_ref[0:1, pl.ds(first, part)]
     extra_ref[...] = jnp.zeros_like(extra_ref)
@@ -56,9 +42,52 @@
         top = jnp.broadcast_to(rest, (SB, part)).astype(extra_ref.dtype)
         extra_ref[:, k * part:(k + 1) * part] = top
         rest = rest - top.astype(jnp.float32)[0:1]
-    extra_copy = pltpu.make_async_copy(extra_ref, quarter_hbm.at[pl.ds(part, SB)], tail_sem.at[0])
+    extra_copy = pltpu.make_async_copy(extra_ref, quarter_hbm.at[pl.ds(part, SB)], sem)
     extra_copy.start()
-
+    for j in range(steps):
+        load(j).wait()
+        store(j).start()
+    for j in range(steps):
+        store(j).wait()
+    extra_copy.wait()
+
+
+def cut_quarter(spec, mass, bins, shifts, table, part):
+    width = table.shape[1]
+    smem = pl.BlockSpec(memory_space=pltpu.SMEM)
+    vmem = pl.BlockSpec(memory_space=pltpu.VMEM)
+    hbm = pl.BlockSpec(memory_space=pltpu.HBM)
+    steps = 4
+    return pl.pallas_call(
+        cut_kernel,
+        out_shape=jax.ShapeDtypeStruct((part + SB, width), table.dtype),
+        in_specs=[smem, smem, vmem, vmem, hbm],
+        out_specs=hbm,
+        scratch_shapes=[
+            pltpu.VMEM((part, width), table.dtype),
+            pltpu.VMEM((SB, width), table.dtype),
+            pltpu.SemaphoreType.DMA((steps,)),
+            pltpu.SemaphoreType.DMA((steps,)),
+            pltpu.SemaphoreType.DMA,
+        ],
+        compiler_params=pltpu.CompilerParams(vmem_limit_bytes=WHOLE_VMEM),
+        name="cut_quarter",
+    )(spec.reshape(1), mass.reshape(1), bins[None], shifts[None], table)
+
+
+def pack_kernel(start_ref, range_ref, count_ref, spectra_hbm, out_hbm, held, meta_ref, load_sem, sem, meta_sem):
+    blocks, rows, width = held.shape
+    batch = blocks // load_sem.shape[0]
+
+    def load(j):
+        at = pl.ds(j * batch, batch)
+        return pltpu.make_async_copy(spectra_hbm.at[at], held.at[at], load_sem.at[j])
+
+    def copy(i):
+        return pltpu.make_async_copy(held.at[i], out_hbm.at[start_ref[i], :, pl.ds(0, width)], sem.at[i])
+
+    for j in range(blocks // batch):
+        load(j).start()
     meta_ref[...] = jnp.zeros_like(meta_ref)
     row = lax.broadcasted_iota(jnp.int32, (rows, LANES), 0)
     lane = lax.broadcasted_iota(jnp.int32, (rows, LANES), 1)
@@ -68,52 +97,36 @@
         ends = range_ref[1, i] - low + 1
         value = jnp.where(lane == 0, lower, jnp.where((lane == 1) & (row < count_ref[i]), ends, 0))
         meta_ref[start_ref[i]] = value.astype(jnp.float32).astype(meta_ref.dtype)
-    meta_copy = pltpu.make_async_copy(meta_ref, out_hbm.at[:, :, pl.ds(width, LANES)], tail_sem.at[1])
+    meta_copy = pltpu.make_async_copy(meta_ref, out_hbm.at[:, :, pl.ds(width, LANES)], meta_sem)
     meta_copy.start()
-    for j in range(steps):
+    for j in range(blocks // batch):
         load(j).wait()
         for i in range(j * batch, (j + 1) * batch):
             copy(i).start()
-        load_part(j).wait()
-        store_part(j).start()
     for i in range(blocks):
         copy(i).wait()
-    for j in range(steps):
-        store_part(j).wait()
-    extra_copy.wait()
     meta_copy.wait()
 
 
-def prepare(spec, mass, block_start, block_range, block_count, bins, shifts, spectra, table, owners, part):
+def pack_blocks(block_start, block_range, block_count, spectra, owners):
     blocks, rows, width = spectra.shape
     smem = pl.BlockSpec(memory_space=pltpu.SMEM)
-    vmem = pl.BlockSpec(memory_space=pltpu.VMEM)
     hbm = pl.BlockSpec(memory_space=pltpu.HBM)
-    steps = 4
     return pl.pallas_call(
-        prepare_kernel,
-        out_shape=(
-            jax.ShapeDtypeStruct((owners, rows, width + LANES), spectra.dtype),
-            jax.ShapeDtypeStruct((part + SB, width), table.dtype),
-        ),
-        in_specs=[smem] * 5 + [vmem] * 2 + [hbm] * 2,
-        out_specs=(hbm, hbm),
+        pack_kernel,
+        out_shape=jax.ShapeDtypeStruct((owners, rows, width + LANES), spectra.dtype),
+        in_specs=[smem, smem, smem, hbm],
+        out_specs=hbm,
         scratch_shapes=[
             pltpu.VMEM((blocks, rows, width), spectra.dtype),
             pltpu.VMEM((owners, rows, LANES), spectra.dtype),
-            pltpu.VMEM((part, width), table.dtype),
-            pltpu.VMEM((SB, width), table.dtype),
-            pltpu.SemaphoreType.DMA((steps,)),
-            pltpu.SemaphoreType.DMA((2 * steps,)),
+            pltpu.SemaphoreType.DMA((4,)),
             pltpu.SemaphoreType.DMA((blocks,)),
-            pltpu.SemaphoreType.DMA((2,)),
+            pltpu.SemaphoreType.DMA,
         ],
         compiler_params=pltpu.CompilerParams(vmem_limit_bytes=WHOLE_VMEM),
-        name="prepare",
-    )(
-        spec.reshape(1), mass.reshape(1), block_start, block_range.T, block_count, bins[None], shifts[None],
-        spectra, table,
-    )
+        name="pack_blocks",
+    )(block_start, block_range.T, block_count, spectra)
 
 
 def pick_kernel(start_ref, home_ref, lse_ref, mean_ref, rows_ref):
@@ -346,10 +359,9 @@
     forth = [(i, (i + 1) % owners) for i in range(owners)]
 
     mass = lax.axis_index("mass")
-    packed, quarter = prepare(
-        spec, mass, block_start, block_range, block_count, peptide_bin, peptide_shift, spectra, peptide_table, owners, part
-    )
+    quarter = cut_quarter(spec, mass, peptide_bin, peptide_shift, peptide_table, part)
     quarters = [lax.ppermute(quarter, "mass", back)]
+    packed = pack_blocks(block_start, block_range, block_count, spectra, owners)
     received = lax.all_to_all(packed, "mass", split_axis=0, concat_axis=0, tiled=True)
     for k in range(1, specs):
         quarters.append(lax.ppermute(quarters[0], "spec", [(i, (i + k) % specs) for i in range(specs)]))

time: 162 us -> 161 us (level)
  starting transfers between devices: 31.6 us -> 28.5 us
  Pallas kernels: 23.2 us -> 25.4 us
    ppermute x3, waiting for transfers between devices: 23.5 us -> 37.5 us  [body(): lax.ppermute(quarters[0], 'spec', [(i, (i + k) % specs) for i in range(sp...]
    all_to_all x1, waiting for transfers between devices: 68.8 us -> 57.3 us  [body(): lax.all_to_all(packed, 'mass', split_axis=0, concat_axis=0, tiled=True)]
    all_to_all x1, starting transfers between devices: 9.16 us -> 5.91 us  [body(): home = lax.all_to_all(ret, 'mass', split_axis=0, concat_axis=0, tiled=True)]
    pallas_call x1 -> x2, Pallas kernels: 4.1 us -> 6.32 us  [the longest x1 3.58 us: pack_blocks(): pl.pallas_call(pack_kernel, out_shape=jax.ShapeDtypeStruct((owners, rows,...]
    ppermute x1, waiting for transfers between devices: 1.66 us -> 0.01 us  [body(): quarters = [lax.ppermute(quarter, 'mass', back)]]
  transfers between devices with their start and end apart: 7 -> 7, of which waited for: 4 -> 4; matrix products, arithmetic and copies ran while one was open for 1% -> 1% of each run, Pallas kernels for 0% -> 2%
where the time goes in v5:
time: 161 us; the launch traced here: 160 us
  waiting for transfers between devices  94.8 us (59%)
  starting transfers between devices  28.5 us (18%)
  Pallas kernels  25.4 us (16%)
  blocking collectives  8.75 us (5%)
    all_to_all x1, waiting for transfers between devices, body(): lax.all_to_all(packed, 'mass', split_axis=0, concat_axis=0, tiled=True)  57.3 us
    ppermute x3, waiting for transfers between devices, body(): lax.ppermute(quarters[0], 'spec', [(i, (i + k) % specs) for i in range(sp...  37.5 us
    pallas_call x1, Pallas kernels, score_blocks(): pl.pallas_call(score_kernel, out_shape=(jax.ShapeDtypeStruct((total // SB...  17.8 us
    all_to_all x1, starting transfers between devices, body(): lax.all_to_all(packed, 'mass', split_axis=0, concat_axis=0, tiled=True)  11.1 us
    psum x1, blocking collectives, body(): support = lax.dynamic_index_in_dim(lax.psum(total, 'spec'), spec, 0, False)  8.75 us
    all_to_all x1, starting transfers between devices, body(): home = lax.all_to_all(ret, 'mass', split_axis=0, concat_axis=0, tiled=True)  5.91 us
    ppermute x3, starting transfers between devices, body(): lax.ppermute(quarters[0], 'spec', [(i, (i + k) % specs) for i in range(sp...  4.87 us
    pallas_call x1, Pallas kernels, pack_blocks(): pl.pallas_call(pack_kernel, out_shape=jax.ShapeDtypeStruct((owners, rows,...  3.58 us
  transfers between devices with their start and end apart: 7, of which 4 were waited for; matrix products, arithmetic and copies ran while one was open for 1% of the time, Pallas kernels for 2%

profile of v5, /device:TPU:1, one launch (start us, length us, event | category | flops | bytes accessed | tf_op | source)
XLA Modules:
  0.0 160.0 jit_solution(16837576367415152061)
XLA Ops:
  0.6 2.7 %cut_quarter.1 = bf16[272,2048]{1,0:T(8,128)(2,1)} custom-call(s32[1]{0:T(128)} %bitcast.spec_ref, s32[1]{0:T(128)} %bitcast.3.mass_ref, s32[1,1024]{1,0:T(1,128)} %bitcast.16, f32[1,1024]{1,0:T(1,128)} %bitcast.18, bf16[1024,2048]{1,0:T(8,128)(2,1)} %own_hbm.1), custom_call_target="tpu_custom_call" | custom-call | tf_op jit(solution)/shard_map/cut_quarter/pallas_call | solution.py:61
  3.4 3.3 %collective-permute-start = (bf16[272,2048]{1,0:T(8,128)(2,1)}, bf16[272,2048]{1,0:T(8,128)(2,1)S(1)}, u32[]{:S(2)}, u32[]{:S(2)}) collective-permute-start(bf16[272,2048]{1,0:T(8,128)(2,1)} %cut_quarter.1), channel_id=1, source_target_pairs={{4,0},{8,4},{12,8},{16,12},{20,16},{24,20},{28,24},{32,28},{36,32}... | collective-permute-start | bytes 3342344 | tf_op jit(solution)/shard_map/ppermute | solution.py:363
  6.7 3.6 %pack_blocks.1 = bf16[64,16,2176]{2,1,0:T(8,128)(2,1)} custom-call(s32[32]{0:T(128)} %start_ref.3, s32[2,32]{1,0:T(2,128)} %bitcast.20, s32[32]{0:T(128)} %count_ref.1, bf16[32,16,2048]{2,1,0:T(8,128)(2,1)} %spectra_hbm.1), custom_call_target="tpu_custom_call" | custom-call | tf_op jit(solution)/shard_map/pack_blocks/pallas_call | solution.py:115
  10.3 0.0 copy-start.1
  10.3 11.1 %all-to-all-start = ((bf16[64,16,2176]{2,1,0:T(8,128)(2,1)}), bf16[64,16,2176]{2,1,0:T(8,128)(2,1)}, u32[]{:S(2)}, u32[]{:S(2)}) async-start(bf16[64,16,2176]{2,1,0:T(8,128)(2,1)} %pack_blocks.1), calls=%async_computation | async-start | bytes 8912896 | tf_op jit(solution)/shard_map/all_to_all | solution.py:365
  21.4 0.0 collective-permute-done.refs_0_
  21.4 0.0 copy-start.2
  21.4 1.2 collective-permute-start.1
  22.7 2.5 %collective-permute-start.2 = (bf16[272,2048]{1,0:T(8,128)(2,1)S(1)}, bf16[272,2048]{1,0:T(8,128)(2,1)S(1)}, u32[]{:S(2)}, u32[]{:S(2)}) collective-permute-start(bf16[272,2048]{1,0:T(8,128)(2,1)S(1)} %collective-permute-done.refs_0_), channel_id=1, source_target_pairs={{0,2},{1,3},{2,0},{3,1},{4,6},{5,7},{6,4},{7,5},{8,10},{9,11},{10,... | collective-permute-start | bytes 3342344 | tf_op jit(solution)/shard_map/ppermute | solution.py:367
  25.1 1.2 collective-permute-start.3
  26.3 0.0 copy-done.1
  26.3 0.6 subtract_convert_fusion
  26.9 10.6 %collective-permute-done.1.refs_1_.q1_hbm = bf16[272,2048]{1,0:T(8,128)(2,1)S(1)} collective-permute-done((bf16[272,2048]{1,0:T(8,128)(2,1)S(1)}, bf16[272,2048]{1,0:T(8,128)(2,1)S(1)}, u32[]{:S(2)}, u32[]{:S(2)}) %collective-permute-start.1) | collective-permute-done | bytes 1114144 | tf_op jit(solution)/shard_map/ppermute | solution.py:367
  37.5 0.0 copy-start.3
  37.5 17.8 %collective-permute-done.2.refs_2_.q2_hbm = bf16[272,2048]{1,0:T(8,128)(2,1)S(1)} collective-permute-done((bf16[272,2048]{1,0:T(8,128)(2,1)S(1)}, bf16[272,2048]{1,0:T(8,128)(2,1)S(1)}, u32[]{:S(2)}, u32[]{:S(2)}) %collective-permute-start.2) | collective-permute-done | bytes 1114144 | tf_op jit(solution)/shard_map/ppermute | solution.py:367
  55.3 0.0 copy-start.4
  55.3 9.2 %collective-permute-done.3.refs_3_.q3_hbm = bf16[272,2048]{1,0:T(8,128)(2,1)} collective-permute-done((bf16[272,2048]{1,0:T(8,128)(2,1)S(1)}, bf16[272,2048]{1,0:T(8,128)(2,1)}, u32[]{:S(2)}, u32[]{:S(2)}) %collective-permute-start.3) | collective-permute-done | bytes 1114144 | tf_op jit(solution)/shard_map/ppermute | solution.py:367
  64.4 0.0 copy-done.2
  64.5 0.0 copy-done.3
  64.5 0.0 copy-done.4
  64.5 57.3 %all-to-all-done = bf16[64,16,2176]{2,1,0:T(8,128)(2,1)} async-done(((bf16[64,16,2176]{2,1,0:T(8,128)(2,1)}), bf16[64,16,2176]{2,1,0:T(8,128)(2,1)}, u32[]{:S(2)}, u32[]{:S(2)}) %all-to-all-start) | async-done | bytes 4456480 | tf_op jit(solution)/shard_map/all_to_all | solution.py:365
  121.7 0.0 copy-start
  121.7 17.8 %score_blocks.1 = (f32[64,128]{1,0:T(8,128)}, f32[4,256]{1,0:T(4,128)}, f32[4,256]{1,0:T(4,128)}) custom-call(s32[1]{0:T(128)} %bitcast.spec_ref, bf16[1024,2176]{1,0:T(8,128)(2,1)} %bitcast.2.x_hbm, bf16[1024,2048]{1,0:T(8,128)(2,1)} %own_hbm.1, bf16[272,2048]{1,0:T(8,128)(2,1)} %after.1.q0_hbm, bf16[272,2048]{1,0:T(8,128)(2,1)} %copy-done.3, ...), custom_call_target="tpu_custom_call" | custom-call | flops 8589934592 | bytes 12582912 | tf_op jit(solution)/shard_map/score_blocks/pallas_call | solution.py:324
  139.6 3.3 %collective-permute-start.4 = (f32[4,256]{1,0:T(4,128)}, f32[4,256]{1,0:T(4,128)S(1)}, u32[]{:S(2)}, u32[]{:S(2)}) collective-permute-start(f32[4,256]{1,0:T(4,128)} %get-tuple-element.12), channel_id=1, source_target_pairs={{0,4},{4,8},{8,12},{12,16},{16,20},{20,24},{24,28},{28,32},{32,36}... | collective-permute-start | bytes 12296 | tf_op jit(solution)/shard_map/ppermute | solution.py:378
  142.8 5.9 %all-to-all-start.1 = ((f32[64,1,128]{2,1,0:T(1,128)}), f32[64,1,128]{2,1,0:T(1,128)S(1)}, u32[]{:S(2)}, u32[]{:S(2)}) async-start(f32[64,1,128]{2,1,0:T(1,128)} %bitcast.15), calls=%async_computation.1 | async-start | bytes 65536 | tf_op jit(solution)/shard_map/all_to_all | solution.py:375
  148.8 0.0 collective-permute-done.4
  148.8 0.7 add.9
  149.5 8.8 %psum.7 = f32[4,256]{1,0:T(4,128)S(1)} all-reduce(f32[4,256]{1,0:T(4,128)S(1)} %add.9), channel_id=1, replica_groups=mesh['mass'=64,'spec'=4] {'spec'}, use_global_device_ids=true, to_apply=%region_0.0 | all-reduce | flops 1024 | bytes 8192 | tf_op jit(solution)/shard_map/psum | solution.py:379
  158.2 0.6 constant_dynamic-slice_fusion
  158.8 0.0 all-to-all-done.1
  158.8 0.0 copy-done
  158.8 1.2 pick.1
  (1 shorter events, 0.0 us)
Async XLA Ops:
  3.4 18.0 %collective-permute-start = (bf16[272,2048]{1,0:T(8,128)(2,1)}, bf16[272,2048]{1,0:T(8,128)(2,1)S(1)}, u32[]{:S(2)}, u32[]{:S(2)}) collective-permute-start(bf16[272,2048]{1,0:T(8,128)(2,1)} %cut_quarter.1), channel_id=1, source_target_pairs={{4,0},{8,4},{12,8},{16,12},{20,16},{24,20},{28,24},{32,28},{36,32}... | collective-permute-start | bytes 3342344 | tf_op jit(solution)/shard_map/ppermute | solution.py:363
  10.3 16.0 %copy-start.1 = (s32[1024]{0:T(1024)S(1)}, s32[1024]{0:T(1024)}, u32[]{:S(2)}) copy-start(s32[1024]{0:T(1024)} %param.12) | copy-start | bytes 12292
  10.3 111.4 %all-to-all-start = ((bf16[64,16,2176]{2,1,0:T(8,128)(2,1)}), bf16[64,16,2176]{2,1,0:T(8,128)(2,1)}, u32[]{:S(2)}, u32[]{:S(2)}) async-start(bf16[64,16,2176]{2,1,0:T(8,128)(2,1)} %pack_blocks.1), calls=%async_computation | async-start | bytes 8912896 | tf_op jit(solution)/shard_map/all_to_all | solution.py:365
  21.4 43.0 %copy-start.2 = (bf16[272,2048]{1,0:T(8,128)(2,1)}, bf16[272,2048]{1,0:T(8,128)(2,1)S(1)}, u32[]{:S(2)}) copy-start(bf16[272,2048]{1,0:T(8,128)(2,1)S(1)} %collective-permute-done.refs_0_) | copy-start | bytes 3342340
  21.4 16.0 %collective-permute-start.1 = (bf16[272,2048]{1,0:T(8,128)(2,1)S(1)}, bf16[272,2048]{1,0:T(8,128)(2,1)S(1)}, u32[]{:S(2)}, u32[]{:S(2)}) collective-permute-start(bf16[272,2048]{1,0:T(8,128)(2,1)S(1)} %collective-permute-done.refs_0_), channel_id=1, source_target_pairs={{0,1},{1,2},{2,3},{3,0},{4,5},{5,6},{6,7},{7,4},{8,9},{9,10},{10,1... | collective-permute-start | bytes 3342344 | tf_op jit(solution)/shard_map/ppermute | solution.py:367
  22.7 32.6 %collective-permute-start.2 = (bf16[272,2048]{1,0:T(8,128)(2,1)S(1)}, bf16[272,2048]{1,0:T(8,128)(2,1)S(1)}, u32[]{:S(2)}, u32[]{:S(2)}) collective-permute-start(bf16[272,2048]{1,0:T(8,128)(2,1)S(1)} %collective-permute-done.refs_0_), channel_id=1, source_target_pairs={{0,2},{1,3},{2,0},{3,1},{4,6},{5,7},{6,4},{7,5},{8,10},{9,11},{10,... | collective-permute-start | bytes 3342344 | tf_op jit(solution)/shard_map/ppermute | solution.py:367
  25.1 39.3 %collective-permute-start.3 = (bf16[272,2048]{1,0:T(8,128)(2,1)S(1)}, bf16[272,2048]{1,0:T(8,128)(2,1)}, u32[]{:S(2)}, u32[]{:S(2)}) collective-permute-start(bf16[272,2048]{1,0:T(8,128)(2,1)S(1)} %collective-permute-done.refs_0_), channel_id=1, source_target_pairs={{0,3},{1,0},{2,1},{3,2},{4,7},{5,4},{6,5},{7,6},{8,11},{9,8},{10,9... | collective-permute-start | bytes 3342344 | tf_op jit(solution)/shard_map/ppermute | solution.py:367
  37.5 27.0 %copy-start.3 = (bf16[272,2048]{1,0:T(8,128)(2,1)}, bf16[272,2048]{1,0:T(8,128)(2,1)S(1)}, u32[]{:S(2)}) copy-start(bf16[272,2048]{1,0:T(8,128)(2,1)S(1)} %collective-permute-done.1.refs_1_.q1_hbm) | copy-start | bytes 3342340
  55.3 9.2 %copy-start.4 = (bf16[272,2048]{1,0:T(8,128)(2,1)}, bf16[272,2048]{1,0:T(8,128)(2,1)S(1)}, u32[]{:S(2)}) copy-start(bf16[272,2048]{1,0:T(8,128)(2,1)S(1)} %collective-permute-done.2.refs_2_.q2_hbm) | copy-start | bytes 3342340
  121.7 37.1 %copy-start = (s32[32]{0:T(128)S(1)}, s32[32]{0:T(128)}, u32[]{:S(2)}) copy-start(s32[32]{0:T(128)} %start_ref.3) | copy-start | bytes 388
  139.6 9.2 %collective-permute-start.4 = (f32[4,256]{1,0:T(4,128)}, f32[4,256]{1,0:T(4,128)S(1)}, u32[]{:S(2)}, u32[]{:S(2)}) collective-permute-start(f32[4,256]{1,0:T(4,128)} %get-tuple-element.12), channel_id=1, source_target_pairs={{0,4},{4,8},{8,12},{12,16},{16,20},{20,24},{24,28},{28,32},{32,36}... | collective-permute-start | bytes 12296 | tf_op jit(solution)/shard_map/ppermute | solution.py:378
  142.8 15.9 %all-to-all-start.1 = ((f32[64,1,128]{2,1,0:T(1,128)}), f32[64,1,128]{2,1,0:T(1,128)S(1)}, u32[]{:S(2)}, u32[]{:S(2)}) async-start(f32[64,1,128]{2,1,0:T(1,128)} %bitcast.15), calls=%async_computation.1 | async-start | bytes 65536 | tf_op jit(solution)/shard_map/all_to_all | solution.py:375

commit v6 on v5

--- a/solution.py
+++ b/solution.py
@@ -19,7 +19,10 @@
 SUB = 8
 
 
-def cut_kernel(spec_ref, mass_ref, bins_ref, shift_ref, table_hbm, quarter_hbm, part_ref, extra_ref, load_sem, store_sem, sem):
+def cut_kernel(
+    spec_ref, mass_ref, bins_hbm, shift_hbm, table_hbm, quarter_hbm,
+    bins_ref, shift_ref, part_ref, extra_ref, small_sem, load_sem, store_sem, sem,
+):
     steps, part = load_sem.shape[0], part_ref.shape[0]
     piece = part // steps
     first = pl.multiple_of(spec_ref[0] * part, part)
@@ -34,6 +37,14 @@
 
     for j in range(steps):
         load(j).start()
+    smalls = [
+        pltpu.make_async_copy(source, into, small_sem.at[k])
+        for k, (source, into) in enumerate(((bins_hbm, bins_ref), (shift_hbm, shift_ref)))
+    ]
+    for small in smalls:
+        small.start()
+    for small in smalls:
+        small.wait()
     bins = (bins_ref[0:1, pl.ds(first, part)] - mass_ref[0] * BIN_DEV).astype(jnp.float32)
     rest = shift_ref[0:1, pl.ds(first, part)]
     extra_ref[...] = jnp.zeros_like(extra_ref)
@@ -55,17 +66,19 @@
 def cut_quarter(spec, mass, bins, shifts, table, part):
     width = table.shape[1]
     smem = pl.BlockSpec(memory_space=pltpu.SMEM)
-    vmem = pl.BlockSpec(memory_space=pltpu.VMEM)
     hbm = pl.BlockSpec(memory_space=pltpu.HBM)
     steps = 4
     return pl.pallas_call(
         cut_kernel,
         out_shape=jax.ShapeDtypeStruct((part + SB, width), table.dtype),
-        in_specs=[smem, smem, vmem, vmem, hbm],
+        in_specs=[smem, smem, hbm, hbm, hbm],
         out_specs=hbm,
         scratch_shapes=[
+            pltpu.VMEM((1, table.shape[0]), bins.dtype),
+            pltpu.VMEM((1, table.shape[0]), shifts.dtype),
             pltpu.VMEM((part, width), table.dtype),
             pltpu.VMEM((SB, width), table.dtype),
+            pltpu.SemaphoreType.DMA((2,)),
             pltpu.SemaphoreType.DMA((steps,)),
             pltpu.SemaphoreType.DMA((steps,)),
             pltpu.SemaphoreType.DMA,
@@ -75,7 +88,10 @@
     )(spec.reshape(1), mass.reshape(1), bins[None], shifts[None], table)
 
 
-def pack_kernel(start_ref, range_ref, count_ref, spectra_hbm, out_hbm, held, meta_ref, load_sem, sem, meta_sem):
+def pack_kernel(
+    start_hbm, range_hbm, count_hbm, spectra_hbm, out_hbm,
+    start_ref, range_ref, count_ref, held, meta_ref, small_sem, load_sem, sem, meta_sem,
+):
     blocks, rows, width = held.shape
     batch = blocks // load_sem.shape[0]
 
@@ -88,7 +104,17 @@
 
     for j in range(blocks // batch):
         load(j).start()
+    smalls = [
+        pltpu.make_async_copy(source, into, small_sem.at[k])
+        for k, (source, into) in enumerate(
+            ((start_hbm, start_ref), (range_hbm, range_ref), (count_hbm, count_ref))
+        )
+    ]
+    for small in smalls:
+        small.start()
     meta_ref[...] = jnp.zeros_like(meta_ref)
+    for small in smalls:
+        small.wait()
     row = lax.broadcasted_iota(jnp.int32, (rows, LANES), 0)
     lane = lax.broadcasted_iota(jnp.int32, (rows, LANES), 1)
     for i in range(blocks):
@@ -110,16 +136,19 @@
 
 def pack_blocks(block_start, block_range, block_count, spectra, owners):
     blocks, rows, width = spectra.shape
-    smem = pl.BlockSpec(memory_space=pltpu.SMEM)
     hbm = pl.BlockSpec(memory_space=pltpu.HBM)
     return pl.pallas_call(
         pack_kernel,
         out_shape=jax.ShapeDtypeStruct((owners, rows, width + LANES), spectra.dtype),
-        in_specs=[smem, smem, smem, hbm],
+        in_specs=[hbm] * 4,
         out_specs=hbm,
         scratch_shapes=[
+            pltpu.SMEM((blocks,), jnp.int32),
+            pltpu.SMEM((2, blocks), jnp.int32),
+            pltpu.SMEM((blocks,), jnp.int32),
             pltpu.VMEM((blocks, rows, width), spectra.dtype),
             pltpu.VMEM((owners, rows, LANES), spectra.dtype),
+            pltpu.SemaphoreType.DMA((3,)),
             pltpu.SemaphoreType.DMA((4,)),
             pltpu.SemaphoreType.DMA((blocks,)),
             pltpu.SemaphoreType.DMA,

time: 161 us -> 160 us (level)
    ppermute x3, waiting for transfers between devices: 37.5 us -> 23.4 us  [body(): lax.ppermute(quarters[0], 'spec', [(i, (i + k) % specs) for i in range(sp...]
    all_to_all x1, waiting for transfers between devices: 57.3 us -> 70.4 us  [body(): lax.all_to_all(packed, 'mass', split_axis=0, concat_axis=0, tiled=True)]
  transfers between devices with their start and end apart: 7 -> 7, of which waited for: 4 -> 3; matrix products, arithmetic and copies ran while one was open for 1% -> 1% of each run, Pallas kernels for 2% -> 2%
where the time goes in v6:
time: 160 us; the launch traced here: 159 us
  waiting for transfers between devices  93.8 us (59%)
  starting transfers between devices  29 us (18%)
  Pallas kernels  24 us (15%)
  blocking collectives  8.96 us (6%)
    all_to_all x1, waiting for transfers between devices, body(): lax.all_to_all(packed, 'mass', split_axis=0, concat_axis=0, tiled=True)  70.4 us
    ppermute x3, waiting for transfers between devices, body(): lax.ppermute(quarters[0], 'spec', [(i, (i + k) % specs) for i in range(sp...  23.4 us
    pallas_call x1, Pallas kernels, score_blocks(): pl.pallas_call(score_kernel, out_shape=(jax.ShapeDtypeStruct((total // SB...  17.8 us
    all_to_all x1, starting transfers between devices, body(): lax.all_to_all(packed, 'mass', split_axis=0, concat_axis=0, tiled=True)  11.1 us
    psum x1, blocking collectives, body(): support = lax.dynamic_index_in_dim(lax.psum(total, 'spec'), spec, 0, False)  8.96 us
    all_to_all x1, starting transfers between devices, body(): home = lax.all_to_all(ret, 'mass', split_axis=0, concat_axis=0, tiled=True)  6.44 us
    ppermute x3, starting transfers between devices, body(): lax.ppermute(quarters[0], 'spec', [(i, (i + k) % specs) for i in range(sp...  4.88 us
    ppermute x1, starting transfers between devices, body(): quarters = [lax.ppermute(quarter, 'mass', back)]  3.32 us
  transfers between devices with their start and end apart: 7, of which 3 were waited for; matrix products, arithmetic and copies ran while one was open for 1% of the time, Pallas kernels for 2%

profile of v6, /device:TPU:1, one launch (start us, length us, event | category | flops | bytes accessed | tf_op | source)
XLA Modules:
  0.0 159.4 jit_solution(12815445175730330630)
XLA Ops:
  0.6 2.1 %cut_quarter.1 = bf16[272,2048]{1,0:T(8,128)(2,1)} custom-call(s32[1]{0:T(128)} %bitcast.spec_ref, s32[1]{0:T(128)} %bitcast.3.mass_ref, s32[1,1024]{1,0:T(1,128)} %bitcast.16, f32[1,1024]{1,0:T(1,128)} %bitcast.18, bf16[1024,2048]{1,0:T(8,128)(2,1)} %own_hbm.1), custom_call_target="tpu_custom_call" | custom-call | tf_op jit(solution)/shard_map/cut_quarter/pallas_call | solution.py:71
  2.8 3.3 %collective-permute-start = (bf16[272,2048]{1,0:T(8,128)(2,1)}, bf16[272,2048]{1,0:T(8,128)(2,1)S(1)}, u32[]{:S(2)}, u32[]{:S(2)}) collective-permute-start(bf16[272,2048]{1,0:T(8,128)(2,1)} %cut_quarter.1), channel_id=1, source_target_pairs={{4,0},{8,4},{12,8},{16,12},{20,16},{24,20},{28,24},{32,28},{36,32}... | collective-permute-start | bytes 3342344 | tf_op jit(solution)/shard_map/ppermute | solution.py:392
  6.1 2.8 %pack_blocks.1 = bf16[64,16,2176]{2,1,0:T(8,128)(2,1)} custom-call(s32[32]{0:T(128)} %start_ref.1, s32[2,32]{1,0:T(2,128)} %bitcast.20, s32[32]{0:T(128)} %count_hbm.1, bf16[32,16,2048]{2,1,0:T(8,128)(2,1)} %spectra_hbm.1), custom_call_target="tpu_custom_call" | custom-call | tf_op jit(solution)/shard_map/pack_blocks/pallas_call | solution.py:140
  8.9 0.0 copy-start.1
  8.9 11.1 %all-to-all-start = ((bf16[64,16,2176]{2,1,0:T(8,128)(2,1)}), bf16[64,16,2176]{2,1,0:T(8,128)(2,1)}, u32[]{:S(2)}, u32[]{:S(2)}) async-start(bf16[64,16,2176]{2,1,0:T(8,128)(2,1)} %pack_blocks.1), calls=%async_computation | async-start | bytes 8912896 | tf_op jit(solution)/shard_map/all_to_all | solution.py:394
  20.0 0.0 collective-permute-done.refs_0_
  20.0 0.0 copy-start.2
  20.0 1.2 collective-permute-start.1
  21.2 2.5 %collective-permute-start.2 = (bf16[272,2048]{1,0:T(8,128)(2,1)S(1)}, bf16[272,2048]{1,0:T(8,128)(2,1)S(1)}, u32[]{:S(2)}, u32[]{:S(2)}) collective-permute-start(bf16[272,2048]{1,0:T(8,128)(2,1)S(1)} %collective-permute-done.refs_0_), channel_id=1, source_target_pairs={{0,2},{1,3},{2,0},{3,1},{4,6},{5,7},{6,4},{7,5},{8,10},{9,11},{10,... | collective-permute-start | bytes 3342344 | tf_op jit(solution)/shard_map/ppermute | solution.py:396
  23.7 1.2 collective-permute-start.3
  24.9 0.0 copy-done.1
  24.9 0.6 subtract_convert_fusion
  25.5 10.6 %collective-permute-done.1.refs_1_.q1_hbm = bf16[272,2048]{1,0:T(8,128)(2,1)S(1)} collective-permute-done((bf16[272,2048]{1,0:T(8,128)(2,1)S(1)}, bf16[272,2048]{1,0:T(8,128)(2,1)S(1)}, u32[]{:S(2)}, u32[]{:S(2)}) %collective-permute-start.1) | collective-permute-done | bytes 1114144 | tf_op jit(solution)/shard_map/ppermute | solution.py:396
  36.1 0.0 copy-start.3
  36.1 12.9 %collective-permute-done.2.refs_2_.q2_hbm = bf16[272,2048]{1,0:T(8,128)(2,1)S(1)} collective-permute-done((bf16[272,2048]{1,0:T(8,128)(2,1)S(1)}, bf16[272,2048]{1,0:T(8,128)(2,1)S(1)}, u32[]{:S(2)}, u32[]{:S(2)}) %collective-permute-start.2) | collective-permute-done | bytes 1114144 | tf_op jit(solution)/shard_map/ppermute | solution.py:396
  48.9 0.0 copy-start.4
  48.9 0.0 collective-permute-done.3.refs_3_.q3_hbm
  48.9 0.0 copy-done.2
  48.9 0.0 copy-done.3
  48.9 1.0 copy-done.4
  49.9 70.4 %all-to-all-done = bf16[64,16,2176]{2,1,0:T(8,128)(2,1)} async-done(((bf16[64,16,2176]{2,1,0:T(8,128)(2,1)}), bf16[64,16,2176]{2,1,0:T(8,128)(2,1)}, u32[]{:S(2)}, u32[]{:S(2)}) %all-to-all-start) | async-done | bytes 4456480 | tf_op jit(solution)/shard_map/all_to_all | solution.py:394
  120.3 0.0 copy-start
  120.3 17.8 %score_blocks.1 = (f32[64,128]{1,0:T(8,128)}, f32[4,256]{1,0:T(4,128)}, f32[4,256]{1,0:T(4,128)}) custom-call(s32[1]{0:T(128)} %bitcast.spec_ref, bf16[1024,2176]{1,0:T(8,128)(2,1)} %bitcast.2.x_hbm, bf16[1024,2048]{1,0:T(8,128)(2,1)} %own_hbm.1, bf16[272,2048]{1,0:T(8,128)(2,1)} %after.1.q0_hbm, bf16[272,2048]{1,0:T(8,128)(2,1)} %copy-done.3, ...), custom_call_target="tpu_custom_call" | custom-call | flops 8589934592 | bytes 12582912 | tf_op jit(solution)/shard_map/score_blocks/pallas_call | solution.py:353
  138.1 3.3 %collective-permute-start.4 = (f32[4,256]{1,0:T(4,128)}, f32[4,256]{1,0:T(4,128)S(1)}, u32[]{:S(2)}, u32[]{:S(2)}) collective-permute-start(f32[4,256]{1,0:T(4,128)} %get-tuple-element.12), channel_id=1, source_target_pairs={{0,4},{4,8},{8,12},{12,16},{16,20},{20,24},{24,28},{28,32},{32,36}... | collective-permute-start | bytes 12296 | tf_op jit(solution)/shard_map/ppermute | solution.py:407
  141.4 6.4 %all-to-all-start.1 = ((f32[64,1,128]{2,1,0:T(1,128)}), f32[64,1,128]{2,1,0:T(1,128)S(1)}, u32[]{:S(2)}, u32[]{:S(2)}) async-start(f32[64,1,128]{2,1,0:T(1,128)} %bitcast.15), calls=%async_computation.1 | async-start | bytes 65536 | tf_op jit(solution)/shard_map/all_to_all | solution.py:404
  147.9 0.0 collective-permute-done.4
  147.9 0.7 add.9
  148.6 9.0 %psum.7 = f32[4,256]{1,0:T(4,128)S(1)} all-reduce(f32[4,256]{1,0:T(4,128)S(1)} %add.9), channel_id=1, replica_groups=mesh['mass'=64,'spec'=4] {'spec'}, use_global_device_ids=true, to_apply=%region_0.0 | all-reduce | flops 1024 | bytes 8192 | tf_op jit(solution)/shard_map/psum | solution.py:408
  157.5 0.6 constant_dynamic-slice_fusion
  158.1 0.0 all-to-all-done.1
  158.1 0.0 copy-done
  158.1 1.2 pick.1
  (1 shorter events, 0.0 us)
Async XLA Ops:
  2.8 17.2 %collective-permute-start = (bf16[272,2048]{1,0:T(8,128)(2,1)}, bf16[272,2048]{1,0:T(8,128)(2,1)S(1)}, u32[]{:S(2)}, u32[]{:S(2)}) collective-permute-start(bf16[272,2048]{1,0:T(8,128)(2,1)} %cut_quarter.1), channel_id=1, source_target_pairs={{4,0},{8,4},{12,8},{16,12},{20,16},{24,20},{28,24},{32,28},{36,32}... | collective-permute-start | bytes 3342344 | tf_op jit(solution)/shard_map/ppermute | solution.py:392
  8.9 16.0 %copy-start.1 = (s32[1024]{0:T(1024)S(1)}, s32[1024]{0:T(1024)}, u32[]{:S(2)}) copy-start(s32[1024]{0:T(1024)} %param.12) | copy-start | bytes 12292
  8.9 111.4 %all-to-all-start = ((bf16[64,16,2176]{2,1,0:T(8,128)(2,1)}), bf16[64,16,2176]{2,1,0:T(8,128)(2,1)}, u32[]{:S(2)}, u32[]{:S(2)}) async-start(bf16[64,16,2176]{2,1,0:T(8,128)(2,1)} %pack_blocks.1), calls=%async_computation | async-start | bytes 8912896 | tf_op jit(solution)/shard_map/all_to_all | solution.py:394
  20.0 28.9 %copy-start.2 = (bf16[272,2048]{1,0:T(8,128)(2,1)}, bf16[272,2048]{1,0:T(8,128)(2,1)S(1)}, u32[]{:S(2)}) copy-start(bf16[272,2048]{1,0:T(8,128)(2,1)S(1)} %collective-permute-done.refs_0_) | copy-start | bytes 3342340
  20.0 16.0 %collective-permute-start.1 = (bf16[272,2048]{1,0:T(8,128)(2,1)S(1)}, bf16[272,2048]{1,0:T(8,128)(2,1)S(1)}, u32[]{:S(2)}, u32[]{:S(2)}) collective-permute-start(bf16[272,2048]{1,0:T(8,128)(2,1)S(1)} %collective-permute-done.refs_0_), channel_id=1, source_target_pairs={{0,1},{1,2},{2,3},{3,0},{4,5},{5,6},{6,7},{7,4},{8,9},{9,10},{10,1... | collective-permute-start | bytes 3342344 | tf_op jit(solution)/shard_map/ppermute | solution.py:396
  21.2 27.7 %collective-permute-start.2 = (bf16[272,2048]{1,0:T(8,128)(2,1)S(1)}, bf16[272,2048]{1,0:T(8,128)(2,1)S(1)}, u32[]{:S(2)}, u32[]{:S(2)}) collective-permute-start(bf16[272,2048]{1,0:T(8,128)(2,1)S(1)} %collective-permute-done.refs_0_), channel_id=1, source_target_pairs={{0,2},{1,3},{2,0},{3,1},{4,6},{5,7},{6,4},{7,5},{8,10},{9,11},{10,... | collective-permute-start | bytes 3342344 | tf_op jit(solution)/shard_map/ppermute | solution.py:396
  23.7 25.2 %collective-permute-start.3 = (bf16[272,2048]{1,0:T(8,128)(2,1)S(1)}, bf16[272,2048]{1,0:T(8,128)(2,1)}, u32[]{:S(2)}, u32[]{:S(2)}) collective-permute-start(bf16[272,2048]{1,0:T(8,128)(2,1)S(1)} %collective-permute-done.refs_0_), channel_id=1, source_target_pairs={{0,3},{1,0},{2,1},{3,2},{4,7},{5,4},{6,5},{7,6},{8,11},{9,8},{10,9... | collective-permute-start | bytes 3342344 | tf_op jit(solution)/shard_map/ppermute | solution.py:396
  36.1 12.9 %copy-start.3 = (bf16[272,2048]{1,0:T(8,128)(2,1)}, bf16[272,2048]{1,0:T(8,128)(2,1)S(1)}, u32[]{:S(2)}) copy-start(bf16[272,2048]{1,0:T(8,128)(2,1)S(1)} %collective-permute-done.1.refs_1_.q1_hbm) | copy-start | bytes 3342340
  48.9 1.0 copy-start.4
  120.3 37.8 %copy-start = (s32[32]{0:T(128)S(1)}, s32[32]{0:T(128)}, u32[]{:S(2)}) copy-start(s32[32]{0:T(128)} %start_ref.1) | copy-start | bytes 388
  138.1 9.7 %collective-permute-start.4 = (f32[4,256]{1,0:T(4,128)}, f32[4,256]{1,0:T(4,128)S(1)}, u32[]{:S(2)}, u32[]{:S(2)}) collective-permute-start(f32[4,256]{1,0:T(4,128)} %get-tuple-element.12), channel_id=1, source_target_pairs={{0,4},{4,8},{8,12},{12,16},{16,20},{20,24},{24,28},{28,32},{32,36}... | collective-permute-start | bytes 12296 | tf_op jit(solution)/shard_map/ppermute | solution.py:407
  141.4 16.7 %all-to-all-start.1 = ((f32[64,1,128]{2,1,0:T(1,128)}), f32[64,1,128]{2,1,0:T(1,128)S(1)}, u32[]{:S(2)}, u32[]{:S(2)}) async-start(f32[64,1,128]{2,1,0:T(1,128)} %bitcast.15), calls=%async_computation.1 | async-start | bytes 65536 | tf_op jit(solution)/shard_map/all_to_all | solution.py:404

commit v7 on v6

--- a/solution.py
+++ b/solution.py
@@ -204,8 +204,8 @@
 
 
 def score_kernel(
-    spec_ref, x_hbm, own_hbm, q0_hbm, q1_hbm, q2_hbm, q3_hbm, bins_ref, shift_ref, ret_ref, mine_ref, next_ref,
-    x_ref, table_ref, extra_ref, small_ref, even_ref, odd_ref, held_ref, sum_ref, x_sem, table_sem, small_sem,
+    spec_ref, x_hbm, own_hbm, q0_hbm, q1_hbm, q2_hbm, q3_hbm, bins_hbm, shift_hbm, ret_ref, mine_ref, next_ref,
+    x_ref, table_ref, bins_ref, shift_ref, extra_ref, small_ref, even_ref, odd_ref, held_ref, sum_ref, x_sem, table_sem, small_sem, own_sem,
 ):
     tiles = x_ref.shape[0]
     width = table_ref.shape[1]
@@ -233,6 +233,12 @@
     for j in range(own, parts):
         fetch_part(j).start()
     for copy in smalls:
+        copy.start()
+    mine = [
+        pltpu.make_async_copy(source, into, own_sem.at[k])
+        for k, (source, into) in enumerate(((bins_hbm, bins_ref), (shift_hbm, shift_ref)))
+    ]
+    for copy in mine:
         copy.start()
     for t in range(2, tiles):
         fetch(t).start()
@@ -314,6 +320,8 @@
         for k in range(j, j + PAIR):
             fetch_part(k).wait()
         multiply(0, j // PAIR, even_ref, PAIR * part)
+    for copy in mine:
+        copy.wait()
     small_ref[0:1, :own * part] = bins_ref[...]
     small_ref[1:2, :own * part] = shift_ref[...]
     for k, copy in enumerate(smalls):
@@ -356,11 +364,13 @@
             jax.ShapeDtypeStruct((total // SB, LANES), jnp.float32),
         )
         + (jax.ShapeDtypeStruct((len(quarters), part), jnp.float32),) * 2,
-        in_specs=[pl.BlockSpec(memory_space=pltpu.SMEM)] + [hbm] * (2 + len(quarters)) + [vmem, vmem],
+        in_specs=[pl.BlockSpec(memory_space=pltpu.SMEM)] + [hbm] * (4 + len(quarters)),
         out_specs=(vmem,) * 3,
         scratch_shapes=[
             pltpu.VMEM((total // TILE, TILE, rows.shape[1]), rows.dtype),
             pltpu.VMEM((wide, width), table.dtype),
+            pltpu.VMEM(bins.shape, bins.dtype),
+            pltpu.VMEM(shifts.shape, shifts.dtype),
             pltpu.VMEM((len(quarters), SB, width), table.dtype),
             pltpu.VMEM((2, wide), jnp.float32),
             pltpu.VMEM((TILE, wide), jnp.float32),
@@ -370,6 +380,7 @@
             pltpu.SemaphoreType.DMA((total // TILE,)),
             pltpu.SemaphoreType.DMA((wide // part,)),
             pltpu.SemaphoreType.DMA((len(quarters),)),
+            pltpu.SemaphoreType.DMA((2,)),
         ],
         compiler_params=pltpu.CompilerParams(vmem_limit_bytes=WHOLE_VMEM),
         cost_estimate=pl.CostEstimate(

time: 160 us -> 160 us (level)
  no operation moved by 1% of the time
where the time goes in v7:
time: 160 us; the launch traced here: 159 us
  waiting for transfers between devices  93.7 us (59%)
  starting transfers between devices  29.2 us (18%)
  Pallas kernels  23.5 us (15%)
  blocking collectives  8.96 us (6%)
    all_to_all x1, waiting for transfers between devices, body(): lax.all_to_all(packed, 'mass', split_axis=0, concat_axis=0, tiled=True)  70.3 us
    ppermute x3, waiting for transfers between devices, body(): lax.ppermute(quarters[0], 'spec', [(i, (i + k) % specs) for i in range(sp...  23.4 us
    pallas_call x1, Pallas kernels, score_blocks(): pl.pallas_call(score_kernel, out_shape=(jax.ShapeDtypeStruct((total // SB...  17.4 us
    all_to_all x1, starting transfers between devices, body(): lax.all_to_all(packed, 'mass', split_axis=0, concat_axis=0, tiled=True)  11.1 us
    psum x1, blocking collectives, body(): support = lax.dynamic_index_in_dim(lax.psum(total, 'spec'), spec, 0, False)  8.96 us
    all_to_all x1, starting transfers between devices, body(): home = lax.all_to_all(ret, 'mass', split_axis=0, concat_axis=0, tiled=True)  6.51 us
    ppermute x3, starting transfers between devices, body(): lax.ppermute(quarters[0], 'spec', [(i, (i + k) % specs) for i in range(sp...  5.01 us
    ppermute x1, starting transfers between devices, body(): quarters = [lax.ppermute(quarter, 'mass', back)]  3.32 us
  transfers between devices with their start and end apart: 7, of which 3 were waited for; matrix products, arithmetic and copies ran while one was open for 1% of the time, Pallas kernels for 2%

profile of v7, /device:TPU:1, one launch (start us, length us, event | category | flops | bytes accessed | tf_op | source)
XLA Modules:
  0.0 158.9 jit_solution(2545846500447281604)
XLA Ops:
  0.6 2.1 %cut_quarter.1 = bf16[272,2048]{1,0:T(8,128)(2,1)} custom-call(s32[1]{0:T(128)} %bitcast.spec_ref, s32[1]{0:T(128)} %bitcast.3.mass_ref, s32[1,1024]{1,0:T(1,128)} %bitcast.16, f32[1,1024]{1,0:T(1,128)} %bitcast.18, bf16[1024,2048]{1,0:T(8,128)(2,1)} %own_hbm.1), custom_call_target="tpu_custom_call" | custom-call | tf_op jit(solution)/shard_map/cut_quarter/pallas_call | solution.py:71
  2.8 3.3 %collective-permute-start = (bf16[272,2048]{1,0:T(8,128)(2,1)}, bf16[272,2048]{1,0:T(8,128)(2,1)S(1)}, u32[]{:S(2)}, u32[]{:S(2)}) collective-permute-start(bf16[272,2048]{1,0:T(8,128)(2,1)} %cut_quarter.1), channel_id=1, source_target_pairs={{4,0},{8,4},{12,8},{16,12},{20,16},{24,20},{28,24},{32,28},{36,32}... | collective-permute-start | bytes 3342344 | tf_op jit(solution)/shard_map/ppermute | solution.py:403
  6.1 2.7 %pack_blocks.1 = bf16[64,16,2176]{2,1,0:T(8,128)(2,1)} custom-call(s32[32]{0:T(128)} %start_ref.1, s32[2,32]{1,0:T(2,128)} %bitcast.20, s32[32]{0:T(128)} %count_hbm.1, bf16[32,16,2048]{2,1,0:T(8,128)(2,1)} %spectra_hbm.1), custom_call_target="tpu_custom_call" | custom-call | tf_op jit(solution)/shard_map/pack_blocks/pallas_call | solution.py:140
  8.8 0.0 copy-start.1
  8.8 11.1 %all-to-all-start = ((bf16[64,16,2176]{2,1,0:T(8,128)(2,1)}), bf16[64,16,2176]{2,1,0:T(8,128)(2,1)}, u32[]{:S(2)}, u32[]{:S(2)}) async-start(bf16[64,16,2176]{2,1,0:T(8,128)(2,1)} %pack_blocks.1), calls=%async_computation | async-start | bytes 8912896 | tf_op jit(solution)/shard_map/all_to_all | solution.py:405
  19.9 0.0 collective-permute-done.refs_0_
  19.9 0.0 copy-start.2
  19.9 1.3 collective-permute-start.1
  21.3 2.4 %collective-permute-start.2 = (bf16[272,2048]{1,0:T(8,128)(2,1)S(1)}, bf16[272,2048]{1,0:T(8,128)(2,1)S(1)}, u32[]{:S(2)}, u32[]{:S(2)}) collective-permute-start(bf16[272,2048]{1,0:T(8,128)(2,1)S(1)} %collective-permute-done.refs_0_), channel_id=1, source_target_pairs={{0,2},{1,3},{2,0},{3,1},{4,6},{5,7},{6,4},{7,5},{8,10},{9,11},{10,... | collective-permute-start | bytes 3342344 | tf_op jit(solution)/shard_map/ppermute | solution.py:407
  23.7 1.3 collective-permute-start.3
  25.0 0.0 copy-done.1
  25.0 0.6 subtract_convert_fusion
  25.6 10.4 %collective-permute-done.1.refs_1_.q1_hbm = bf16[272,2048]{1,0:T(8,128)(2,1)S(1)} collective-permute-done((bf16[272,2048]{1,0:T(8,128)(2,1)S(1)}, bf16[272,2048]{1,0:T(8,128)(2,1)S(1)}, u32[]{:S(2)}, u32[]{:S(2)}) %collective-permute-start.1) | collective-permute-done | bytes 1114144 | tf_op jit(solution)/shard_map/ppermute | solution.py:407
  36.0 0.0 copy-start.3
  36.0 12.9 %collective-permute-done.2.refs_2_.q2_hbm = bf16[272,2048]{1,0:T(8,128)(2,1)S(1)} collective-permute-done((bf16[272,2048]{1,0:T(8,128)(2,1)S(1)}, bf16[272,2048]{1,0:T(8,128)(2,1)S(1)}, u32[]{:S(2)}, u32[]{:S(2)}) %collective-permute-start.2) | collective-permute-done | bytes 1114144 | tf_op jit(solution)/shard_map/ppermute | solution.py:407
  48.9 0.0 copy-start.4
  48.9 0.0 collective-permute-done.3.refs_3_.q3_hbm
  48.9 0.0 copy-done.2
  48.9 0.0 copy-done.3
  48.9 1.0 copy-done.4
  49.9 70.3 %all-to-all-done = bf16[64,16,2176]{2,1,0:T(8,128)(2,1)} async-done(((bf16[64,16,2176]{2,1,0:T(8,128)(2,1)}), bf16[64,16,2176]{2,1,0:T(8,128)(2,1)}, u32[]{:S(2)}, u32[]{:S(2)}) %all-to-all-start) | async-done | bytes 4456480 | tf_op jit(solution)/shard_map/all_to_all | solution.py:405
  120.2 0.0 copy-start
  120.2 17.4 %score_blocks.1 = (f32[64,128]{1,0:T(8,128)}, f32[4,256]{1,0:T(4,128)}, f32[4,256]{1,0:T(4,128)}) custom-call(s32[1]{0:T(128)} %bitcast.spec_ref, bf16[1024,2176]{1,0:T(8,128)(2,1)} %bitcast.2.x_hbm, bf16[1024,2048]{1,0:T(8,128)(2,1)} %own_hbm.1, bf16[272,2048]{1,0:T(8,128)(2,1)} %after.1.q0_hbm, bf16[272,2048]{1,0:T(8,128)(2,1)} %copy-done.3, ...), custom_call_target="tpu_custom_call" | custom-call | flops 8589934592 | bytes 12582912 | tf_op jit(solution)/shard_map/score_blocks/pallas_call | solution.py:361
  137.6 3.3 %collective-permute-start.4 = (f32[4,256]{1,0:T(4,128)}, f32[4,256]{1,0:T(4,128)S(1)}, u32[]{:S(2)}, u32[]{:S(2)}) collective-permute-start(f32[4,256]{1,0:T(4,128)} %get-tuple-element.12), channel_id=1, source_target_pairs={{0,4},{4,8},{8,12},{12,16},{16,20},{20,24},{24,28},{28,32},{32,36}... | collective-permute-start | bytes 12296 | tf_op jit(solution)/shard_map/ppermute | solution.py:418
  140.9 6.5 %all-to-all-start.1 = ((f32[64,1,128]{2,1,0:T(1,128)}), f32[64,1,128]{2,1,0:T(1,128)S(1)}, u32[]{:S(2)}, u32[]{:S(2)}) async-start(f32[64,1,128]{2,1,0:T(1,128)} %bitcast.15), calls=%async_computation.1 | async-start | bytes 65536 | tf_op jit(solution)/shard_map/all_to_all | solution.py:415
  147.4 0.0 collective-permute-done.4
  147.5 0.7 add.9
  148.1 9.0 %psum.7 = f32[4,256]{1,0:T(4,128)S(1)} all-reduce(f32[4,256]{1,0:T(4,128)S(1)} %add.9), channel_id=1, replica_groups=mesh['mass'=64,'spec'=4] {'spec'}, use_global_device_ids=true, to_apply=%region_0.0 | all-reduce | flops 1024 | bytes 8192 | tf_op jit(solution)/shard_map/psum | solution.py:419
  157.1 0.6 constant_dynamic-slice_fusion
  157.7 0.0 all-to-all-done.1
  157.7 0.0 copy-done
  157.7 1.2 pick.1
  (1 shorter events, 0.0 us)
Async XLA Ops:
  2.8 17.2 %collective-permute-start = (bf16[272,2048]{1,0:T(8,128)(2,1)}, bf16[272,2048]{1,0:T(8,128)(2,1)S(1)}, u32[]{:S(2)}, u32[]{:S(2)}) collective-permute-start(bf16[272,2048]{1,0:T(8,128)(2,1)} %cut_quarter.1), channel_id=1, source_target_pairs={{4,0},{8,4},{12,8},{16,12},{20,16},{24,20},{28,24},{32,28},{36,32}... | collective-permute-start | bytes 3342344 | tf_op jit(solution)/shard_map/ppermute | solution.py:403
  8.8 16.1 %copy-start.1 = (s32[1024]{0:T(1024)S(1)}, s32[1024]{0:T(1024)}, u32[]{:S(2)}) copy-start(s32[1024]{0:T(1024)} %param.12) | copy-start | bytes 12292
  8.8 111.4 %all-to-all-start = ((bf16[64,16,2176]{2,1,0:T(8,128)(2,1)}), bf16[64,16,2176]{2,1,0:T(8,128)(2,1)}, u32[]{:S(2)}, u32[]{:S(2)}) async-start(bf16[64,16,2176]{2,1,0:T(8,128)(2,1)} %pack_blocks.1), calls=%async_computation | async-start | bytes 8912896 | tf_op jit(solution)/shard_map/all_to_all | solution.py:405
  19.9 29.0 %copy-start.2 = (bf16[272,2048]{1,0:T(8,128)(2,1)}, bf16[272,2048]{1,0:T(8,128)(2,1)S(1)}, u32[]{:S(2)}) copy-start(bf16[272,2048]{1,0:T(8,128)(2,1)S(1)} %collective-permute-done.refs_0_) | copy-start | bytes 3342340
  19.9 16.0 %collective-permute-start.1 = (bf16[272,2048]{1,0:T(8,128)(2,1)S(1)}, bf16[272,2048]{1,0:T(8,128)(2,1)S(1)}, u32[]{:S(2)}, u32[]{:S(2)}) collective-permute-start(bf16[272,2048]{1,0:T(8,128)(2,1)S(1)} %collective-permute-done.refs_0_), channel_id=1, source_target_pairs={{0,1},{1,2},{2,3},{3,0},{4,5},{5,6},{6,7},{7,4},{8,9},{9,10},{10,1... | collective-permute-start | bytes 3342344 | tf_op jit(solution)/shard_map/ppermute | solution.py:407
  21.3 27.6 %collective-permute-start.2 = (bf16[272,2048]{1,0:T(8,128)(2,1)S(1)}, bf16[272,2048]{1,0:T(8,128)(2,1)S(1)}, u32[]{:S(2)}, u32[]{:S(2)}) collective-permute-start(bf16[272,2048]{1,0:T(8,128)(2,1)S(1)} %collective-permute-done.refs_0_), channel_id=1, source_target_pairs={{0,2},{1,3},{2,0},{3,1},{4,6},{5,7},{6,4},{7,5},{8,10},{9,11},{10,... | collective-permute-start | bytes 3342344 | tf_op jit(solution)/shard_map/ppermute | solution.py:407
  23.7 25.2 %collective-permute-start.3 = (bf16[272,2048]{1,0:T(8,128)(2,1)S(1)}, bf16[272,2048]{1,0:T(8,128)(2,1)}, u32[]{:S(2)}, u32[]{:S(2)}) collective-permute-start(bf16[272,2048]{1,0:T(8,128)(2,1)S(1)} %collective-permute-done.refs_0_), channel_id=1, source_target_pairs={{0,3},{1,0},{2,1},{3,2},{4,7},{5,4},{6,5},{7,6},{8,11},{9,8},{10,9... | collective-permute-start | bytes 3342344 | tf_op jit(solution)/shard_map/ppermute | solution.py:407
  36.0 12.9 %copy-start.3 = (bf16[272,2048]{1,0:T(8,128)(2,1)}, bf16[272,2048]{1,0:T(8,128)(2,1)S(1)}, u32[]{:S(2)}) copy-start(bf16[272,2048]{1,0:T(8,128)(2,1)S(1)} %collective-permute-done.1.refs_1_.q1_hbm) | copy-start | bytes 3342340
  48.9 1.0 copy-start.4
  120.2 37.5 %copy-start = (s32[32]{0:T(128)S(1)}, s32[32]{0:T(128)}, u32[]{:S(2)}) copy-start(s32[32]{0:T(128)} %start_ref.1) | copy-start | bytes 388
  137.6 9.8 %collective-permute-start.4 = (f32[4,256]{1,0:T(4,128)}, f32[4,256]{1,0:T(4,128)S(1)}, u32[]{:S(2)}, u32[]{:S(2)}) collective-permute-start(f32[4,256]{1,0:T(4,128)} %get-tuple-element.12), channel_id=1, source_target_pairs={{0,4},{4,8},{8,12},{12,16},{16,20},{20,24},{24,28},{28,32},{32,36}... | collective-permute-start | bytes 12296 | tf_op jit(solution)/shard_map/ppermute | solution.py:418
  140.9 16.8 %all-to-all-start.1 = ((f32[64,1,128]{2,1,0:T(1,128)}), f32[64,1,128]{2,1,0:T(1,128)S(1)}, u32[]{:S(2)}, u32[]{:S(2)}) async-start(f32[64,1,128]{2,1,0:T(1,128)} %bitcast.15), calls=%async_computation.1 | async-start | bytes 65536 | tf_op jit(solution)/shard_map/all_to_all | solution.py:415
